TPU v7x, 32 devices: a whole 2x2x4 slice. The times are simulated.
32 devices in a mesh: dp: 4 (over y, core), ctx: 8 (over z, x).
Axes of the slice: x: 2, y: 2, z: 4, core: 2. Of those that a mesh axis runs over, the one named last changes fastest.
Arguments:
- inputs: bfloat16 [2, 4, 1024, 1600], P(None, 'dp', 'ctx'), may hold values from -12 to 12
- grad_out: bfloat16 [2, 4, 1024, 1600], P(None, 'dp', 'ctx'), may hold values from -6 to 6
- w_qkv: bfloat16 [7680000], P(('dp', 'ctx')), may hold values from -1.5 to 1.5
- w_proj: bfloat16 [2560000], P(('dp', 'ctx')), may hold values from -2.5 to 2.5
- w_fc: bfloat16 [10240000], P(('dp', 'ctx')), may hold values from -0.15625 to 0.15625
- w_out: bfloat16 [10240000], P(('dp', 'ctx')), may hold values from -0.15625 to 0.15625
- smalls: bfloat16 [19200], P(('dp', 'ctx')), may hold values from -1.3 to 1.5
Outputs:
- outputs: bfloat16 [2, 4, 1024, 1600], P(None, 'dp', 'ctx')
- grad_in: float32 [2, 4, 1024, 1600], P(None, 'dp', 'ctx')
- grad_qkv: float32 [7680000], P(('dp', 'ctx'))
- grad_proj: float32 [2560000], P(('dp', 'ctx'))
- grad_fc: float32 [10240000], P(('dp', 'ctx'))
- grad_out_w: float32 [10240000], P(('dp', 'ctx'))
- grad_smalls: float32 [6400], P(('dp', 'ctx'))
- grad_rest: float32 [12800], P(('dp', 'ctx'))
All inputs are finite; a program needn't handle non-finite values.
Results may differ from a plain program's by a relative error of at most 0.012.
Values may be sent and summed in bfloat16 or wider, within the bound.
A program may use at most 448 MiB of HBM per device.

v0:
```python
import jax
import jax.numpy as jnp
from jax import lax
from jax.sharding import PartitionSpec as P

D = 1600
HEADS = 25
HEAD = 64
FF = 6400
MICRO = 2


EPS = 1e-05


def layer_norm(values, gain, shift):
    center = values - jnp.mean(values, axis=-1, keepdims=True)
    spread = jnp.mean(center * center, axis=-1, keepdims=True)
    return center * lax.rsqrt(spread + EPS) * gain + shift


def gelu_tanh(values):
    return jax.nn.gelu(values, approximate=True)


def unpack(gathered):
    packed_qkv, packed_proj, packed_fc, packed_out, packed_small = gathered
    return (
        packed_qkv.reshape(D, 3 * D),
        packed_proj.reshape(D, D),
        packed_fc.reshape(D, FF),
        packed_out.reshape(FF, D),
        packed_small.astype(jnp.float32),
    )


def fetch(w_qkv, w_proj, w_fc, w_out, smalls):
    return unpack(
        (
            lax.all_gather(w_qkv, ("dp", "ctx"), axis=0, tiled=True),
            lax.all_gather(w_proj, ("dp", "ctx"), axis=0, tiled=True),
            lax.all_gather(w_fc, ("dp", "ctx"), axis=0, tiled=True),
            lax.all_gather(w_out, ("dp", "ctx"), axis=0, tiled=True),
            lax.all_gather(smalls, ("dp", "ctx"), axis=0, tiled=True),
        )
    )


def fetch_again(w_qkv, w_proj, w_fc, w_out, smalls):
    return unpack(
        (
            lax.all_gather(w_qkv, ("dp", "ctx"), axis=0, tiled=True),
            lax.all_gather(w_proj, ("dp", "ctx"), axis=0, tiled=True),
            lax.all_gather(w_fc, ("dp", "ctx"), axis=0, tiled=True),
            lax.all_gather(w_out, ("dp", "ctx"), axis=0, tiled=True),
            lax.all_gather(smalls, ("dp", "ctx"), axis=0, tiled=True),
        )
    )


def outer_sum(left, right):
    return lax.dot_general(
        left, right, (((0,), (0,)), ((), ())), preferred_element_type=jnp.float32
    )


def back_product(grad, weight):
    return lax.dot_general(
        grad, weight, (((1,), (1,)), ((), ())), preferred_element_type=jnp.float32
    )


def flat_term(left, right, start, count):
    width = right.shape[1]
    span = count // width + 2
    padded = jnp.pad(left, ((0, 0), (0, span)))
    first_row = start // width
    piece = lax.dynamic_slice_in_dim(padded, first_row, span, 1)
    block = outer_sum(piece, right).reshape(-1)
    return lax.dynamic_slice_in_dim(block, start, count, 0)


def masked_scores(queries, keys, query_start, key_start):
    scores = (
        jnp.einsum("sqhe,skhe->shqk", queries, keys, preferred_element_type=jnp.float32) * 0.125
    )
    query_pos = query_start + jnp.arange(queries.shape[1])
    key_pos = key_start + jnp.arange(keys.shape[1])
    allowed = query_pos[:, None] >= key_pos[None, :]
    return jnp.where(allowed[None, None], scores, -1e30)


def segment(small_vals, which):
    return small_vals[which * D : (which + 1) * D]


def shards(inputs, grad_out, w_qkv, w_proj, w_fc, w_out, smalls):
    seqs = inputs.shape[1]
    local_len = inputs.shape[2]
    rows = seqs * local_len
    offset = lax.axis_index("ctx") * local_len
    acc_small = [jnp.zeros((D,), jnp.float32) for _ in range(7)]
    acc_fc_bias = jnp.zeros((FF,), jnp.float32)
    acc_out_bias = jnp.zeros((D,), jnp.float32)
    result_list = []
    grad_list = []
    kept_hidden_one = []
    kept_mixed_grad = []
    kept_context = []
    kept_branch_grad = []
    kept_hidden_two = []
    kept_pre_grad = []
    kept_activ = []
    kept_out_grad = []
    for batch_index in range(MICRO):
        params = fetch(w_qkv, w_proj, w_fc, w_out, smalls)
        mat_qkv, mat_proj, mat_fc, mat_out, small_vals = params
        tokens = inputs[batch_index].astype(jnp.float32).reshape(rows, D)
        hidden_one, ln1_pull = jax.vjp(
            layer_norm, tokens, segment(small_vals, 0), segment(small_vals, 1)
        )
        hidden_one = hidden_one.astype(jnp.bfloat16)
        qkv_bias = jnp.concatenate(
            [segment(small_vals, 2), jnp.zeros((D,), jnp.float32), segment(small_vals, 3)]
        )
        mixed = (
            jnp.dot(hidden_one, mat_qkv, preferred_element_type=jnp.float32) + qkv_bias
        ).astype(jnp.bfloat16)
        queries = mixed[:, :D].reshape(seqs, local_len, HEADS, HEAD)
        keys_local = mixed[:, D : 2 * D].reshape(seqs, local_len, D)
        values_local = mixed[:, 2 * D :].reshape(seqs, local_len, D)
        keys_all, values_all = (
            lax.all_gather(keys_local, "ctx", axis=1, tiled=True),
            lax.all_gather(values_local, "ctx", axis=1, tiled=True),
        )
        keys_all = keys_all.reshape(seqs, -1, HEADS, HEAD)
        values_all = values_all.reshape(seqs, -1, HEADS, HEAD)
        scores = masked_scores(queries, keys_all, offset, 0)
        row_peak = jnp.max(scores, axis=-1, keepdims=True)
        log_total = row_peak + jnp.log(jnp.sum(jnp.exp(scores - row_peak), axis=-1, keepdims=True))
        attn_low = jnp.exp(scores - log_total).astype(jnp.bfloat16)
        context = jnp.einsum(
            "shqk,skhe->sqhe", attn_low, values_all, preferred_element_type=jnp.float32
        )
        context = context.reshape(rows, D).astype(jnp.bfloat16)
        resid = (
            tokens
            + jnp.dot(context, mat_proj, preferred_element_type=jnp.float32)
            + segment(small_vals, 4)
        )
        hidden_two, ln2_pull = jax.vjp(
            layer_norm, resid, segment(small_vals, 5), segment(small_vals, 6)
        )
        hidden_two = hidden_two.astype(jnp.bfloat16)
        pre_act = (
            jnp.dot(hidden_two, mat_fc, preferred_element_type=jnp.float32)
            + small_vals[7 * D : 7 * D + FF]
        )
        activ, gelu_pull = jax.vjp(gelu_tanh, pre_act)
        activ = activ.astype(jnp.bfloat16)
        result = (
            resid
            + jnp.dot(activ, mat_out, preferred_element_type=jnp.float32)
            + small_vals[7 * D + FF :]
        )
        result_list.append(result.astype(jnp.bfloat16).reshape(seqs, local_len, D))
        back_params = fetch_again(w_qkv, w_proj, w_fc, w_out, smalls)
        mat_qkv, mat_proj, mat_fc, mat_out, small_vals = back_params
        grad_low = grad_out[batch_index].reshape(rows, D)
        grad_full = grad_low.astype(jnp.float32)
        acc_out_bias = acc_out_bias + jnp.sum(grad_full, axis=0)
        grad_act = back_product(grad_low, mat_out)
        (grad_pre,) = gelu_pull(grad_act)
        grad_pre = grad_pre.astype(jnp.bfloat16)
        acc_fc_bias = acc_fc_bias + jnp.sum(grad_pre.astype(jnp.float32), axis=0)
        grad_hidden_two = back_product(grad_pre, mat_fc)
        grad_ln_two, grad_gain_two, grad_shift_two = ln2_pull(grad_hidden_two)
        acc_small[5] = acc_small[5] + grad_gain_two
        acc_small[6] = acc_small[6] + grad_shift_two
        grad_resid = grad_full + grad_ln_two
        grad_branch = grad_resid.astype(jnp.bfloat16)
        acc_small[4] = acc_small[4] + jnp.sum(grad_branch.astype(jnp.float32), axis=0)
        grad_context = (
            back_product(grad_branch, mat_proj)
            .astype(jnp.bfloat16)
            .reshape(seqs, local_len, HEADS, HEAD)
        )
        scores = masked_scores(queries, keys_all, offset, 0)
        attn_prob = jnp.exp(scores - log_total)
        grad_attn = jnp.einsum(
            "sqhe,skhe->shqk", grad_context, values_all, preferred_element_type=jnp.float32
        )
        row_delta = jnp.sum(attn_prob * grad_attn, axis=-1, keepdims=True)
        grad_scores = (attn_prob * (grad_attn - row_delta)).astype(jnp.bfloat16)
        grad_queries = (
            jnp.einsum("shqk,skhe->sqhe", grad_scores, keys_all, preferred_element_type=jnp.float32)
            * 0.125
        )
        query_all, dctx_all = (
            lax.all_gather(queries.reshape(seqs, local_len, D), "ctx", axis=1, tiled=True),
            lax.all_gather(grad_context.reshape(seqs, local_len, D), "ctx", axis=1, tiled=True),
        )
        lse_all, delta_all = (
            lax.all_gather(jnp.transpose(log_total[..., 0], (0, 2, 1)), "ctx", axis=1, tiled=True),
            lax.all_gather(jnp.transpose(row_delta[..., 0], (0, 2, 1)), "ctx", axis=1, tiled=True),
        )
        query_all = query_all.reshape(seqs, -1, HEADS, HEAD)
        dctx_all = dctx_all.reshape(seqs, -1, HEADS, HEAD)
        lse_all = jnp.transpose(lse_all, (0, 2, 1))[..., None]
        delta_all = jnp.transpose(delta_all, (0, 2, 1))[..., None]
        own_keys = keys_local.reshape(seqs, local_len, HEADS, HEAD)
        own_values = values_local.reshape(seqs, local_len, HEADS, HEAD)
        col_scores = masked_scores(query_all, own_keys, 0, offset)
        col_prob = jnp.exp(col_scores - lse_all)
        col_dattn = jnp.einsum(
            "sqhe,skhe->shqk", dctx_all, own_values, preferred_element_type=jnp.float32
        )
        col_ds = (col_prob * (col_dattn - delta_all)).astype(jnp.bfloat16)
        grad_keys = (
            jnp.einsum("shqk,sqhe->skhe", col_ds, query_all, preferred_element_type=jnp.float32)
            * 0.125
        )
        grad_values = jnp.einsum(
            "shqk,sqhe->skhe",
            col_prob.astype(jnp.bfloat16),
            dctx_all,
            preferred_element_type=jnp.float32,
        )
        grad_mixed = jnp.concatenate(
            [
                grad_queries.reshape(rows, D),
                grad_keys.reshape(rows, D),
                grad_values.reshape(rows, D),
            ],
            axis=1,
        ).astype(jnp.bfloat16)
        bias_terms = jnp.sum(grad_mixed.astype(jnp.float32), axis=0)
        acc_small[2] = acc_small[2] + bias_terms[:D]
        acc_small[3] = acc_small[3] + bias_terms[2 * D :]
        grad_hidden_one = back_product(grad_mixed, mat_qkv)
        grad_ln_one, grad_gain_one, grad_shift_one = ln1_pull(grad_hidden_one)
        acc_small[0] = acc_small[0] + grad_gain_one
        acc_small[1] = acc_small[1] + grad_shift_one
        grad_list.append((grad_resid + grad_ln_one).reshape(seqs, local_len, D))
        kept_hidden_one.append(hidden_one)
        kept_mixed_grad.append(grad_mixed)
        kept_context.append(context)
        kept_branch_grad.append(grad_branch)
        kept_hidden_two.append(hidden_two)
        kept_pre_grad.append(grad_pre)
        kept_activ.append(activ)
        kept_out_grad.append(grad_low)
    front_grads = jnp.concatenate(acc_small[0:4])
    tail_grads = jnp.concatenate(acc_small[4:7] + [acc_fc_bias, acc_out_bias])
    grad_qkv = lax.psum_scatter(
        flat_term(
            jnp.concatenate(kept_hidden_one),
            jnp.concatenate(kept_mixed_grad),
            jnp.int32(0),
            lax.axis_size(("dp", "ctx")) * w_qkv.shape[0],
        ),
        ("dp", "ctx"),
        scatter_dimension=0,
        tiled=True,
    )
    grad_proj = lax.psum_scatter(
        flat_term(
            jnp.concatenate(kept_context),
            jnp.concatenate(kept_branch_grad),
            jnp.int32(0),
            lax.axis_size(("dp", "ctx")) * w_proj.shape[0],
        ),
        ("dp", "ctx"),
        scatter_dimension=0,
        tiled=True,
    )
    grad_fc = lax.psum_scatter(
        flat_term(
            jnp.concatenate(kept_hidden_two),
            jnp.concatenate(kept_pre_grad),
            jnp.int32(0),
            lax.axis_size(("dp", "ctx")) * w_fc.shape[0],
        ),
        ("dp", "ctx"),
        scatter_dimension=0,
        tiled=True,
    )
    grad_out_w = lax.psum_scatter(
        flat_term(
            jnp.concatenate(kept_activ),
            jnp.concatenate(kept_out_grad),
            jnp.int32(0),
            lax.axis_size(("dp", "ctx")) * w_out.shape[0],
        ),
        ("dp", "ctx"),
        scatter_dimension=0,
        tiled=True,
    )
    grad_front, grad_tail = (
        lax.psum_scatter(front_grads, ("dp", "ctx"), scatter_dimension=0, tiled=True),
        lax.psum_scatter(tail_grads, ("dp", "ctx"), scatter_dimension=0, tiled=True),
    )
    return (
        jnp.stack(result_list),
        jnp.stack(grad_list),
        grad_qkv,
        grad_proj,
        grad_fc,
        grad_out_w,
        grad_front,
        grad_tail,
    )


def solution(mesh):
    placed = (
        P(None, "dp", "ctx", None),
        P(None, "dp", "ctx", None),
        P(("dp", "ctx")),
        P(("dp", "ctx")),
        P(("dp", "ctx")),
        P(("dp", "ctx")),
        P(("dp", "ctx")),
    )
    return jax.shard_map(
        shards,
        mesh=mesh,
        in_specs=placed,
        out_specs=(
            P(None, "dp", "ctx", None),
            P(None, "dp", "ctx", None),
            P(("dp", "ctx")),
            P(("dp", "ctx")),
            P(("dp", "ctx")),
            P(("dp", "ctx")),
            P(("dp", "ctx")),
            P(("dp", "ctx")),
        ),
        check_vma=False,
    )
```

profile of v0, /device:TPU:0, one launch (start us, length us, event | category | flops | bytes accessed | tf_op | source)
XLA Modules:
  0.0 3782.5 jit_solution(4601798413777071998)
XLA Ops:
  7.2 6.3 reshape.651
  16.3 44.1 %all-reduce.4 = bf16[19200]{0:T(1024)(128)(2,1)S(1)} all-reduce(bf16[19200]{0:T(1024)(128)(2,1)S(1)} %dynamic-update-slice), channel_id=1, replica_groups=mesh['dp'=4,'ctx'=8] {'dp','ctx'}, use_global_device_ids=true, to_apply=%add.4 | all-reduce | flops 19200 | bytes 76800
  61.7 137.4 %all-gather.41.cloned.1.call-done = bf16[32,1,240000]{2,1,0:T(2,128)(2,1)} async-done(((bf16[1,1,240000]{2,1,0:T(2,128)(2,1)}), bf16[32,1,240000]{2,1,0:T(2,128)(2,1)}) %all-gather.41.cloned.1.call-update) | async-done | bytes 15360016 | tf_op jit(solution)/shard_map/all_gather | solution.py:40
  199.1 316.5 %reduce.14 = bf16[32,240000]{1,0:T(8,128)(2,1)} reduce(bf16[32,1,240000]{2,1,0:T(2,128)(2,1)} %all-gather.41.cloned.1.call-done, bf16[]{:T(256)} %constant.142), dimensions={1}, to_apply=%all-gather.8.reduce_sub_computation | reduce | bytes 30720002 | tf_op jit(solution)/shard_map/all_gather | solution.py:40
  515.6 17.8 reshape.603
  533.4 12.1 fusion.14
  548.2 12.4 fusion.15
  562.3 8.1 reshape.655
  570.6 8.1 reshape.657
  580.9 32.6 reduce.15
  613.6 9.2 reshape.609
  623.1 4.3 fusion.168
  627.5 2.5 exponential_reduce_fusion.1
  632.2 42.1 %all-gather.25.cloned.1.call-done = bf16[1024,1600]{0,1:T(8,128)(2,1)} async-done(((bf16[128,1600]{0,1:T(8,128)(2,1)}), bf16[1024,1600]{0,1:T(8,128)(2,1)}) %all-gather.25.cloned.1.call-update) | async-done | bytes 3276816 | tf_op jit(solution)/shard_map/all_gather | solution.py:134
  674.3 8.3 fusion.74
  687.2 51.8 %all-gather.31.cloned.1.call-done = bf16[1024,1600]{0,1:T(8,128)(2,1)} async-done(((bf16[128,1600]{0,1:T(8,128)(2,1)}), bf16[1024,1600]{0,1:T(8,128)(2,1)}) %all-gather.31.cloned.1.call-update) | async-done | bytes 3276816 | tf_op jit(solution)/shard_map/all_gather | solution.py:133
  739.0 4.9 fusion.167
  743.9 3.4 exponential_reduce_fusion
  749.1 54.5 %all-gather.29.cloned.1.call-done = bf16[1024,1600]{0,1:T(8,128)(2,1)} async-done(((bf16[128,1600]{0,1:T(8,128)(2,1)}), bf16[1024,1600]{0,1:T(8,128)(2,1)}) %all-gather.29.cloned.1.call-update) | async-done | bytes 3276816 | tf_op jit(solution)/shard_map/all_gather | solution.py:134
  803.7 8.3 fusion.77
  815.9 220.0 %all-gather.45.cloned.1.call-done = bf16[32,1,320000]{2,1,0:T(2,128)(2,1)} async-done(((bf16[1,1,320000]{2,1,0:T(2,128)(2,1)}), bf16[32,1,320000]{2,1,0:T(2,128)(2,1)}) %all-gather.45.cloned.1.call-update) | async-done | bytes 20480016 | tf_op jit(solution)/shard_map/all_gather | solution.py:42
  1035.9 123.8 %reduce.16 = bf16[32,320000]{1,0:T(8,128)(2,1)} reduce(bf16[32,1,320000]{2,1,0:T(2,128)(2,1)} %all-gather.45.cloned.1.call-done, bf16[]{:T(256)} %constant.142), dimensions={1}, to_apply=%all-gather.10.reduce_sub_computation | reduce | bytes 40960000 | tf_op jit(solution)/shard_map/all_gather | solution.py:42
  1159.7 49.4 %reshape.610 = bf16[1600,6400]{1,0:T(8,128)(2,1)} reshape(bf16[32,320000]{1,0:T(8,128)(2,1)} %reduce.16) | data formatting | bytes 40960000 | tf_op jit(solution)/shard_map/reshape | solution.py:31
  1209.1 58.8 %all-gather.47.cloned.1.call-done = bf16[32,1,320000]{2,1,0:T(2,128)(2,1)} async-done(((bf16[1,1,320000]{2,1,0:T(2,128)(2,1)}), bf16[32,1,320000]{2,1,0:T(2,128)(2,1)}) %all-gather.47.cloned.1.call-update) | async-done | bytes 20480016 | tf_op jit(solution)/shard_map/all_gather | solution.py:43
  1268.0 122.1 %reduce.17 = bf16[32,320000]{1,0:T(8,128)(2,1)} reduce(bf16[32,1,320000]{2,1,0:T(2,128)(2,1)} %all-gather.47.cloned.1.call-done, bf16[]{:T(256)} %constant.142), dimensions={1}, to_apply=%all-gather.11.reduce_sub_computation | reduce | bytes 40960000 | tf_op jit(solution)/shard_map/all_gather | solution.py:43
  1390.1 36.4 reshape.611
  1426.5 13.2 multiply_convert_fusion.7
  1439.7 12.7 multiply_convert_fusion.6
  1452.5 12.7 convert_reduce_fusion
  1465.2 10.2 fusion.171
  1475.5 12.2 convert_reduce_fusion.1
  1487.7 12.2 multiply_reduce_fusion.3
  1503.2 2.4 convolution_convert_fusion
  1507.3 31.2 all_gather.74
  1538.5 31.2 all_gather.78
  1569.8 9.6 subtract_exponential_fusion.1
  1579.4 9.3 subtract_exponential_fusion
  1591.1 17.9 fusion.30
  1609.0 13.8 multiply_reduce_fusion.1
  1622.8 10.8 multiply_reduce_fusion
  1633.7 18.2 fusion.34
  1651.9 6.8 fusion.115
  1658.7 13.2 dynamic_slice.37
  1671.9 39.9 %dynamic_slice.40 = f32[10240000]{0:T(1024)} reshape(f32[1600,6400]{1,0:T(8,128)} %fusion.30) | data formatting | bytes 81920000 | tf_op jit(solution)/shard_map/dynamic_slice | solution.py:80
  1711.8 48.0 %dynamic_slice.43 = f32[10240000]{0:T(1024)} reshape(f32[6400,1600]{1,0:T(8,128)} %fusion.34) | data formatting | bytes 81920000 | tf_op jit(solution)/shard_map/dynamic_slice | solution.py:80
  1760.6 30.5 all_gather.76
  1791.1 30.7 all_gather.80
  1821.8 11.2 fusion.64
  1833.0 13.3 fusion.65
  1846.4 7.6 fusion.71
  1854.0 12.4 fusion.67
  1868.0 11.3 fusion.130
  1879.3 6.8 fusion.68
  1886.2 12.5 fusion.66
  1899.2 10.1 fusion.103
  1912.3 15.3 fusion.40
  1927.6 36.6 dynamic_slice.34
  1965.3 12.4 fusion.57
  1977.7 12.3 fusion.56
  1995.9 34.9 all-reduce.16.cloned.1.call-done
  2033.4 1732.6 %all-reduce.18.cloned.1.call-done = (f32[7680000]{0:T(1024)}, f32[2560000]{0:T(1024)}, f32[10240000]{0:T(1024)}, f32[10240000]{0:T(1024)}) async-done(((f32[7680000]{0:T(1024)}, f32[2560000]{0:T(1024)}, f32[10240000]{0:T(1024)}, f32[10240000]{0:T(1024)}), (f32[7680000]{0:T(1024)}, f32[2560000]{0:T(1024)}, f32[10240000]{0:T(1024)}, f32[10240000]{0:T(1024)})) %all-reduce.18.cloned.1.call-update) | async-done | bytes 122880016
  3766.0 2.8 dynamic-slice.2
  3768.7 2.8 dynamic-slice.3
  3771.5 2.5 dynamic-slice
  (291 shorter events, 47.9 us)
Async XLA Ops:
  7.2 54.0 %copy-start.2 = (bf16[2,1,128,1600]{2,3,1,0:T(8,128)(2,1)S(1)}, bf16[2,1,128,1600]{2,3,1,0:T(8,128)(2,1)}, u32[]{:S(2)}) copy-start(bf16[2,1,128,1600]{2,3,1,0:T(8,128)(2,1)} %param.7) | copy-start | bytes 2457604
  7.2 191.9 %all-gather.41.cloned.1.call-start = ((), (), s32[]{:S(2)}) async-start(), calls=%async_computation.8 | async-start | bytes 31680000 | tf_op jit(solution)/shard_map/all_gather | solution.py:40
  13.5 567.4 %all-gather.43.cloned.1.call-start = ((), (), s32[]{:S(2)}) async-start(), calls=%async_computation.9 | async-start | bytes 10560000 | tf_op jit(solution)/shard_map/all_gather | solution.py:41
  15.4 607.7 %all-gather.27.cloned.1.call-start = ((), (), s32[]{:S(2)}) async-start(), calls=%async_computation.1 | async-start | bytes 3686400 | tf_op jit(solution)/shard_map/all_gather | solution.py:133
  61.1 486.5 %copy-start.52 = (f32[1600]{0:T(1024)}, f32[1600]{0:T(1024)S(1)}, u32[]{:S(2)}) copy-start(f32[1600]{0:T(1024)S(1)} %get-tuple-element.70) | copy-start | bytes 19204
  61.1 486.6 %copy-start.57 = (f32[1600]{0:T(1024)}, f32[1600]{0:T(1024)S(1)}, u32[]{:S(2)}) copy-start(f32[1600]{0:T(1024)S(1)} %get-tuple-element.71) | copy-start | bytes 19204
  61.4 471.9 %copy-start.68 = (f32[128]{0:T(128)}, f32[128]{0:T(128)S(1)}, u32[]{:S(2)}) copy-start(f32[128]{0:T(128)S(1)} %get-tuple-element.104) | copy-start | bytes 1540
  61.5 486.2 %copy-start.66 = (f32[128]{0:T(128)}, f32[128]{0:T(128)S(1)}, u32[]{:S(2)}) copy-start(f32[128]{0:T(128)S(1)} %get-tuple-element.103) | copy-start | bytes 1540
  61.7 453.9 %copy-start.85 = (f32[128]{0:T(128)}, f32[128]{0:T(128)S(1)}, u32[]{:S(2)}) copy-start(f32[128]{0:T(128)S(1)} %get-tuple-element.26) | copy-start | bytes 1540
  61.7 485.9 %copy-start.83 = (f32[128]{0:T(128)}, f32[128]{0:T(128)S(1)}, u32[]{:S(2)}) copy-start(f32[128]{0:T(128)S(1)} %get-tuple-element.27) | copy-start | bytes 1540
  61.7 471.6 %copy-start.72 = (f32[128]{0:T(128)}, f32[128]{0:T(128)S(1)}, u32[]{:S(2)}) copy-start(f32[128]{0:T(128)S(1)} %fusion.148) | copy-start | bytes 1540
  546.6 127.7 %all-gather.25.cloned.1.call-start = ((), (), s32[]{:S(2)}) async-start(), calls=%async_computation | async-start | bytes 3686400 | tf_op jit(solution)/shard_map/all_gather | solution.py:134
  547.2 191.8 %all-gather.31.cloned.1.call-start = ((), (), s32[]{:S(2)}) async-start(), calls=%async_computation.3 | async-start | bytes 3686400 | tf_op jit(solution)/shard_map/all_gather | solution.py:133
  561.7 242.0 %all-gather.29.cloned.1.call-start = ((), (), s32[]{:S(2)}) async-start(), calls=%async_computation.2 | async-start | bytes 3686400 | tf_op jit(solution)/shard_map/all_gather | solution.py:134
  562.3 473.6 %all-gather.45.cloned.1.call-start = ((), (), s32[]{:S(2)}) async-start(), calls=%async_computation.10 | async-start | bytes 42240000 | tf_op jit(solution)/shard_map/all_gather | solution.py:42
  570.4 697.6 %all-gather.47.cloned.1.call-start = ((), (), s32[]{:S(2)}) async-start(), calls=%async_computation.11 | async-start | bytes 42240000 | tf_op jit(solution)/shard_map/all_gather | solution.py:43
  578.7 991.1 %all-gather.33.cloned.1.call-start = ((), (), s32[]{:S(2)}) async-start(), calls=%async_computation.4 | async-start | bytes 3686400 | tf_op jit(solution)/shard_map/all_gather | solution.py:200
  579.5 999.9 %all-gather.37.cloned.1.call-start = ((), (), s32[]{:S(2)}) async-start(), calls=%async_computation.6 | async-start | bytes 3686400 | tf_op jit(solution)/shard_map/all_gather | solution.py:200
  580.9 42.2 %copy-start.46 = (pred[128,1024]{1,0:T(8,128)(4,1)}, pred[128,1024]{1,0:T(8,128)(4,1)S(1)}, u32[]{:S(2)}) copy-start(pred[128,1024]{1,0:T(8,128)(4,1)S(1)} %iota_compare_fusion.1) | copy-start | bytes 393220
  622.8 1223.6 %all-gather.39.cloned.1.call-start = ((), (), s32[]{:S(2)}) async-start(), calls=%async_computation.7 | async-start | bytes 3686400 | tf_op jit(solution)/shard_map/all_gather | solution.py:201
  627.5 55.2 %slice-start = ((s8[5324800]{0:T(1024)(128)(4,1)}), s8[1130496]{0:T(1024)(128)(4,1)S(1)}, s32[]{:S(2)}) async-start(s8[5324800]{0:T(1024)(128)(4,1)} %bitcast.240), calls=%async_computation.14 | async-start | bytes 2260992
  682.7 56.3 %copy-start.30 = (bf16[128,1600]{0,1:T(8,128)(2,1)S(1)}, bf16[128,1600]{0,1:T(8,128)(2,1)}, u32[]{:S(2)}) copy-start(bf16[128,1600]{0,1:T(8,128)(2,1)} %get-tuple-element.50) | copy-start | bytes 1228804
  743.9 68.1 %slice-start.2 = ((s8[5324800]{0:T(1024)(128)(4,1)}), s8[1130496]{0:T(1024)(128)(4,1)S(1)}, s32[]{:S(2)}) async-start(s8[5324800]{0:T(1024)(128)(4,1)} %bitcast.242), calls=%async_computation.16 | async-start | bytes 2260992
  749.1 873.7 %copy-start.49 = (f32[25,128]{1,0:T(8,128)}, f32[25,128]{1,0:T(8,128)S(1)}, u32[]{:S(2)}) copy-start(f32[25,128]{1,0:T(8,128)S(1)} %log_add_fusion) | copy-start | bytes 38404
  815.9 623.9 %copy-start.27 = (bf16[128,1600]{0,1:T(8,128)(2,1)}, bf16[128,1600]{0,1:T(8,128)(2,1)S(1)}, u32[]{:S(2)}) copy-start(bf16[128,1600]{0,1:T(8,128)(2,1)S(1)} %get-tuple-element.75) | copy-start | bytes 1228804
  1390.1 36.4 copy-start.51
  1439.7 12.7 copy-start.20
  1452.5 181.1 %copy-start.13 = (bf16[128,6400]{1,0:T(8,128)(2,1)}, bf16[128,6400]{1,0:T(8,128)(2,1)S(1)}, u32[]{:S(2)}) copy-start(bf16[128,6400]{1,0:T(8,128)(2,1)S(1)} %get-tuple-element.89) | copy-start | bytes 4915204
  1475.5 12.2 copy-start.8
  1475.5 12.2 copy-start.11
  1487.7 12.2 copy-start.18
  1487.7 15.5 slice-start.4
  1487.7 12.3 copy-start.88
  1487.7 15.5 slice-start.5
  1505.6 373.8 %all-gather.35.cloned.1.call-start = ((), (), s32[]{:S(2)}) async-start(), calls=%async_computation.5 | async-start | bytes 3686400 | tf_op jit(solution)/shard_map/all_gather | solution.py:201
  1569.8 18.9 slice-start.6
  1591.1 17.9 copy-start.45
  1609.0 421.8 %all-reduce.16.cloned.1.call-start = ((), (), s32[]{:S(2)}) async-start(), calls=%async_computation.12 | async-start | bytes 163840
  1609.0 13.8 copy-start.17
  1609.0 13.8 copy-start.44
  1622.8 137.8 %copy-start.55 = (f32[25,128]{1,0:T(8,128)}, f32[25,128]{1,0:T(8,128)S(1)}, u32[]{:S(2)}) copy-start(f32[25,128]{1,0:T(8,128)S(1)} %get-tuple-element.96) | copy-start | bytes 38404
  1622.8 10.8 copy-start.14
  1622.8 10.8 copy-start.41
  1633.6 18.2 copy-start.32
  1633.6 18.2 copy-start.34
  1711.8 48.0 %copy-start.64 = (f32[6400]{0:T(1024)S(1)}, f32[6400]{0:T(1024)}, u32[]{:S(2)}) copy-start(f32[6400]{0:T(1024)} %get-tuple-element.101) | copy-start | bytes 76804
  1711.8 48.0 %copy-start.65 = (f32[6400]{0:T(1024)S(1)}, f32[6400]{0:T(1024)}, u32[]{:S(2)}) copy-start(f32[6400]{0:T(1024)} %get-tuple-element.99) | copy-start | bytes 76804
  1711.8 110.0 %copy-start.16 = (bf16[1024,1600]{0,1:T(8,128)(2,1)S(1)}, bf16[1024,1600]{0,1:T(8,128)(2,1)}, u32[]{:S(2)}) copy-start(bf16[1024,1600]{0,1:T(8,128)(2,1)} %all-gather.27.cloned.1.call-done) | copy-start | bytes 9830404
  1821.8 11.2 copy-start.50
  1821.8 11.2 copy-start.54
  1886.1 12.5 copy-start.37
  1886.1 12.9 copy-start.5
  1886.1 12.9 copy-start.53
  1886.1 12.9 copy-start.67
  1886.2 12.9 copy-start.69
  1899.1 10.3 copy-start.39
  1899.1 10.3 copy-start.58
  1899.1 10.3 copy-start.73
  1912.2 1853.8 %all-reduce.18.cloned.1.call-start = ((), (), s32[]{:S(2)}) async-start(), calls=%async_computation.13 | async-start | bytes 245760000
  1965.3 12.4 copy-start.12
  1977.7 14.5 copy-start.23
  1977.7 14.5 copy-start.25
  1977.7 14.5 copy-start.78
  1977.7 14.5 copy-start.80
  (47 other events, 221.3 us)
Sparse Core Ops, SparseCore 0:
  13.6 185.4 all-gather.40
  202.6 83.7 all-gather.42
  546.7 62.7 all-gather.26
  611.4 62.8 all-gather.24
  676.2 62.7 all-gather.30
  740.9 62.7 all-gather.28
  807.0 228.7 all-gather.44
  1039.3 228.6 all-gather.46
  1270.0 62.7 all-gather.32
  1334.7 62.7 all-gather.36
  1505.7 64.9 all-gather.38
  1609.1 62.9 all-gather.34
  1912.3 118.3 all-reduce.15
  2037.0 1728.9 all-reduce.17
where the time goes:
time: 3790 us; the launch traced here: 3780 us
  waiting for transfers between devices  2330 us (61%)
  other arithmetic  616 us (16%)
  matrix products  345 us (9%)
  local copies, waits for them, and re-layouts  304 us (8%)
  blocking collectives  168 us (4%)
    unnamed x16, waiting for transfers between devices  1770 us
    all_gather x1, other arithmetic, fetch(): lax.all_gather(w_qkv, ('dp', 'ctx'), axis=0, tiled=True)  316 us
    all_gather x1, waiting for transfers between devices, fetch(): lax.all_gather(w_fc, ('dp', 'ctx'), axis=0, tiled=True)  220 us
    dynamic_slice x4, local copies, waits for them, and re-layouts, flat_term(): return lax.dynamic_slice_in_dim(block, start, count, 0)  138 us
    all_gather x1, waiting for transfers between devices, fetch(): lax.all_gather(w_qkv, ('dp', 'ctx'), axis=0, tiled=True)  137 us
    all_gather x1, other arithmetic, fetch(): lax.all_gather(w_fc, ('dp', 'ctx'), axis=0, tiled=True)  124 us
    all_gather x1, other arithmetic, fetch(): lax.all_gather(w_out, ('dp', 'ctx'), axis=0, tiled=True)  122 us
    all_gather x2, waiting for transfers between devices, shards(): lax.all_gather(values_local, 'ctx', axis=1, tiled=True)  96.6 us
  transfers between devices with their start and end apart: 14, of which 8 were waited for; matrix products, arithmetic and copies ran while one was open for 32% of the time, Pallas kernels for 0%

commit v1 on v0

--- a/solution.py
+++ b/solution.py
@@ -76,7 +76,7 @@
     padded = jnp.pad(left, ((0, 0), (0, span)))
     first_row = start // width
     piece = lax.dynamic_slice_in_dim(padded, first_row, span, 1)
-    block = outer_sum(piece, right).reshape(-1)
+    block = outer_sum(piece, right).astype(jnp.bfloat16).reshape(-1)
     return lax.dynamic_slice_in_dim(block, start, count, 0)
 
 
@@ -262,7 +262,7 @@
         ("dp", "ctx"),
         scatter_dimension=0,
         tiled=True,
-    )
+    ).astype(jnp.float32)
     grad_proj = lax.psum_scatter(
         flat_term(
             jnp.concatenate(kept_context),
@@ -273,7 +273,7 @@
         ("dp", "ctx"),
         scatter_dimension=0,
         tiled=True,
-    )
+    ).astype(jnp.float32)
     grad_fc = lax.psum_scatter(
         flat_term(
             jnp.concatenate(kept_hidden_two),
@@ -284,7 +284,7 @@
         ("dp", "ctx"),
         scatter_dimension=0,
         tiled=True,
-    )
+    ).astype(jnp.float32)
     grad_out_w = lax.psum_scatter(
         flat_term(
             jnp.concatenate(kept_activ),
@@ -295,7 +295,7 @@
         ("dp", "ctx"),
         scatter_dimension=0,
         tiled=True,
-    )
+    ).astype(jnp.float32)
     grad_front, grad_tail = (
         lax.psum_scatter(front_grads, ("dp", "ctx"), scatter_dimension=0, tiled=True),
         lax.psum_scatter(tail_grads, ("dp", "ctx"), scatter_dimension=0, tiled=True),
@@ -312,6 +312,297 @@
     )
 
 
+DP, CTX = 4, 8
+ZN, XN, YN, CN = 4, 2, 2, 2
+NDEV = 32
+AXES = ("dp", "ctx")
+SLOTS = 7
+HW = SLOTS * HEAD
+STARTS = (0, 7, 13, 19)
+COUNTS = (7, 6, 6, 6)
+BLK = 128
+
+
+def place(index):
+    dp, ctx = divmod(index, CTX)
+    y, c = divmod(dp, CN)
+    z, x = divmod(ctx, XN)
+    return y, c, z, x
+
+
+def number(y, c, z, x):
+    return (y * CN + c) * CTX + z * XN + x
+
+
+def pairs(target):
+    found = []
+    for index in range(NDEV):
+        where = target(*place(index))
+        if where is not None:
+            found.append((index, number(*where)))
+    return found
+
+
+def send(values, target):
+    return lax.ppermute(values, AXES, pairs(target))
+
+
+def swap_x(values):
+    return send(values, lambda y, c, z, x: (y, c, z, 1 - x))
+
+
+def swap_core(values):
+    return send(values, lambda y, c, z, x: (y, 1 - c, z, x))
+
+
+def swap_y(values):
+    return send(values, lambda y, c, z, x: (1 - y, c, z, x))
+
+
+def pick(values, index):
+    return lax.dynamic_index_in_dim(values, index, 0, keepdims=False)
+
+
+def ordered(own, other, position, axis):
+    first = jnp.where(position == 0, own, other)
+    second = jnp.where(position == 0, other, own)
+    return jnp.stack([first, second], axis=axis)
+
+
+def line_gather(piece, z):
+    right = left = piece
+    rights, lefts = [], []
+    for turn in range(1, ZN):
+        right = send(right, lambda y, c, z, x: (y, c, z + 1, x) if turn - 1 <= z < ZN - 1 else None)
+        left = send(left, lambda y, c, z, x: (y, c, z - 1, x) if 0 < z <= ZN - turn else None)
+        rights.append(right)
+        lefts.append(left)
+    band = jnp.stack(rights[::-1] + [piece] + lefts)
+    return lax.dynamic_slice_in_dim(band, ZN - 1 - z, ZN, 0)
+
+
+def line_scatter(parts, z):
+    right = left = None
+    for turn in range(1, ZN):
+        up = pick(parts, jnp.clip(z + ZN - turn, 0, ZN - 1))
+        down = pick(parts, jnp.clip(z - ZN + turn, 0, ZN - 1))
+        if right is not None:
+            up, down = up + right, down + left
+        right = send(up, lambda y, c, z, x: (y, c, z + 1, x) if z <= turn - 1 and z < ZN - 1 else None)
+        left = send(down, lambda y, c, z, x: (y, c, z - 1, x) if z >= ZN - turn and z > 0 else None)
+    return pick(parts, z) + right + left
+
+
+def gather_zy(piece, y, z):
+    column = line_gather(piece, z)
+    return ordered(column, swap_y(column), y, 0)
+
+
+def scatter_zy(parts, y, z):
+    mine = pick(parts, y)
+    theirs = pick(parts, 1 - y)
+    return line_scatter(mine + swap_y(theirs), z)
+
+
+def team_swap(parts, c, x):
+    by_x = jnp.moveaxis(parts, 1, 0)
+    got = swap_x(pick(by_x, 1 - x))
+    both = ordered(pick(by_x, x), got, x, 1)
+    got = swap_core(pick(both, 1 - c))
+    return ordered(pick(both, c), got, c, 0)
+
+
+def team_gather(values, c, x):
+    mine = values.reshape(2, BLK, -1)
+    row = ordered(mine, swap_x(mine), x, 1)
+    return ordered(row, swap_core(row), c, 0).reshape(8 * BLK, -1)
+
+
+def team_scatter(values, c, x):
+    parts = values.reshape(2, 2, 2, BLK, -1)
+    got = swap_core(pick(parts, 1 - c).astype(jnp.bfloat16))
+    mine = jnp.moveaxis(pick(parts, c) + got.astype(jnp.float32), 1, 0)
+    got = swap_x(pick(mine, 1 - x).astype(jnp.bfloat16))
+    return (pick(mine, x) + got.astype(jnp.float32)).reshape(2 * BLK, -1)
+
+
+def to_teams(values, z, c):
+    half = z // 2
+    got = []
+    for k in range(2):
+        block = pick(values, (z + k) % 2)[0]
+        got.append(
+            send(block, lambda y, c, z, x: (y, z // 2, 2 * ((z + k) % 2) + c, x))
+        )
+    return jnp.concatenate(
+        [jnp.where(half == 0, got[0], got[1]), jnp.where(half == 0, got[1], got[0])]
+    )
+
+
+def from_teams(values, z, c):
+    half = z // 2
+    parts = values.reshape(2, BLK, -1)
+    back = []
+    for k in range(2):
+        block = pick(parts, (half + k) % 2)
+
+        def target(y, c, z, x, k=k):
+            m, core = z // 2, z % 2
+            return (y, core, 2 * c + (m + k) % 2, x)
+
+        back.append(send(block, target))
+    first = jnp.where(z % 2 == 0, back[0], back[1])
+    second = jnp.where(z % 2 == 0, back[1], back[0])
+    return jnp.stack([first, second])[:, None]
+
+
+def head_parts(columns):
+    found = []
+    for start, count in zip(STARTS, COUNTS):
+        part = columns[:, start * HEAD : (start + count) * HEAD]
+        found.append(jnp.pad(part, ((0, 0), (0, (SLOTS - count) * HEAD))))
+    return jnp.stack(found)
+
+
+def head_join(parts):
+    return jnp.concatenate(
+        [parts[r][:, : COUNTS[r] * HEAD] for r in range(4)], axis=1
+    )
+
+
+def fast_shards(inputs, grad_out, w_qkv, w_proj, w_fc, w_out, smalls):
+    dp, ctx = lax.axis_index("dp"), lax.axis_index("ctx")
+    y, c, z, x = dp // CN, dp % CN, ctx // XN, ctx % XN
+    rank = c * XN + x
+    low = jnp.bfloat16
+    small = lax.all_gather(smalls, AXES, axis=0, tiled=True).astype(jnp.float32)
+    gain1, shift1, bias_q, bias_v, bias_proj, gain2, shift2 = [segment(small, i) for i in range(7)]
+    bias_fc = small[7 * D : 7 * D + FF].reshape(YN, CN, ZN, XN, 200)
+    bias_fc = lax.dynamic_index_in_dim(bias_fc, c, 1, keepdims=False)
+    bias_fc = lax.dynamic_index_in_dim(bias_fc, x, 2, keepdims=False).reshape(-1)
+    bias_out = small[7 * D + FF :]
+    bias_qkv = jnp.stack(
+        [head_parts(bias_q[None]), jnp.zeros((4, 1, HW)), head_parts(bias_v[None])], axis=1
+    )
+    bias_qkv = pick(bias_qkv, rank).reshape(3 * HW)
+
+    tokens = to_teams(inputs, z, c).astype(jnp.float32)
+    cotangent = to_teams(grad_out, z, c)
+
+    rows = w_qkv.reshape(50, 3, D)
+    parts = jnp.stack([head_parts(rows[:, i]) for i in range(3)], axis=2)
+    parts = parts.reshape(CN, XN, 50, 3 * HW)
+    piece = team_swap(parts, c, x)
+    gathered = gather_zy(piece, y, z)
+    mat_qkv = gathered.transpose(0, 2, 1, 3, 4, 5).reshape(D, 3 * HW)
+
+    piece = w_proj.reshape(50, D)
+    gathered = gather_zy(piece, y, z)
+    both = ordered(gathered, swap_x(gathered), x, 2)
+    full = ordered(both, swap_core(both), c, 1)
+    mat_proj = full.reshape(D, D)
+
+    parts = w_fc.reshape(50, YN, CN, ZN, XN, 200).transpose(2, 4, 0, 1, 3, 5)
+    parts = parts.reshape(CN, XN, 50, D)
+    piece = team_swap(parts, c, x)
+    gathered = gather_zy(piece, y, z)
+    mat_fc = gathered.transpose(0, 2, 1, 3, 4, 5).reshape(D, D)
+
+    mat_out = gather_zy(w_out.reshape(200, D), y, z).reshape(D, D)
+
+    hidden_one, ln1_pull = jax.vjp(layer_norm, tokens, gain1, shift1)
+    hidden_one = team_gather(hidden_one.astype(low), c, x)
+    mixed = (jnp.dot(hidden_one, mat_qkv, preferred_element_type=jnp.float32) + bias_qkv).astype(low)
+    queries, keys, values = [
+        mixed[:, i * HW : (i + 1) * HW].reshape(1, 8 * BLK, SLOTS, HEAD) for i in range(3)
+    ]
+    scores = masked_scores(queries, keys, 0, 0)
+    peak = jnp.max(scores, axis=-1, keepdims=True)
+    log_total = peak + jnp.log(jnp.sum(jnp.exp(scores - peak), axis=-1, keepdims=True))
+    attn = jnp.exp(scores - log_total)
+    attn_low = attn.astype(low)
+    context = jnp.einsum("shqk,skhe->sqhe", attn_low, values, preferred_element_type=jnp.float32)
+    context = context.astype(low).reshape(2, 2, 2, BLK, HW)
+    context = team_swap(jnp.moveaxis(context, 2, 1), c, x).reshape(4, 2 * BLK, HW)
+    context = head_join(context)
+    resid = tokens + jnp.dot(context, mat_proj, preferred_element_type=jnp.float32) + bias_proj
+    hidden_two, ln2_pull = jax.vjp(layer_norm, resid, gain2, shift2)
+    hidden_two = team_gather(hidden_two.astype(low), c, x)
+    pre_act = jnp.dot(hidden_two, mat_fc, preferred_element_type=jnp.float32) + bias_fc
+    activ, gelu_pull = jax.vjp(gelu_tanh, pre_act)
+    activ = activ.astype(low)
+    result = team_scatter(jnp.dot(activ, mat_out, preferred_element_type=jnp.float32), c, x)
+    result = (resid + result + bias_out).astype(low)
+    outputs = from_teams(result, z, c)
+
+    grad_full = cotangent.astype(jnp.float32)
+    grad_all = team_gather(cotangent, c, x)
+    (grad_pre,) = gelu_pull(back_product(grad_all, mat_out))
+    grad_pre = grad_pre.astype(low)
+    grad_hidden_two = team_scatter(back_product(grad_pre, mat_fc), c, x)
+    grad_ln_two, grad_gain_two, grad_shift_two = ln2_pull(grad_hidden_two)
+    grad_resid = grad_full + grad_ln_two
+    grad_branch = grad_resid.astype(low)
+    grad_context = back_product(grad_branch, mat_proj).astype(low)
+    grad_context = team_swap(head_parts(grad_context).reshape(CN, XN, 2, BLK, HW), c, x)
+    grad_context = jnp.moveaxis(grad_context, 1, 2).reshape(1, 8 * BLK, SLOTS, HEAD)
+    grad_attn = jnp.einsum("sqhe,skhe->shqk", grad_context, values, preferred_element_type=jnp.float32)
+    delta = jnp.sum(attn * grad_attn, axis=-1, keepdims=True)
+    grad_scores = (attn * (grad_attn - delta)).astype(low)
+    grad_q = jnp.einsum("shqk,skhe->sqhe", grad_scores, keys, preferred_element_type=jnp.float32) * 0.125
+    grad_k = jnp.einsum("shqk,sqhe->skhe", grad_scores, queries, preferred_element_type=jnp.float32) * 0.125
+    grad_v = jnp.einsum("shqk,sqhe->skhe", attn_low, grad_context, preferred_element_type=jnp.float32)
+    grad_mixed = jnp.concatenate(
+        [g.reshape(8 * BLK, HW) for g in (grad_q, grad_k, grad_v)], axis=1
+    ).astype(low)
+    grad_hidden_one = team_scatter(back_product(grad_mixed, mat_qkv), c, x)
+    grad_ln_one, grad_gain_one, grad_shift_one = ln1_pull(grad_hidden_one)
+    grad_in = from_teams((grad_resid + grad_ln_one).astype(low), z, c).astype(jnp.float32)
+
+    total = outer_sum(activ, grad_all).astype(low)
+    grad_out_w = scatter_zy(total.reshape(YN, ZN, 200, D), y, z)
+    grad_out_w = grad_out_w.astype(jnp.float32).reshape(-1)
+
+    total = outer_sum(hidden_two, grad_pre).astype(low)
+    total = total.reshape(YN, CN, ZN, XN, 50, D).transpose(0, 2, 1, 3, 4, 5)
+    part = team_swap(scatter_zy(total, y, z), c, x)
+    grad_fc = part.reshape(CN, XN, 50, YN, ZN, 200).transpose(2, 3, 0, 4, 1, 5)
+    grad_fc = grad_fc.astype(jnp.float32).reshape(-1)
+
+    total = outer_sum(context, grad_branch).astype(low)
+    total = total.reshape(YN, CN, ZN, XN, 50, D).transpose(1, 3, 0, 2, 4, 5)
+    total = pick(total, c) + swap_core(pick(total, 1 - c))
+    total = pick(total, x) + swap_x(pick(total, 1 - x))
+    grad_proj = scatter_zy(total, y, z).astype(jnp.float32).reshape(-1)
+
+    total = outer_sum(hidden_one, grad_mixed).astype(low)
+    total = total.reshape(YN, CN, ZN, XN, 50, 3 * HW).transpose(0, 2, 1, 3, 4, 5)
+    part = team_swap(scatter_zy(total, y, z), c, x).reshape(4, 50, 3, HW)
+    grad_qkv = jnp.stack([head_join(part[:, :, i]) for i in range(3)], axis=1)
+    grad_qkv = grad_qkv.astype(jnp.float32).reshape(-1)
+
+    terms = jnp.sum(grad_mixed.astype(jnp.float32), axis=0).reshape(3, HW)
+    here = (jnp.arange(4) == rank).astype(jnp.float32)[:, None, None]
+    grad_bq = head_join(here * terms[0][None, None])[0]
+    grad_bv = head_join(here * terms[2][None, None])[0]
+    fc_terms = jnp.sum(grad_pre.astype(jnp.float32), axis=0).reshape(YN, 1, ZN, 1, 200)
+    spot = (jnp.arange(CN) == c)[None, :, None, None, None] & (jnp.arange(XN) == x)[None, None, None, :, None]
+    grad_fc_bias = jnp.where(spot, fc_terms, 0.0).reshape(-1)
+    front = jnp.concatenate([grad_gain_one, grad_shift_one, grad_bq, grad_bv])
+    tail = jnp.concatenate(
+        [
+            jnp.sum(grad_branch.astype(jnp.float32), axis=0),
+            grad_gain_two,
+            grad_shift_two,
+            grad_fc_bias,
+            jnp.sum(grad_full, axis=0),
+        ]
+    )
+    grad_front = lax.psum_scatter(front, AXES, scatter_dimension=0, tiled=True)
+    grad_tail = lax.psum_scatter(tail, AXES, scatter_dimension=0, tiled=True)
+    return (outputs, grad_in, grad_qkv, grad_proj, grad_fc, grad_out_w, grad_front, grad_tail)
+
+
 def solution(mesh):
     placed = (
         P(None, "dp", "ctx", None),
@@ -322,8 +613,9 @@
         P(("dp", "ctx")),
         P(("dp", "ctx")),
     )
+    fast = dict(mesh.shape) == {"dp": DP, "ctx": CTX}
     return jax.shard_map(
-        shards,
+        fast_shards if fast else shards,
         mesh=mesh,
         in_specs=placed,
         out_specs=(

time: 3790 us -> 1270 us (0.34)
  waiting for transfers between devices: 2330 us -> 412 us
  other arithmetic: 616 us -> 179 us
  matrix products: 345 us -> 175 us
  starting transfers between devices: 1.36 us -> 171 us
  blocking collectives: 168 us -> 44.7 us
  local copies, waits for them, and re-layouts: 304 us -> 261 us
    unnamed x16 -> x2, waiting for transfers between devices: 1770 us -> 118 us
    all_gather x4 -> x0, other arithmetic: 595 us -> none  [the longest x1 316 us: fetch(): lax.all_gather(w_qkv, ('dp', 'ctx'), axis=0, tiled=True)]
    all_gather x12 -> x0, waiting for transfers between devices: 565 us -> none  [the longest x1 220 us: fetch(): lax.all_gather(w_fc, ('dp', 'ctx'), axis=0, tiled=True)]
    ppermute x0 -> x92, waiting for transfers between devices: none -> 294 us  [send(): return lax.ppermute(values, AXES, pairs(target))]
    ppermute x0 -> x92, starting transfers between devices: none -> 171 us  [send(): return lax.ppermute(values, AXES, pairs(target))]
    all_gather x4 -> x0, blocking collectives: 124 us -> none  [the longest x2 62.5 us: shards(): lax.all_gather(jnp.transpose(log_total[..., 0], (0, 2, 1)), 'ctx', axis=1...]
    dynamic_slice x4 -> x21, local copies, waits for them, and re-layouts: 138 us -> 26.4 us  [the longest x15 17.9 us: pick(): return lax.dynamic_index_in_dim(values, index, 0, keepdims=False)]
    dot_general x18 -> x9, matrix products: 185 us -> 99.6 us  [the longest x1 21.5 us: fast_shards(): jnp.einsum('sqhe,skhe->shqk', grad_context, values, preferred_element_typ...]
  transfers between devices with their start and end apart: 14 -> 93, of which waited for: 8 -> 27; matrix products, arithmetic and copies ran while one was open for 32% -> 42% of each run, Pallas kernels for 0% -> 0%
where the time goes in v1:
time: 1270 us; the launch traced here: 1260 us
  waiting for transfers between devices  412 us (32%)
  local copies, waits for them, and re-layouts  261 us (21%)
  other arithmetic  179 us (14%)
  matrix products  175 us (14%)
  starting transfers between devices  171 us (13%)
  blocking collectives  44.7 us (4%)
  between operations  17.7 us (1%)
    ppermute x92, waiting for transfers between devices, send(): return lax.ppermute(values, AXES, pairs(target))  294 us
    ppermute x92, starting transfers between devices, send(): return lax.ppermute(values, AXES, pairs(target))  171 us
    unnamed x2, waiting for transfers between devices  118 us
    another operation x40, other arithmetic, ordered(): return jnp.stack([first, second], axis=axis)  57 us
    unnamed x1, blocking collectives  44.7 us
    dot_general x4, matrix products, back_product(): lax.dot_general(grad, weight, (((1,), (1,)), ((), ())), preferred_element...  34.3 us
    unnamed x247, local copies, waits for them, and re-layouts  31.2 us
    dot_general x4, matrix products, outer_sum(): lax.dot_general(left, right, (((0,), (0,)), ((), ())), preferred_element_...  29 us
  transfers between devices with their start and end apart: 93, of which 27 were waited for; matrix products, arithmetic and copies ran while one was open for 42% of the time, Pallas kernels for 0%

profile of v1, /device:TPU:0, one launch (start us, length us, event | category | flops | bytes accessed | tf_op | source)
XLA Modules:
  0.0 1259.6 jit_solution(1587189688611923170)
XLA Ops:
  10.3 6.3 collective-permute-start.15
  37.9 44.7 %all-reduce.18 = bf16[19200]{0:T(1024)(128)(2,1)S(1)} all-reduce(bf16[19200]{0:T(1024)(128)(2,1)S(1)} %dynamic-update-slice), channel_id=1, replica_groups=mesh['dp'=4,'ctx'=8] {'dp','ctx'}, use_global_device_ids=true, to_apply=%add.18 | all-reduce | flops 19200 | bytes 76800
  103.9 12.1 collective-permute-start.47
  123.5 6.7 collective-permute-start.5
  131.1 11.9 collective-permute-done.19
  146.3 5.7 collective-permute-done.20
  161.1 11.4 collective-permute-done.21
  177.6 12.3 collective-permute-done.48
  200.9 8.9 collective-permute-done.39
  215.3 19.1 %collective-permute-done.40 = bf16[200,1600]{1,0:T(8,128)(2,1)S(1)} collective-permute-done((bf16[200,1600]{1,0:T(8,128)(2,1)S(1)}, bf16[200,1600]{1,0:T(8,128)(2,1)S(1)}, u32[]{:S(2)}, u32[]{:S(2)}) %collective-permute-start.40) | collective-permute-done | bytes 640032 | tf_op jit(solution)/shard_map/ppermute | solution.py:347
  244.2 11.5 collective-permute-done.11
  259.8 9.8 collective-permute-done.32
  281.9 10.8 collective-permute-done.33
  299.6 5.4 copy.444
  308.9 5.8 copy.481
  314.8 64.0 %collective-permute-done.12 = bf16[4,2,2,50,1344]{4,2,3,1,0:T(2,128)(2,1)} collective-permute-done((bf16[4,2,2,50,1344]{4,2,3,1,0:T(2,128)(2,1)}, bf16[4,2,2,50,1344]{4,2,3,1,0:T(2,128)(2,1)}, u32[]{:S(2)}, u32[]{:S(2)}) %collective-permute-start.12) | collective-permute-done | bytes 2150432 | tf_op jit(solution)/shard_map/ppermute | solution.py:347
  378.8 8.1 fusion.24
  386.9 11.0 maximum_bitcast_fusion.1
  403.1 7.7 reshape.658
  410.8 8.4 add_convert_fusion
  419.5 12.0 fusion
  431.5 13.4 %exponential_reduce_fusion = f32[7,1024]{1,0:T(8,128)S(1)} fusion(f32[7,1024,1024]{1,2,0:T(8,128)} %get-tuple-element.253, f32[7,1024]{1,0:T(8,128)S(1)} %get-tuple-element.252, pred[1024,1024]{0,1:T(8,128)(4,1)S(1)} %iota_compare_fusion), kind=kLoop, calls=%fused_computation.3 | loop fusion | flops 29352960 | bytes 30466048 | tf_op jit(solution)/shard_map/reduce_sum | solution.py:521
  445.0 13.2 %fusion.41 = bf16[1,1024,7,64]{1,3,2,0:T(8,128)(2,1)S(1)} fusion(bf16[1024,7,64]{0,2,1:T(8,128)(2,1)S(1)} %bitcast.749, f32[7,1024,1024]{1,2,0:T(8,128)} %get-tuple-element.253, f32[7,1024]{1,0:T(8,128)S(1)} %log_add_fusion, pred[1024,1024]{0,1:T(8,128)(4,1)S(1)} %iota_compare_fusion), kind=kOutput, calls=%fused_computation.133 | convolution fusion | flops 969342976 | bytes 32272384 | tf_op jit(solution)/shard_map/shqk,skhe->sqhe/dot_general | solution.py:524
  477.7 8.7 reshape.665
  495.8 6.2 fusion.22
  502.0 13.0 %collective-permute-done.24 = bf16[2,128,1600]{1,2,0:T(8,128)(2,1)S(1)} collective-permute-done((bf16[2,128,1600]{1,2,0:T(8,128)(2,1)S(1)}, bf16[2,128,1600]{1,2,0:T(8,128)(2,1)S(1)}, u32[]{:S(2)}, u32[]{:S(2)}) %collective-permute-start.24) | collective-permute-done | bytes 819232 | tf_op jit(solution)/shard_map/ppermute | solution.py:347
  517.3 8.1 maximum_bitcast_fusion
  528.8 8.3 reshape.712
  537.2 8.4 reshape.670
  549.1 5.5 copy.466
  554.6 9.8 fusion.106
  564.5 13.6 %convert_reduce_fusion = (f32[1600]{0:T(1024)S(1)}, bf16[1024,1600]{0,1:T(8,128)(2,1)S(1)}, bf16[1024,1600]{0,1:T(8,128)(2,1)}) fusion(f32[1024,1600]{0,1:T(8,128)S(1)} %fusion.106, f32[1600]{0:T(1024)S(1)} %copy-done.80, bf16[1024,1600]{1,0:T(8,128)(2,1)S(1)} %bitcast.760, bf16[1600,1600]{1,0:T(8,128)(2,1)} %bitcast.747), kind=kOutput, calls=%fused_computation.20 | convolution fusion | flops 5283838464 | bytes 21516800 | tf_op jit(solution)/shard_map/dot_general | solution.py:68
  579.7 8.5 convolution_convert_fusion.2
  588.2 8.5 dot_general.68
  596.7 9.0 fusion.9
  610.3 8.9 dot_general.65
  619.2 10.1 fusion.14
  633.6 7.8 convolution_convert_fusion.1
  643.7 8.0 reshape.691
  667.6 13.2 %collective-permute-done.51 = bf16[2,128,1600]{1,2,0:T(8,128)(2,1)S(1)} collective-permute-done((bf16[2,128,1600]{1,2,0:T(8,128)(2,1)S(1)}, bf16[2,128,1600]{1,2,0:T(8,128)(2,1)S(1)}, u32[]{:S(2)}, u32[]{:S(2)}) %collective-permute-start.51) | collective-permute-done | bytes 819232 | tf_op jit(solution)/shard_map/ppermute | solution.py:347
  683.1 14.0 %collective-permute-done.43 = bf16[2,128,1600]{1,2,0:T(8,128)(2,1)S(1)} collective-permute-done((bf16[2,128,1600]{1,2,0:T(8,128)(2,1)S(1)}, bf16[2,128,1600]{1,2,0:T(8,128)(2,1)S(1)}, u32[]{:S(2)}, u32[]{:S(2)}) %collective-permute-start.43) | collective-permute-done | bytes 819232 | tf_op jit(solution)/shard_map/ppermute | solution.py:347
  704.9 5.6 collective-permute-start.45
  727.6 8.3 reshape.688
  743.9 28.5 %collective-permute-done.76 = bf16[4,2,2,50,1600]{4,0,3,2,1:T(4,128)(2,1)} collective-permute-done((bf16[4,2,2,50,1600]{4,0,3,2,1:T(4,128)(2,1)}, bf16[4,2,2,50,1600]{4,0,3,2,1:T(4,128)(2,1)}, u32[]{:S(2)}, u32[]{:S(2)}) %collective-permute-start.76) | collective-permute-done | bytes 2560032 | tf_op jit(solution)/shard_map/ppermute | solution.py:347
  772.4 8.3 collective-permute-start.86
  796.9 11.5 collective-permute-done.77
  822.4 13.7 %convolution_convert_fusion.5 = bf16[7,64,1024]{2,1,0:T(8,128)(2,1)S(1)} fusion(bf16[1024,7,64]{0,2,1:T(8,128)(2,1)S(1)} %reshape.680, f32[7,1024,1024]{1,2,0:T(8,128)} %get-tuple-element.253, f32[7,1024]{1,0:T(8,128)S(1)} %copy-done.50, pred[1024,1024]{0,1:T(8,128)(4,1)S(1)} %copy-done.1), kind=kOutput, calls=%fused_computation.131 | convolution fusion | flops 969342976 | bytes 32272384 | tf_op jit(solution)/shard_map/shqk,sqhe->skhe/dot_general | solution.py:554
  836.1 21.5 %multiply_reduce_fusion = (f32[7,1024]{1,0:T(8,128)S(1)}, f32[7,1024,1024]{1,2,0:T(8,128)}) fusion(f32[7,1024,1024]{1,2,0:T(8,128)} %get-tuple-element.253, f32[7,1024]{1,0:T(8,128)S(1)} %copy-done.50, pred[1024,1024]{0,1:T(8,128)(4,1)S(1)} %copy-done.1, bf16[1024,7,64]{0,2,1:T(8,128)(2,1)S(1)} %reshape.680, bf16[1024,7,64]{0,2,1:T(8,128)(2,1)S(1)} %bitcast.750), kind=kOutput, calls=%fused_computation.1 | convolution fusion | flops 976217088 | bytes 61661184 | tf_op jit(solution)/shard_map/sqhe,skhe->shqk/dot_general | solution.py:549
  857.5 26.0 %multiply_convert_fusion = bf16[7,1024,1024]{1,2,0:T(8,128)(2,1)} fusion(f32[7,1024,1024]{1,2,0:T(8,128)} %get-tuple-element.257, f32[7,1024,1024]{1,2,0:T(8,128)} %get-tuple-element.253, f32[7,1024]{1,0:T(8,128)S(1)} %get-tuple-element.256, f32[7,1024]{1,0:T(8,128)S(1)} %copy-done.50, pred[1024,1024]{0,1:T(8,128)(4,1)S(1)} %copy-done.1), kind=kLoop, calls=%fused_computation | loop fusion | flops 44040192 | bytes 74506240 | tf_op jit(solution)/shard_map/convert_element_type | solution.py:551
  883.5 9.8 multiply_convert_fusion.2
  893.4 8.0 multiply_convert_fusion.3
  901.8 8.6 convolution_convert_fusion
  917.6 7.3 fusion.11
  929.1 7.4 copy.497
  936.4 7.3 reshape.686
  978.7 6.1 collective-permute-done.83
  999.7 11.3 collective-permute-done.91
  1031.1 5.4 collective-permute-start.59
  1054.8 118.1 %all-reduce.24.cloned.1.call-done = (f32[6400]{0:T(1024)}, f32[12800]{0:T(1024)}) async-done(((f32[6400]{0:T(1024)}, f32[12800]{0:T(1024)}), (f32[6400]{0:T(1024)}, f32[12800]{0:T(1024)})) %all-reduce.24.cloned.1.call-update) | async-done | bytes 76816
  1177.4 6.2 collective-permute-start.60
  1197.5 5.3 collective-permute-done.69
  1205.6 5.3 collective-permute-start.70
  1219.1 6.7 collective-permute-done.64
  1237.1 7.4 collective-permute-done.75
  (691 shorter events, 408.8 us)
Async XLA Ops:
  7.2 1165.7 %all-reduce.24.cloned.1.call-start = ((), (), s32[]{:S(2)}) async-start(), calls=%async_computation | async-start | bytes 163840
  9.0 109.4 %collective-permute-start.18 = (bf16[50,1600]{1,0:T(8,128)(2,1)}, bf16[50,1600]{1,0:T(8,128)(2,1)}, u32[]{:S(2)}, u32[]{:S(2)}) collective-permute-start(bf16[50,1600]{1,0:T(8,128)(2,1)} %reshape.664), channel_id=1, source_target_pairs={{2,0},{3,1},{4,2},{5,3},{6,4},{7,5},{10,8},{11,9},{12,10},{13,11},... | collective-permute-start | bytes 480008 | tf_op jit(solution)/shard_map/ppermute | solution.py:347
  10.3 93.0 %collective-permute-start.15 = (bf16[50,1600]{1,0:T(8,128)(2,1)}, bf16[50,1600]{1,0:T(8,128)(2,1)}, u32[]{:S(2)}, u32[]{:S(2)}) collective-permute-start(bf16[50,1600]{1,0:T(8,128)(2,1)} %reshape.664), channel_id=1, source_target_pairs={{0,2},{1,3},{2,4},{3,5},{4,6},{5,7},{8,10},{9,11},{10,12},{11,13},... | collective-permute-start | bytes 480008 | tf_op jit(solution)/shard_map/ppermute | solution.py:347
  24.0 68.0 %collective-permute-start.4 = (bf16[2,50,1344]{2,0,1:T(2,128)(2,1)}, bf16[2,50,1344]{2,0,1:T(2,128)(2,1)}, u32[]{:S(2)}, u32[]{:S(2)}) collective-permute-start(bf16[2,50,1344]{2,0,1:T(2,128)(2,1)} %bitcast.706), channel_id=1, source_target_pairs={{0,1},{1,0},{2,3},{3,2},{4,5},{5,4},{6,7},{7,6},{8,9},{9,8},{10,11... | collective-permute-start | bytes 806408 | tf_op jit(solution)/shard_map/ppermute | solution.py:347
  27.3 146.8 %collective-permute-start.38 = (bf16[200,1600]{1,0:T(8,128)(2,1)}, bf16[200,1600]{1,0:T(8,128)(2,1)}, u32[]{:S(2)}, u32[]{:S(2)}) collective-permute-start(bf16[200,1600]{1,0:T(8,128)(2,1)} %reshape.672), channel_id=1, source_target_pairs={{2,0},{3,1},{4,2},{5,3},{6,4},{7,5},{10,8},{11,9},{12,10},{13,11},... | collective-permute-start | bytes 1920008 | tf_op jit(solution)/shard_map/ppermute | solution.py:347
  37.2 59.7 %collective-permute-start.26 = (bf16[2,50,1600]{2,0,1:T(2,128)(2,1)}, bf16[2,50,1600]{2,0,1:T(2,128)(2,1)}, u32[]{:S(2)}, u32[]{:S(2)}) collective-permute-start(bf16[2,50,1600]{2,0,1:T(2,128)(2,1)} %bitcast.705), channel_id=1, source_target_pairs={{0,1},{1,0},{2,3},{3,2},{4,5},{5,4},{6,7},{7,6},{8,9},{9,8},{10,11... | collective-permute-start | bytes 960008 | tf_op jit(solution)/shard_map/ppermute | solution.py:347
  97.0 19.1 %collective-permute-start.1 = (bf16[128,1600]{0,1:T(8,128)(2,1)S(1)}, bf16[128,1600]{0,1:T(8,128)(2,1)S(1)}, u32[]{:S(2)}, u32[]{:S(2)}) collective-permute-start(bf16[128,1600]{0,1:T(8,128)(2,1)S(1)} %copy-done.57), channel_id=1, source_target_pairs={{0,4},{1,5},{2,0},{3,1},{4,12},{5,13},{6,8},{7,9},{8,6},{9,7},{10,... | collective-permute-start | bytes 1228808 | tf_op jit(solution)/shard_map/ppermute | solution.py:347
  103.2 20.2 %collective-permute-start.46 = (bf16[128,1600]{0,1:T(8,128)(2,1)S(1)}, bf16[128,1600]{0,1:T(8,128)(2,1)S(1)}, u32[]{:S(2)}, u32[]{:S(2)}) collective-permute-start(bf16[128,1600]{0,1:T(8,128)(2,1)S(1)} %get-tuple-element.177), channel_id=1, source_target_pairs={{0,0},{1,1},{2,4},{3,5},{4,8},{5,9},{6,12},{7,13},{8,2},{9,3},{10,... | collective-permute-start | bytes 1228808 | tf_op jit(solution)/shard_map/ppermute | solution.py:347
  103.9 26.3 %collective-permute-start.47 = (bf16[128,1600]{0,1:T(8,128)(2,1)S(1)}, bf16[128,1600]{0,1:T(8,128)(2,1)S(1)}, u32[]{:S(2)}, u32[]{:S(2)}) collective-permute-start(bf16[128,1600]{0,1:T(8,128)(2,1)S(1)} %get-tuple-element.178), channel_id=1, source_target_pairs={{0,4},{1,5},{2,0},{3,1},{4,12},{5,13},{6,8},{7,9},{8,6},{9,7},{10,... | collective-permute-start | bytes 1228808 | tf_op jit(solution)/shard_map/ppermute | solution.py:347
  118.4 41.3 %collective-permute-start.35 = (bf16[200,1600]{1,0:T(8,128)(2,1)}, bf16[200,1600]{1,0:T(8,128)(2,1)S(1)}, u32[]{:S(2)}, u32[]{:S(2)}) collective-permute-start(bf16[200,1600]{1,0:T(8,128)(2,1)} %reshape.672), channel_id=1, source_target_pairs={{0,2},{1,3},{2,4},{3,5},{4,6},{5,7},{8,10},{9,11},{10,12},{11,13},... | collective-permute-start | bytes 1920008 | tf_op jit(solution)/shard_map/ppermute | solution.py:347
  122.2 20.8 %collective-permute-start.19 = (bf16[50,1600]{1,0:T(8,128)(2,1)}, bf16[50,1600]{1,0:T(8,128)(2,1)S(1)}, u32[]{:S(2)}, u32[]{:S(2)}) collective-permute-start(bf16[50,1600]{1,0:T(8,128)(2,1)} %collective-permute-done.18), channel_id=1, source_target_pairs={{2,0},{3,1},{4,2},{5,3},{10,8},{11,9},{12,10},{13,11},{18,16},{19,... | collective-permute-start | bytes 480008 | tf_op jit(solution)/shard_map/ppermute | solution.py:347
  123.5 31.1 %collective-permute-start.5 = (bf16[2,50,1344]{2,0,1:T(2,128)(2,1)S(1)}, bf16[2,50,1344]{2,0,1:T(2,128)(2,1)S(1)}, u32[]{:S(2)}, u32[]{:S(2)}) collective-permute-start(bf16[2,50,1344]{2,0,1:T(2,128)(2,1)S(1)} %bitcast.776), channel_id=1, source_target_pairs={{0,8},{1,9},{2,10},{3,11},{4,12},{5,13},{6,14},{7,15},{8,0},{9,1},... | collective-permute-start | bytes 806408 | tf_op jit(solution)/shard_map/ppermute | solution.py:347
  152.0 24.3 %collective-permute-start.2 = (bf16[2,128,1600]{1,2,0:T(8,128)(2,1)S(1)}, bf16[2,128,1600]{1,2,0:T(8,128)(2,1)S(1)}, u32[]{:S(2)}, u32[]{:S(2)}) collective-permute-start(bf16[2,128,1600]{1,2,0:T(8,128)(2,1)S(1)} %add_convert_fusion.2), channel_id=1, source_target_pairs={{0,1},{1,0},{2,3},{3,2},{4,5},{5,4},{6,7},{7,6},{8,9},{9,8},{10,11... | collective-permute-start | bytes 2457608 | tf_op jit(solution)/shard_map/ppermute | solution.py:347
  154.6 35.3 %collective-permute-start.48 = (bf16[2,128,1600]{1,2,0:T(8,128)(2,1)S(1)}, bf16[2,128,1600]{1,2,0:T(8,128)(2,1)S(1)}, u32[]{:S(2)}, u32[]{:S(2)}) collective-permute-start(bf16[2,128,1600]{1,2,0:T(8,128)(2,1)S(1)} %copy_bitcast_fusion.1), channel_id=1, source_target_pairs={{0,1},{1,0},{2,3},{3,2},{4,5},{5,4},{6,7},{7,6},{8,9},{9,8},{10,11... | collective-permute-start | bytes 2457608 | tf_op jit(solution)/shard_map/ppermute | solution.py:347
  159.8 35.1 %collective-permute-start.9 = (bf16[2,2,50,1344]{3,1,2,0:T(2,128)(2,1)S(1)}, bf16[2,2,50,1344]{3,1,2,0:T(2,128)(2,1)S(1)}, u32[]{:S(2)}, u32[]{:S(2)}) collective-permute-start(bf16[2,2,50,1344]{3,1,2,0:T(2,128)(2,1)S(1)} %pad_maximum_fusion.19), channel_id=1, source_target_pairs={{2,0},{3,1},{4,2},{5,3},{6,4},{7,5},{10,8},{11,9},{12,10},{13,11},... | collective-permute-start | bytes 1612808 | tf_op jit(solution)/shard_map/ppermute | solution.py:347
  174.1 25.6 %collective-permute-start.6 = (bf16[2,2,50,1344]{3,1,2,0:T(2,128)(2,1)S(1)}, bf16[2,2,50,1344]{3,1,2,0:T(2,128)(2,1)S(1)}, u32[]{:S(2)}, u32[]{:S(2)}) collective-permute-start(bf16[2,2,50,1344]{3,1,2,0:T(2,128)(2,1)S(1)} %pad_maximum_fusion.19), channel_id=1, source_target_pairs={{0,2},{1,3},{2,4},{3,5},{4,6},{5,7},{8,10},{9,11},{10,12},{11,13},... | collective-permute-start | bytes 1612808 | tf_op jit(solution)/shard_map/ppermute | solution.py:347
  176.3 66.1 %collective-permute-start.31 = (bf16[2,2,50,1600]{3,1,2,0:T(2,128)(2,1)S(1)}, bf16[2,2,50,1600]{3,1,2,0:T(2,128)(2,1)S(1)}, u32[]{:S(2)}, u32[]{:S(2)}) collective-permute-start(bf16[2,2,50,1600]{3,1,2,0:T(2,128)(2,1)S(1)} %pad_maximum_fusion.18), channel_id=1, source_target_pairs={{2,0},{3,1},{4,2},{5,3},{6,4},{7,5},{10,8},{11,9},{12,10},{13,11},... | collective-permute-start | bytes 1920008 | tf_op jit(solution)/shard_map/ppermute | solution.py:347
  189.9 20.0 %collective-permute-start.39 = (bf16[200,1600]{1,0:T(8,128)(2,1)}, bf16[200,1600]{1,0:T(8,128)(2,1)S(1)}, u32[]{:S(2)}, u32[]{:S(2)}) collective-permute-start(bf16[200,1600]{1,0:T(8,128)(2,1)} %collective-permute-done.38), channel_id=1, source_target_pairs={{2,0},{3,1},{4,2},{5,3},{10,8},{11,9},{12,10},{13,11},{18,16},{19,... | collective-permute-start | bytes 1920008 | tf_op jit(solution)/shard_map/ppermute | solution.py:347
  191.2 19.4 %collective-permute-start.37 = (bf16[200,1600]{1,0:T(8,128)(2,1)S(1)}, bf16[200,1600]{1,0:T(8,128)(2,1)S(1)}, u32[]{:S(2)}, u32[]{:S(2)}) collective-permute-start(bf16[200,1600]{1,0:T(8,128)(2,1)S(1)} %collective-permute-done.36), channel_id=1, source_target_pairs={{4,6},{5,7},{12,14},{13,15},{20,22},{21,23},{28,30},{29,31}} | collective-permute-start | bytes 1920008 | tf_op jit(solution)/shard_map/ppermute | solution.py:347
  194.9 48.0 %collective-permute-start.28 = (bf16[2,2,50,1600]{3,1,2,0:T(2,128)(2,1)S(1)}, bf16[2,2,50,1600]{3,1,2,0:T(2,128)(2,1)S(1)}, u32[]{:S(2)}, u32[]{:S(2)}) collective-permute-start(bf16[2,2,50,1600]{3,1,2,0:T(2,128)(2,1)S(1)} %pad_maximum_fusion.18), channel_id=1, source_target_pairs={{0,2},{1,3},{2,4},{3,5},{4,6},{5,7},{8,10},{9,11},{10,12},{11,13},... | collective-permute-start | bytes 1920008 | tf_op jit(solution)/shard_map/ppermute | solution.py:347
  199.6 38.6 %collective-permute-start.10 = (bf16[2,2,50,1344]{3,1,2,0:T(2,128)(2,1)S(1)}, bf16[2,2,50,1344]{3,1,2,0:T(2,128)(2,1)S(1)}, u32[]{:S(2)}, u32[]{:S(2)}) collective-permute-start(bf16[2,2,50,1344]{3,1,2,0:T(2,128)(2,1)S(1)} %collective-permute-done.9), channel_id=1, source_target_pairs={{2,0},{3,1},{4,2},{5,3},{10,8},{11,9},{12,10},{13,11},{18,16},{19,... | collective-permute-start | bytes 1612808 | tf_op jit(solution)/shard_map/ppermute | solution.py:347
  210.6 23.8 %collective-permute-start.40 = (bf16[200,1600]{1,0:T(8,128)(2,1)S(1)}, bf16[200,1600]{1,0:T(8,128)(2,1)S(1)}, u32[]{:S(2)}, u32[]{:S(2)}) collective-permute-start(bf16[200,1600]{1,0:T(8,128)(2,1)S(1)} %collective-permute-done.39), channel_id=1, source_target_pairs={{2,0},{3,1},{10,8},{11,9},{18,16},{19,17},{26,24},{27,25}} | collective-permute-start | bytes 1920008 | tf_op jit(solution)/shard_map/ppermute | solution.py:347
  213.4 58.9 %collective-permute-start.22 = (bf16[2,4,50,1600]{3,1,2,0:T(4,128)(2,1)S(1)}, bf16[2,4,50,1600]{3,1,2,0:T(4,128)(2,1)S(1)}, u32[]{:S(2)}, u32[]{:S(2)}) collective-permute-start(bf16[2,4,50,1600]{3,1,2,0:T(4,128)(2,1)S(1)} %copy.456), channel_id=1, source_target_pairs={{0,1},{1,0},{2,3},{3,2},{4,5},{5,4},{6,7},{7,6},{8,9},{9,8},{10,11... | collective-permute-start | bytes 3840008 | tf_op jit(solution)/shard_map/ppermute | solution.py:347
  238.2 58.4 %collective-permute-start.3 = (bf16[2,2,128,1600]{2,3,0,1:T(8,128)(2,1)S(1)}, bf16[2,2,128,1600]{2,3,0,1:T(8,128)(2,1)S(1)}, u32[]{:S(2)}, u32[]{:S(2)}) collective-permute-start(bf16[2,2,128,1600]{2,3,0,1:T(8,128)(2,1)S(1)} %pad_maximum_fusion.7), channel_id=1, source_target_pairs={{0,8},{1,9},{2,10},{3,11},{4,12},{5,13},{6,14},{7,15},{8,0},{9,1},... | collective-permute-start | bytes 4915208 | tf_op jit(solution)/shard_map/ppermute | solution.py:347
  242.3 62.8 %collective-permute-start.49 = (bf16[2,2,128,1600]{2,3,0,1:T(8,128)(2,1)}, bf16[2,2,128,1600]{2,3,0,1:T(8,128)(2,1)}, u32[]{:S(2)}, u32[]{:S(2)}) collective-permute-start(bf16[2,2,128,1600]{2,3,0,1:T(8,128)(2,1)} %pad_maximum_fusion.9), channel_id=1, source_target_pairs={{0,8},{1,9},{2,10},{3,11},{4,12},{5,13},{6,14},{7,15},{8,0},{9,1},... | collective-permute-start | bytes 4915208 | tf_op jit(solution)/shard_map/ppermute | solution.py:347
  242.9 26.7 %collective-permute-start.32 = (bf16[2,2,50,1600]{3,1,2,0:T(2,128)(2,1)S(1)}, bf16[2,2,50,1600]{3,1,2,0:T(2,128)(2,1)S(1)}, u32[]{:S(2)}, u32[]{:S(2)}) collective-permute-start(bf16[2,2,50,1600]{3,1,2,0:T(2,128)(2,1)S(1)} %collective-permute-done.31), channel_id=1, source_target_pairs={{2,0},{3,1},{4,2},{5,3},{10,8},{11,9},{12,10},{13,11},{18,16},{19,... | collective-permute-start | bytes 1920008 | tf_op jit(solution)/shard_map/ppermute | solution.py:347
  269.6 192.8 %collective-permute-start.41 = (bf16[4,200,1600]{2,1,0:T(8,128)(2,1)}, bf16[4,200,1600]{2,1,0:T(8,128)(2,1)}, u32[]{:S(2)}, u32[]{:S(2)}) collective-permute-start(bf16[4,200,1600]{2,1,0:T(8,128)(2,1)} %constant_dynamic-slice_fusion.33), channel_id=1, source_target_pairs={{0,16},{1,17},{2,18},{3,19},{4,20},{5,21},{6,22},{7,23},{8,24},{9,... | collective-permute-start | bytes 7680008 | tf_op jit(solution)/shard_map/ppermute | solution.py:347
  271.0 21.7 %collective-permute-start.33 = (bf16[2,2,50,1600]{3,1,2,0:T(2,128)(2,1)S(1)}, bf16[2,2,50,1600]{3,1,2,0:T(2,128)(2,1)S(1)}, u32[]{:S(2)}, u32[]{:S(2)}) collective-permute-start(bf16[2,2,50,1600]{3,1,2,0:T(2,128)(2,1)S(1)} %collective-permute-done.32), channel_id=1, source_target_pairs={{2,0},{3,1},{10,8},{11,9},{18,16},{19,17},{26,24},{27,25}} | collective-permute-start | bytes 1920008 | tf_op jit(solution)/shard_map/ppermute | solution.py:347
  278.2 100.6 %collective-permute-start.12 = (bf16[4,2,2,50,1344]{4,2,3,1,0:T(2,128)(2,1)}, bf16[4,2,2,50,1344]{4,2,3,1,0:T(2,128)(2,1)}, u32[]{:S(2)}, u32[]{:S(2)}) collective-permute-start(bf16[4,2,2,50,1344]{4,2,3,1,0:T(2,128)(2,1)} %constant_dynamic-slice_fusion.41), channel_id=1, source_target_pairs={{0,16},{1,17},{2,18},{3,19},{4,20},{5,21},{6,22},{7,23},{8,24},{9,... | collective-permute-start | bytes 6451208 | tf_op jit(solution)/shard_map/ppermute | solution.py:347
  292.8 178.4 %collective-permute-start.23 = (bf16[2,4,2,50,1600]{4,1,3,2,0:T(4,128)(2,1)}, bf16[2,4,2,50,1600]{4,1,3,2,0:T(4,128)(2,1)}, u32[]{:S(2)}, u32[]{:S(2)}) collective-permute-start(bf16[2,4,2,50,1600]{4,1,3,2,0:T(4,128)(2,1)} %copy.459), channel_id=1, source_target_pairs={{0,8},{1,9},{2,10},{3,11},{4,12},{5,13},{6,14},{7,15},{8,0},{9,1},... | collective-permute-start | bytes 7680008 | tf_op jit(solution)/shard_map/ppermute | solution.py:347
  296.7 199.1 %collective-permute-start.34 = (bf16[4,2,2,50,1600]{4,2,3,1,0:T(2,128)(2,1)}, bf16[4,2,2,50,1600]{4,2,3,1,0:T(2,128)(2,1)}, u32[]{:S(2)}, u32[]{:S(2)}) collective-permute-start(bf16[4,2,2,50,1600]{4,2,3,1,0:T(2,128)(2,1)} %constant_dynamic-slice_fusion.35), channel_id=1, source_target_pairs={{0,16},{1,17},{2,18},{3,19},{4,20},{5,21},{6,22},{7,23},{8,24},{9,... | collective-permute-start | bytes 7680008 | tf_op jit(solution)/shard_map/ppermute | solution.py:347
  494.3 20.7 %collective-permute-start.24 = (bf16[2,128,1600]{1,2,0:T(8,128)(2,1)S(1)}, bf16[2,128,1600]{1,2,0:T(8,128)(2,1)S(1)}, u32[]{:S(2)}, u32[]{:S(2)}) collective-permute-start(bf16[2,128,1600]{1,2,0:T(8,128)(2,1)S(1)} %copy_bitcast_fusion.2), channel_id=1, source_target_pairs={{0,1},{1,0},{2,3},{3,2},{4,5},{5,4},{6,7},{7,6},{8,9},{9,8},{10,11... | collective-permute-start | bytes 2457608 | tf_op jit(solution)/shard_map/ppermute | solution.py:347
  517.3 28.2 %collective-permute-start.25 = (bf16[2,2,128,1600]{2,3,0,1:T(8,128)(2,1)}, bf16[2,2,128,1600]{2,3,0,1:T(8,128)(2,1)}, u32[]{:S(2)}, u32[]{:S(2)}) collective-permute-start(bf16[2,2,128,1600]{2,3,0,1:T(8,128)(2,1)} %pad_maximum_fusion.8), channel_id=1, source_target_pairs={{0,8},{1,9},{2,10},{3,11},{4,12},{5,13},{6,14},{7,15},{8,0},{9,1},... | collective-permute-start | bytes 4915208 | tf_op jit(solution)/shard_map/ppermute | solution.py:347
  609.8 47.0 %collective-permute-start.50 = (bf16[2,2,128,1600]{2,3,1,0:T(8,128)(2,1)}, bf16[2,2,128,1600]{2,3,1,0:T(8,128)(2,1)}, u32[]{:S(2)}, u32[]{:S(2)}) collective-permute-start(bf16[2,2,128,1600]{2,3,1,0:T(8,128)(2,1)} %fusion.34), channel_id=1, source_target_pairs={{0,8},{1,9},{2,10},{3,11},{4,12},{5,13},{6,14},{7,15},{8,0},{9,1},... | collective-permute-start | bytes 4915208 | tf_op jit(solution)/shard_map/ppermute | solution.py:347
  629.6 30.8 %collective-permute-start.42 = (bf16[2,2,128,1600]{2,3,1,0:T(8,128)(2,1)S(1)}, bf16[2,2,128,1600]{2,3,1,0:T(8,128)(2,1)}, u32[]{:S(2)}, u32[]{:S(2)}) collective-permute-start(bf16[2,2,128,1600]{2,3,1,0:T(8,128)(2,1)S(1)} %fusion.33), channel_id=1, source_target_pairs={{0,8},{1,9},{2,10},{3,11},{4,12},{5,13},{6,14},{7,15},{8,0},{9,1},... | collective-permute-start | bytes 4915208 | tf_op jit(solution)/shard_map/ppermute | solution.py:347
  655.3 85.2 %collective-permute-start.85 = (bf16[4,200,1600]{2,1,0:T(8,128)(2,1)}, bf16[4,200,1600]{2,1,0:T(8,128)(2,1)}, u32[]{:S(2)}, u32[]{:S(2)}) collective-permute-start(bf16[4,200,1600]{2,1,0:T(8,128)(2,1)} %dynamic-slice_bitcast_fusion.2), channel_id=1, source_target_pairs={{0,16},{1,17},{2,18},{3,19},{4,20},{5,21},{6,22},{7,23},{8,24},{9,... | collective-permute-start | bytes 7680008 | tf_op jit(solution)/shard_map/ppermute | solution.py:347
  659.6 21.2 %collective-permute-start.51 = (bf16[2,128,1600]{1,2,0:T(8,128)(2,1)S(1)}, bf16[2,128,1600]{1,2,0:T(8,128)(2,1)S(1)}, u32[]{:S(2)}, u32[]{:S(2)}) collective-permute-start(bf16[2,128,1600]{1,2,0:T(8,128)(2,1)S(1)} %fusion.47), channel_id=1, source_target_pairs={{0,1},{1,0},{2,3},{3,2},{4,5},{5,4},{6,7},{7,6},{8,9},{9,8},{10,11... | collective-permute-start | bytes 2457608 | tf_op jit(solution)/shard_map/ppermute | solution.py:347
  662.6 34.5 %collective-permute-start.43 = (bf16[2,128,1600]{1,2,0:T(8,128)(2,1)S(1)}, bf16[2,128,1600]{1,2,0:T(8,128)(2,1)S(1)}, u32[]{:S(2)}, u32[]{:S(2)}) collective-permute-start(bf16[2,128,1600]{1,2,0:T(8,128)(2,1)S(1)} %fusion.46), channel_id=1, source_target_pairs={{0,1},{1,0},{2,3},{3,2},{4,5},{5,4},{6,7},{7,6},{8,9},{9,8},{10,11... | collective-permute-start | bytes 2457608 | tf_op jit(solution)/shard_map/ppermute | solution.py:347
  666.6 105.7 %collective-permute-start.76 = (bf16[4,2,2,50,1600]{4,0,3,2,1:T(4,128)(2,1)}, bf16[4,2,2,50,1600]{4,0,3,2,1:T(4,128)(2,1)}, u32[]{:S(2)}, u32[]{:S(2)}) collective-permute-start(bf16[4,2,2,50,1600]{4,0,3,2,1:T(4,128)(2,1)} %copy.517), channel_id=1, source_target_pairs={{0,16},{1,17},{2,18},{3,19},{4,20},{5,21},{6,22},{7,23},{8,24},{9,... | collective-permute-start | bytes 7680008 | tf_op jit(solution)/shard_map/ppermute | solution.py:347
  704.9 80.9 %collective-permute-start.45 = (bf16[128,1600]{0,1:T(8,128)(2,1)}, bf16[128,1600]{0,1:T(8,128)(2,1)}, u32[]{:S(2)}, u32[]{:S(2)}) collective-permute-start(bf16[128,1600]{0,1:T(8,128)(2,1)} %bitcast.700), channel_id=1, source_target_pairs={{0,2},{1,3},{2,10},{3,11},{4,0},{5,1},{6,8},{7,9},{8,6},{9,7},{10,... | collective-permute-start | bytes 1228808 | tf_op jit(solution)/shard_map/ppermute | solution.py:347
  710.5 76.8 %collective-permute-start.44 = (bf16[128,1600]{0,1:T(8,128)(2,1)}, bf16[128,1600]{0,1:T(8,128)(2,1)}, u32[]{:S(2)}, u32[]{:S(2)}) collective-permute-start(bf16[128,1600]{0,1:T(8,128)(2,1)} %bitcast.701), channel_id=1, source_target_pairs={{0,0},{1,1},{2,8},{3,9},{4,2},{5,3},{6,10},{7,11},{8,4},{9,5},{10,... | collective-permute-start | bytes 1228808 | tf_op jit(solution)/shard_map/ppermute | solution.py:347
  722.1 68.6 %collective-permute-start.52 = (bf16[2,2,128,448]{2,3,1,0:T(8,128)(2,1)S(1)}, bf16[2,2,128,448]{2,3,1,0:T(8,128)(2,1)}, u32[]{:S(2)}, u32[]{:S(2)}) collective-permute-start(bf16[2,2,128,448]{2,3,1,0:T(8,128)(2,1)S(1)} %bitcast.772), channel_id=1, source_target_pairs={{0,1},{1,0},{2,3},{3,2},{4,5},{5,4},{6,7},{7,6},{8,9},{9,8},{10,11... | collective-permute-start | bytes 1376264 | tf_op jit(solution)/shard_map/ppermute | solution.py:347
  740.6 250.8 %collective-permute-start.67 = (bf16[2,2,4,50,1600]{4,2,3,1,0:T(4,128)(2,1)}, bf16[2,2,4,50,1600]{4,2,3,1,0:T(4,128)(2,1)}, u32[]{:S(2)}, u32[]{:S(2)}) collective-permute-start(bf16[2,2,4,50,1600]{4,2,3,1,0:T(4,128)(2,1)} %copy.513), channel_id=1, source_target_pairs={{0,8},{1,9},{2,10},{3,11},{4,12},{5,13},{6,14},{7,15},{8,0},{9,1},... | collective-permute-start | bytes 7680008 | tf_op jit(solution)/shard_map/ppermute | solution.py:347
  772.4 23.6 %collective-permute-start.86 = (bf16[200,1600]{1,0:T(8,128)(2,1)S(1)}, bf16[200,1600]{1,0:T(8,128)(2,1)S(1)}, u32[]{:S(2)}, u32[]{:S(2)}) collective-permute-start(bf16[200,1600]{1,0:T(8,128)(2,1)S(1)} %get-tuple-element.104), channel_id=1, source_target_pairs={{0,2},{1,3},{8,10},{9,11},{16,18},{17,19},{24,26},{25,27}} | collective-permute-start | bytes 1920008 | tf_op jit(solution)/shard_map/ppermute | solution.py:347
  785.8 176.8 %collective-permute-start.89 = (bf16[200,1600]{1,0:T(8,128)(2,1)}, bf16[200,1600]{1,0:T(8,128)(2,1)}, u32[]{:S(2)}, u32[]{:S(2)}) collective-permute-start(bf16[200,1600]{1,0:T(8,128)(2,1)} %get-tuple-element.105), channel_id=1, source_target_pairs={{6,4},{7,5},{14,12},{15,13},{22,20},{23,21},{30,28},{31,29}} | collective-permute-start | bytes 1920008 | tf_op jit(solution)/shard_map/ppermute | solution.py:347
  787.3 21.1 %collective-permute-start.77 = (bf16[2,2,50,1600]{3,1,2,0:T(2,128)(2,1)S(1)}, bf16[2,2,50,1600]{3,1,2,0:T(2,128)(2,1)S(1)}, u32[]{:S(2)}, u32[]{:S(2)}) collective-permute-start(bf16[2,2,50,1600]{3,1,2,0:T(2,128)(2,1)S(1)} %bitcast.771), channel_id=1, source_target_pairs={{0,2},{1,3},{8,10},{9,11},{16,18},{17,19},{24,26},{25,27}} | collective-permute-start | bytes 1920008 | tf_op jit(solution)/shard_map/ppermute | solution.py:347
  790.8 24.5 %collective-permute-start.80 = (bf16[2,2,50,1600]{3,1,2,0:T(2,128)(2,1)S(1)}, bf16[2,2,50,1600]{3,1,2,0:T(2,128)(2,1)S(1)}, u32[]{:S(2)}, u32[]{:S(2)}) collective-permute-start(bf16[2,2,50,1600]{3,1,2,0:T(2,128)(2,1)S(1)} %bitcast.770), channel_id=1, source_target_pairs={{6,4},{7,5},{14,12},{15,13},{22,20},{23,21},{30,28},{31,29}} | collective-permute-start | bytes 1920008 | tf_op jit(solution)/shard_map/ppermute | solution.py:347
  796.0 23.0 %collective-permute-start.53 = (bf16[2,2,128,448]{2,3,1,0:T(8,128)(2,1)S(1)}, bf16[2,2,128,448]{2,3,1,0:T(8,128)(2,1)S(1)}, u32[]{:S(2)}, u32[]{:S(2)}) collective-permute-start(bf16[2,2,128,448]{2,3,1,0:T(8,128)(2,1)S(1)} %fusion.54), channel_id=1, source_target_pairs={{0,8},{1,9},{2,10},{3,11},{4,12},{5,13},{6,14},{7,15},{8,0},{9,1},... | collective-permute-start | bytes 1376264 | tf_op jit(solution)/shard_map/ppermute | solution.py:347
  808.4 154.3 %collective-permute-start.87 = (bf16[200,1600]{1,0:T(8,128)(2,1)}, bf16[200,1600]{1,0:T(8,128)(2,1)}, u32[]{:S(2)}, u32[]{:S(2)}) collective-permute-start(bf16[200,1600]{1,0:T(8,128)(2,1)} %bitcast_add_fusion.14), channel_id=1, source_target_pairs={{0,2},{1,3},{2,4},{3,5},{8,10},{9,11},{10,12},{11,13},{16,18},{17,... | collective-permute-start | bytes 1920008 | tf_op jit(solution)/shard_map/ppermute | solution.py:347
  815.2 132.1 %collective-permute-start.78 = (bf16[2,2,50,1600]{3,1,2,0:T(2,128)(2,1)}, bf16[2,2,50,1600]{3,1,2,0:T(2,128)(2,1)}, u32[]{:S(2)}, u32[]{:S(2)}) collective-permute-start(bf16[2,2,50,1600]{3,1,2,0:T(2,128)(2,1)} %bitcast_add_fusion.19), channel_id=1, source_target_pairs={{0,2},{1,3},{2,4},{3,5},{8,10},{9,11},{10,12},{11,13},{16,18},{17,... | collective-permute-start | bytes 1920008 | tf_op jit(solution)/shard_map/ppermute | solution.py:347
  819.0 133.7 %collective-permute-start.81 = (bf16[2,2,50,1600]{3,1,2,0:T(2,128)(2,1)}, bf16[2,2,50,1600]{3,1,2,0:T(2,128)(2,1)}, u32[]{:S(2)}, u32[]{:S(2)}) collective-permute-start(bf16[2,2,50,1600]{3,1,2,0:T(2,128)(2,1)} %bitcast_add_fusion.17), channel_id=1, source_target_pairs={{4,2},{5,3},{6,4},{7,5},{12,10},{13,11},{14,12},{15,13},{20,18},{2... | collective-permute-start | bytes 1920008 | tf_op jit(solution)/shard_map/ppermute | solution.py:347
  962.6 27.3 %collective-permute-start.54 = (bf16[2,2,128,1600]{2,3,1,0:T(8,128)(2,1)S(1)}, bf16[2,2,128,1600]{2,3,1,0:T(8,128)(2,1)S(1)}, u32[]{:S(2)}, u32[]{:S(2)}) collective-permute-start(bf16[2,2,128,1600]{2,3,1,0:T(8,128)(2,1)S(1)} %copy-done.51), channel_id=1, source_target_pairs={{0,8},{1,9},{2,10},{3,11},{4,12},{5,13},{6,14},{7,15},{8,0},{9,1},... | collective-permute-start | bytes 4915208 | tf_op jit(solution)/shard_map/ppermute | solution.py:347
  962.7 61.5 %collective-permute-start.58 = (bf16[4,2,2,50,1344]{4,0,3,2,1:T(4,128)(2,1)}, bf16[4,2,2,50,1344]{4,0,3,2,1:T(4,128)(2,1)}, u32[]{:S(2)}, u32[]{:S(2)}) collective-permute-start(bf16[4,2,2,50,1344]{4,0,3,2,1:T(4,128)(2,1)} %copy.498), channel_id=1, source_target_pairs={{0,16},{1,17},{2,18},{3,19},{4,20},{5,21},{6,22},{7,23},{8,24},{9,... | collective-permute-start | bytes 6451208 | tf_op jit(solution)/shard_map/ppermute | solution.py:347
  965.3 33.5 %collective-permute-start.88 = (bf16[200,1600]{1,0:T(8,128)(2,1)S(1)}, bf16[200,1600]{1,0:T(8,128)(2,1)S(1)}, u32[]{:S(2)}, u32[]{:S(2)}) collective-permute-start(bf16[200,1600]{1,0:T(8,128)(2,1)S(1)} %get-tuple-element.102), channel_id=1, source_target_pairs={{0,2},{1,3},{2,4},{3,5},{4,6},{5,7},{8,10},{9,11},{10,12},{11,13},... | collective-permute-start | bytes 1920008 | tf_op jit(solution)/shard_map/ppermute | solution.py:347
  984.8 26.3 %collective-permute-start.91 = (bf16[200,1600]{1,0:T(8,128)(2,1)S(1)}, bf16[200,1600]{1,0:T(8,128)(2,1)S(1)}, u32[]{:S(2)}, u32[]{:S(2)}) collective-permute-start(bf16[200,1600]{1,0:T(8,128)(2,1)S(1)} %bitcast_add_fusion.13), channel_id=1, source_target_pairs={{2,0},{3,1},{4,2},{5,3},{6,4},{7,5},{10,8},{11,9},{12,10},{13,11},... | collective-permute-start | bytes 1920008 | tf_op jit(solution)/shard_map/ppermute | solution.py:347
  989.9 25.4 %collective-permute-start.84 = (bf16[2,50,1600]{2,0,1:T(2,128)(2,1)}, bf16[2,50,1600]{2,0,1:T(2,128)(2,1)}, u32[]{:S(2)}, u32[]{:S(2)}) collective-permute-start(bf16[2,50,1600]{2,0,1:T(2,128)(2,1)} %bitcast.702), channel_id=1, source_target_pairs={{0,8},{1,9},{2,10},{3,11},{4,12},{5,13},{6,14},{7,15},{8,0},{9,1},... | collective-permute-start | bytes 960008 | tf_op jit(solution)/shard_map/ppermute | solution.py:347
  992.3 45.8 %collective-permute-start.55 = (bf16[2,128,1600]{1,2,0:T(8,128)(2,1)}, bf16[2,128,1600]{1,2,0:T(8,128)(2,1)}, u32[]{:S(2)}, u32[]{:S(2)}) collective-permute-start(bf16[2,128,1600]{1,2,0:T(8,128)(2,1)} %fusion.48), channel_id=1, source_target_pairs={{0,1},{1,0},{2,3},{3,2},{4,5},{5,4},{6,7},{7,6},{8,9},{9,8},{10,11... | collective-permute-start | bytes 2457608 | tf_op jit(solution)/shard_map/ppermute | solution.py:347
  998.8 188.5 %collective-permute-start.68 = (bf16[2,4,50,1600]{3,1,2,0:T(4,128)(2,1)}, bf16[2,4,50,1600]{3,1,2,0:T(4,128)(2,1)}, u32[]{:S(2)}, u32[]{:S(2)}) collective-permute-start(bf16[2,4,50,1600]{3,1,2,0:T(4,128)(2,1)} %bitcast.691), channel_id=1, source_target_pairs={{0,1},{1,0},{2,3},{3,2},{4,5},{5,4},{6,7},{7,6},{8,9},{9,8},{10,11... | collective-permute-start | bytes 3840008 | tf_op jit(solution)/shard_map/ppermute | solution.py:347
  1031.1 144.4 %collective-permute-start.59 = (bf16[2,2,50,1344]{3,1,2,0:T(2,128)(2,1)}, bf16[2,2,50,1344]{3,1,2,0:T(2,128)(2,1)}, u32[]{:S(2)}, u32[]{:S(2)}) collective-permute-start(bf16[2,2,50,1344]{3,1,2,0:T(2,128)(2,1)} %bitcast.695), channel_id=1, source_target_pairs={{0,2},{1,3},{8,10},{9,11},{16,18},{17,19},{24,26},{25,27}} | collective-permute-start | bytes 1612808 | tf_op jit(solution)/shard_map/ppermute | solution.py:347
  1036.5 147.2 %collective-permute-start.62 = (bf16[2,2,50,1344]{3,1,2,0:T(2,128)(2,1)}, bf16[2,2,50,1344]{3,1,2,0:T(2,128)(2,1)}, u32[]{:S(2)}, u32[]{:S(2)}) collective-permute-start(bf16[2,2,50,1344]{3,1,2,0:T(2,128)(2,1)} %bitcast.694), channel_id=1, source_target_pairs={{6,4},{7,5},{14,12},{15,13},{22,20},{23,21},{30,28},{31,29}} | collective-permute-start | bytes 1612808 | tf_op jit(solution)/shard_map/ppermute | solution.py:347
  1049.7 136.3 %collective-permute-start.57 = (bf16[128,1600]{0,1:T(8,128)(2,1)}, bf16[128,1600]{0,1:T(8,128)(2,1)}, u32[]{:S(2)}, u32[]{:S(2)}) collective-permute-start(bf16[128,1600]{0,1:T(8,128)(2,1)} %bitcast.698), channel_id=1, source_target_pairs={{0,2},{1,3},{2,10},{3,11},{4,0},{5,1},{6,8},{7,9},{8,6},{9,7},{10,... | collective-permute-start | bytes 1228808 | tf_op jit(solution)/shard_map/ppermute | solution.py:347
  1049.7 136.3 %collective-permute-start.56 = (bf16[128,1600]{0,1:T(8,128)(2,1)}, bf16[128,1600]{0,1:T(8,128)(2,1)}, u32[]{:S(2)}, u32[]{:S(2)}) collective-permute-start(bf16[128,1600]{0,1:T(8,128)(2,1)} %bitcast.699), channel_id=1, source_target_pairs={{0,0},{1,1},{2,8},{3,9},{4,2},{5,3},{6,10},{7,11},{8,4},{9,5},{10,... | collective-permute-start | bytes 1228808 | tf_op jit(solution)/shard_map/ppermute | solution.py:347
  1185.4 25.5 %collective-permute-start.63 = (bf16[2,2,50,1344]{3,1,2,0:T(2,128)(2,1)S(1)}, bf16[2,2,50,1344]{3,1,2,0:T(2,128)(2,1)S(1)}, u32[]{:S(2)}, u32[]{:S(2)}) collective-permute-start(bf16[2,2,50,1344]{3,1,2,0:T(2,128)(2,1)S(1)} %bitcast_add_fusion.23), channel_id=1, source_target_pairs={{4,2},{5,3},{6,4},{7,5},{12,10},{13,11},{14,12},{15,13},{20,18},{2... | collective-permute-start | bytes 1612808 | tf_op jit(solution)/shard_map/ppermute | solution.py:347
  1193.1 26.0 %collective-permute-start.61 = (bf16[2,2,50,1344]{3,1,2,0:T(2,128)(2,1)S(1)}, bf16[2,2,50,1344]{3,1,2,0:T(2,128)(2,1)S(1)}, u32[]{:S(2)}, u32[]{:S(2)}) collective-permute-start(bf16[2,2,50,1344]{3,1,2,0:T(2,128)(2,1)S(1)} %bitcast_add_fusion.26), channel_id=1, source_target_pairs={{0,2},{1,3},{2,4},{3,5},{4,6},{5,7},{8,10},{9,11},{10,12},{11,13},... | collective-permute-start | bytes 1612808 | tf_op jit(solution)/shard_map/ppermute | solution.py:347
  (128 other events, 2975.5 us)
Sparse Core Ops, SparseCore 0:
  1046.3 126.5 all-reduce.23

commit v2 on v0

--- a/solution.py
+++ b/solution.py
@@ -1,6 +1,11 @@
+import functools
+
 import jax
 import jax.numpy as jnp
+import numpy as np
 from jax import lax
+from jax.experimental import pallas as pl
+from jax.experimental.pallas import tpu as pltpu
 from jax.sharding import PartitionSpec as P
 
 D = 1600
@@ -76,7 +81,7 @@
     padded = jnp.pad(left, ((0, 0), (0, span)))
     first_row = start // width
     piece = lax.dynamic_slice_in_dim(padded, first_row, span, 1)
-    block = outer_sum(piece, right).reshape(-1)
+    block = outer_sum(piece, right).astype(jnp.bfloat16).reshape(-1)
     return lax.dynamic_slice_in_dim(block, start, count, 0)
 
 
@@ -262,7 +267,7 @@
         ("dp", "ctx"),
         scatter_dimension=0,
         tiled=True,
-    )
+    ).astype(jnp.float32)
     grad_proj = lax.psum_scatter(
         flat_term(
             jnp.concatenate(kept_context),
@@ -273,7 +278,7 @@
         ("dp", "ctx"),
         scatter_dimension=0,
         tiled=True,
-    )
+    ).astype(jnp.float32)
     grad_fc = lax.psum_scatter(
         flat_term(
             jnp.concatenate(kept_hidden_two),
@@ -284,7 +289,7 @@
         ("dp", "ctx"),
         scatter_dimension=0,
         tiled=True,
-    )
+    ).astype(jnp.float32)
     grad_out_w = lax.psum_scatter(
         flat_term(
             jnp.concatenate(kept_activ),
@@ -295,7 +300,7 @@
         ("dp", "ctx"),
         scatter_dimension=0,
         tiled=True,
-    )
+    ).astype(jnp.float32)
     grad_front, grad_tail = (
         lax.psum_scatter(front_grads, ("dp", "ctx"), scatter_dimension=0, tiled=True),
         lax.psum_scatter(tail_grads, ("dp", "ctx"), scatter_dimension=0, tiled=True),
@@ -312,6 +317,910 @@
     )
 
 
+DP, CTX = 4, 8
+YN, CN, ZN, XN = 2, 2, 4, 2
+SLOTS = 7
+HW = SLOTS * HEAD
+QW = 3 * HW
+STARTS = (0, 7, 13, 19)
+COUNTS = (7, 6, 6, 6)
+BLK = 128
+SEQ = 8 * BLK
+PIECE = 208
+WIDE = 8 * PIECE
+PB = 64
+PROJ = 32 * PB
+LOW = jnp.bfloat16
+F32 = jnp.float32
+VMEM_BYTES = 60 * 1024 * 1024
+ANY = pl.BlockSpec(memory_space=pl.ANY)
+VM = pl.BlockSpec(memory_space=pltpu.VMEM)
+
+
+def here():
+    dp, ctx = lax.axis_index("dp"), lax.axis_index("ctx")
+    return dp // CN, dp % CN, ctx // XN, ctx % XN
+
+
+def device(y, c, z, x):
+    return (y * CN + c, z * XN + x)
+
+
+class Wires:
+    def __init__(self, sems):
+        self.sems, self.used = sems, 0
+
+    def one(self):
+        self.used += 1
+        return self.sems.at[self.used - 1]
+
+    def far(self, source, target, where):
+        return pltpu.make_async_remote_copy(
+            src_ref=source,
+            dst_ref=target,
+            send_sem=self.one(),
+            recv_sem=self.one(),
+            device_id=where,
+            device_id_type=pl.DeviceIdType.MESH,
+        )
+
+    def near(self, source, target):
+        return pltpu.make_async_copy(source, target, self.one())
+
+
+def signal(where):
+    pl.semaphore_signal(
+        pltpu.get_barrier_semaphore(), inc=1, device_id=where, device_id_type=pl.DeviceIdType.MESH
+    )
+
+
+def team_peers(y, c, z, x):
+    return [device(y, 1 - c, z, x), device(y, c, z, 1 - x), device(y, 1 - c, z, 1 - x)]
+
+
+def grid_peers(y, c, z, x):
+    ring = [device(y, c, lax.rem(z + k, ZN), x) for k in range(1, ZN)]
+    return ring + [device(1 - y, c, z, x)]
+
+
+def meet(peers):
+    for peer in peers:
+        signal(peer)
+    pl.semaphore_wait(pltpu.get_barrier_semaphore(), len(peers))
+
+
+def call(body, name, ident, ins, outs, in_specs, out_specs, scratch, sems, cost=None):
+    return pl.pallas_call(
+        body,
+        out_shape=[jax.ShapeDtypeStruct(s, d) for s, d in outs],
+        in_specs=in_specs,
+        out_specs=out_specs,
+        scratch_shapes=list(scratch) + [pltpu.SemaphoreType.DMA((sems,))],
+        compiler_params=pltpu.CompilerParams(
+            collective_id=ident, has_side_effects=True, vmem_limit_bytes=VMEM_BYTES
+        ),
+        name=name,
+    )(*ins)
+
+
+class Gather:
+    def __init__(self, wires, piece, whole, spot):
+        y, c, z, x = self.spot = spot
+        self.z = z
+        self.across = device(1 - y, c, z, x)
+        up = device(y, c, lax.min(z + 1, ZN - 1), x)
+        down = device(y, c, lax.max(z - 1, 0), x)
+        self.local = wires.near(piece, whole.at[y, z])
+        self.mine = wires.far(piece, whole.at[y, z], self.across)
+        self.ups, self.downs, self.from_low, self.from_high = [], [], [], []
+        for turn in range(1, ZN):
+            low = lax.max(z - (turn - 1), 0)
+            high = lax.min(z + (turn - 1), ZN - 1)
+            source = piece if turn == 1 else whole.at[y, low]
+            self.ups.append(wires.far(source, whole.at[y, low], up))
+            source = piece if turn == 1 else whole.at[y, high]
+            self.downs.append(wires.far(source, whole.at[y, high], down))
+            low = lax.max(z - turn, 0)
+            high = lax.min(z + turn, ZN - 1)
+            self.from_low.append(wires.far(whole.at[y, low], whole.at[y, low], self.across))
+            self.from_high.append(wires.far(whole.at[y, high], whole.at[y, high], self.across))
+
+    def send_up(self, turn):
+        return (self.z >= turn - 1) & (self.z < ZN - 1)
+
+    def send_down(self, turn):
+        return (self.z <= ZN - turn) & (self.z > 0)
+
+    def start(self):
+        self.local.start()
+        self.mine.start()
+        pl.when(self.send_up(1))(self.ups[0].start)
+        pl.when(self.send_down(1))(self.downs[0].start)
+
+    def step(self, turn):
+        @pl.when(self.z >= turn)
+        def _():
+            self.ups[turn - 1].wait_recv()
+            if turn < ZN - 1:
+                pl.when(self.send_up(turn + 1))(self.ups[turn].start)
+            self.from_low[turn - 1].start()
+
+        @pl.when(self.z + turn <= ZN - 1)
+        def _():
+            self.downs[turn - 1].wait_recv()
+            if turn < ZN - 1:
+                pl.when(self.send_down(turn + 1))(self.downs[turn].start)
+            self.from_high[turn - 1].start()
+
+    def finish(self):
+        self.local.wait()
+        self.mine.wait()
+        for turn in range(1, ZN):
+            pl.when(self.send_up(turn))(self.ups[turn - 1].wait_send)
+            pl.when(self.send_down(turn))(self.downs[turn - 1].wait_send)
+            pl.when(self.z >= turn)(self.from_low[turn - 1].wait)
+            pl.when(self.z + turn <= ZN - 1)(self.from_high[turn - 1].wait)
+
+
+GATHER_SEMS = 1 + 2 + 2 * 4 * 3
+
+
+class Scatter:
+    def __init__(self, wires, parts, landed, arrived, spot):
+        y, c, z, x = spot
+        self.y, self.z = y, z
+        self.parts, self.landed, self.arrived = parts, landed, arrived
+        across = device(1 - y, c, z, x)
+        self.order = [lax.rem(z + k, ZN) for k in (1, 2, 3, 0)]
+        self.over = [wires.far(parts.at[1 - y, o], landed.at[o], across) for o in self.order]
+        self.along = [
+            wires.far(landed.at[o], arrived.at[k], device(y, c, o, x))
+            for k, o in enumerate(self.order[:3])
+        ]
+
+    def start(self):
+        for copy in self.over:
+            copy.start()
+
+    def step(self, k):
+        o = self.order[k]
+        self.over[k].wait_recv()
+        self.landed[o] = (self.landed[o].astype(F32) + self.parts[self.y, o].astype(F32)).astype(LOW)
+        self.along[k].start()
+
+    def finish(self, total):
+        self.over[3].wait_recv()
+        summed = self.landed[self.z].astype(F32) + self.parts[self.y, self.z].astype(F32)
+        for k in range(3):
+            self.along[k].wait_recv()
+            summed = summed + self.arrived[k].astype(F32)
+        total[...] = summed.astype(total.dtype)
+        for copy in self.over + self.along:
+            copy.wait_send()
+
+
+SCATTER_SEMS = 2 * 7
+
+
+class TeamGather:
+    def __init__(self, wires, block, whole, spot):
+        y, c, z, x = spot
+        mate, beside = device(y, 1 - c, z, x), device(y, c, z, 1 - x)
+        self.local = [wires.near(block.at[s], whole.at[c, s, x]) for s in range(2)]
+        self.to_mate = [wires.far(block.at[s], whole.at[c, s, x], mate) for s in range(2)]
+        self.to_side = [wires.far(block.at[s], whole.at[c, s, x], beside) for s in range(2)]
+        self.relay = [
+            wires.far(whole.at[c, s, 1 - x], whole.at[c, s, 1 - x], mate) for s in range(2)
+        ]
+
+    def start(self):
+        for copy in self.to_side + self.to_mate + self.local:
+            copy.start()
+
+    def step(self, s):
+        self.to_side[s].wait_recv()
+        self.relay[s].start()
+
+    def finish(self):
+        for copy in self.local + self.to_mate + self.relay:
+            copy.wait()
+        for copy in self.to_side:
+            copy.wait_send()
+
+
+TEAM_GATHER_SEMS = 2 + 2 * 6
+
+
+class TeamSwap:
+    def __init__(self, wires, source, target, spot):
+        y, c, z, x = spot
+        self.local = wires.near(source(c, x), target(c, x))
+        self.copies = [
+            wires.far(source(p, q), target(c, x), device(y, p, z, q))
+            for p, q in ((c, 1 - x), (1 - c, 1 - x), (1 - c, x))
+        ]
+
+    def start(self):
+        for copy in self.copies + [self.local]:
+            copy.start()
+
+    def finish(self):
+        for copy in self.copies + [self.local]:
+            copy.wait()
+
+
+TEAM_SWAP_SEMS = 1 + 2 * 3
+
+
+class TeamScatter:
+    def __init__(self, wires, parts, landed, leaving, arrived, spot):
+        y, c, z, x = spot
+        self.c, self.x = c, x
+        self.parts, self.landed, self.leaving, self.arrived = parts, landed, leaving, arrived
+        mate, beside = device(y, 1 - c, z, x), device(y, c, z, 1 - x)
+        self.to_mate = [wires.far(parts.at[1 - c, s], landed.at[s], mate) for s in range(2)]
+        self.to_side = [wires.far(leaving.at[s], arrived.at[s], beside) for s in range(2)]
+
+    def start(self):
+        for copy in self.to_mate:
+            copy.start()
+
+    def step(self, s):
+        self.to_mate[s].wait_recv()
+        far = 1 - self.x
+        self.leaving[s] = (
+            self.landed[s, far].astype(F32) + self.parts[self.c, s, far].astype(F32)
+        ).astype(LOW)
+        self.to_side[s].start()
+
+    def finish(self, total):
+        for s in range(2):
+            self.to_side[s].wait_recv()
+            total[s] = (
+                self.landed[s, self.x].astype(F32)
+                + self.parts[self.c, s, self.x].astype(F32)
+                + self.arrived[s].astype(F32)
+            )
+        for copy in self.to_mate + self.to_side:
+            copy.wait_send()
+
+
+TEAM_SCATTER_SEMS = 2 * 4
+
+
+def team_scatter_scratch(width):
+    return [
+        pltpu.VMEM((2, 2, BLK, width), LOW),
+        pltpu.VMEM((2, BLK, width), LOW),
+        pltpu.VMEM((2, BLK, width), LOW),
+    ]
+
+
+def scatter_scratch(rows, width):
+    return [pltpu.VMEM((ZN, rows, width), LOW), pltpu.VMEM((ZN - 1, rows, width), LOW)]
+
+
+class Tokens:
+    def __init__(self, wires, source, target, spot, back):
+        y, c, z, x = spot
+        self.own, self.local, self.copies, self.peers = [], [], [], []
+        for k in range(2):
+            if not back:
+                m = lax.rem(z + k, 2)
+                goal_c, goal_z = z // 2, 2 * m + c
+                block, landing = source.at[m], target.at[lax.rem(z, 2)]
+            else:
+                m = z // 2
+                s = lax.rem(m + k, 2)
+                goal_c, goal_z = lax.rem(z, 2), 2 * c + s
+                block, landing = source.at[s], target.at[m]
+            goal = device(y, goal_c, goal_z, x)
+            stays = (goal_c == c) & (goal_z == z)
+            self.own.append(stays)
+            self.peers.append(goal)
+            self.local.append(wires.near(block, landing))
+            self.copies.append(wires.far(block, landing, goal))
+
+    def start(self):
+        for stays, local, copy in zip(self.own, self.local, self.copies):
+            pl.when(stays)(local.start)
+            pl.when(jnp.logical_not(stays))(copy.start)
+
+    def finish(self):
+        for stays, local, copy in zip(self.own, self.local, self.copies):
+            pl.when(stays)(local.wait)
+            pl.when(jnp.logical_not(stays))(copy.wait)
+
+
+TOKENS_SEMS = 2 * 3
+
+
+def token_sources(spot, back):
+    y, c, z, x = spot
+    found = []
+    for k in range(2):
+        if back:
+            m = lax.rem(z + k, 2)
+            goal = (z // 2, 2 * m + c)
+        else:
+            s = lax.rem(z // 2 + k, 2)
+            goal = (lax.rem(z, 2), 2 * c + s)
+        found.append((device(y, goal[0], goal[1], x), (goal[0] == c) & (goal[1] == z)))
+    return found
+
+
+def meet_tokens(peers, spot, back):
+    for peer in peers:
+        signal(peer)
+    for source, stays in token_sources(spot, back):
+        pl.when(jnp.logical_not(stays))(functools.partial(signal, source))
+    leaving = sum(jnp.where(stays, 0, 1) for _, stays in token_sources(spot, not back))
+    pl.semaphore_wait(pltpu.get_barrier_semaphore(), len(peers) + leaving)
+
+
+def prologue(inputs, units_qkv, units_fc, small, tokens, got_qkv, got_fc, smalls, sems):
+    spot = y, c, z, x = here()
+    wires = Wires(sems)
+    meet_tokens(team_peers(*spot) + grid_peers(*spot), spot, False)
+    first = TeamSwap(
+        wires, lambda p, q: small, lambda p, q: smalls.at[y, z, p * XN + q], spot
+    )
+    qkv = TeamSwap(
+        wires, lambda p, q: units_qkv.at[p * XN + q], lambda p, q: got_qkv.at[p * XN + q], spot
+    )
+    fc = TeamSwap(
+        wires, lambda p, q: units_fc.at[p * XN + q], lambda p, q: got_fc.at[p * XN + q], spot
+    )
+    move = Tokens(wires, inputs, tokens, spot, False)
+    first.start()
+    move.start()
+    qkv.start()
+    fc.start()
+    first.finish()
+    column = [
+        wires.far(smalls.at[y, z], smalls.at[y, z], device(y, c, lax.rem(z + k, ZN), x))
+        for k in range(1, ZN)
+    ]
+    for copy in column:
+        copy.start()
+    for copy in column:
+        copy.wait()
+    over = wires.far(smalls.at[y], smalls.at[y], device(1 - y, c, z, x))
+    over.start()
+    over.wait()
+    qkv.finish()
+    fc.finish()
+    move.finish()
+
+
+def gather_all(
+    hidden, grads, piece_qkv, piece_fc, piece_out, piece_proj,
+    hidden_all, cotangent, all_qkv, all_fc, all_out, all_proj, sems,
+):
+    spot = y, c, z, x = here()
+    wires = Wires(sems)
+    rank = c * XN + x
+    meet_tokens(team_peers(*spot) + grid_peers(*spot), spot, False)
+    team = TeamGather(wires, hidden, hidden_all, spot)
+    qkv = Gather(wires, piece_qkv, all_qkv, spot)
+    proj = Gather(wires, piece_proj, all_proj.at[rank], spot)
+    fc = Gather(wires, piece_fc, all_fc, spot)
+    out = Gather(wires, piece_out, all_out, spot)
+    move = Tokens(wires, grads, cotangent, spot, False)
+    side = wires.far(all_proj.at[rank], all_proj.at[rank], device(y, c, z, 1 - x))
+    other = c * XN + 1 - x
+    mate = device(y, 1 - c, z, x)
+    relay = [
+        wires.far(all_proj.at[r], all_proj.at[r], mate) for r in (rank, other)
+    ]
+    team.start()
+    jobs = [qkv, proj, fc, out]
+    for job in jobs:
+        job.start()
+        if job is qkv:
+            team.step(0)
+            team.step(1)
+        for turn in range(1, ZN):
+            job.step(turn)
+        if job is fc:
+            proj.finish()
+            side.start()
+            relay[0].start()
+    move.start()
+    side.wait_recv()
+    relay[1].start()
+    for job in (qkv, fc, out):
+        job.finish()
+    team.finish()
+    move.finish()
+    side.wait_send()
+    for copy in relay:
+        copy.wait()
+
+
+def swap_context(context, got, sems):
+    spot = y, c, z, x = here()
+    wires = Wires(sems)
+    meet(team_peers(*spot))
+    copies = [
+        TeamSwap(wires, lambda p, q: context.at[p, s, q], lambda p, q: got.at[p * XN + q, s], spot)
+        for s in range(2)
+    ]
+    for copy in copies:
+        copy.start()
+    for copy in copies:
+        copy.finish()
+
+
+def gather_two(left, right, left_all, right_all, sems):
+    spot = here()
+    wires = Wires(sems)
+    meet(team_peers(*spot))
+    one = TeamGather(wires, left, left_all, spot)
+    two = TeamGather(wires, right, right_all, spot)
+    one.start()
+    one.step(0)
+    one.step(1)
+    two.start()
+    two.step(0)
+    two.step(1)
+    one.finish()
+    two.finish()
+
+
+def middle(
+    result_part, hidden_part, grad_out_part, grad_fc_part,
+    result, hidden, grad_out_w, grad_fc,
+    l1, s1, a1, l2, s2, a2, l3, a3, l4, a4, sems,
+):
+    spot = here()
+    wires = Wires(sems)
+    meet(team_peers(*spot) + grid_peers(*spot))
+    second = TeamScatter(wires, hidden_part, l2, s2, a2, spot)
+    first = TeamScatter(wires, result_part, l1, s1, a1, spot)
+    out = Scatter(wires, grad_out_part, l3, a3, spot)
+    fc = Scatter(wires, grad_fc_part, l4, a4, spot)
+    out.start()
+    second.start()
+    second.step(0)
+    second.step(1)
+    out.step(0)
+    first.start()
+    out.step(1)
+    first.step(0)
+    first.step(1)
+    second.finish(hidden)
+    out.step(2)
+    fc.start()
+    first.finish(result)
+    out.finish(grad_out_w)
+    fc.step(0)
+    fc.step(1)
+    fc.step(2)
+    fc.finish(grad_fc)
+
+
+def swap_grad_context(parts, whole, sems):
+    spot = y, c, z, x = here()
+    wires = Wires(sems)
+    meet(team_peers(*spot))
+    copies = [
+        TeamSwap(wires, lambda p, q: parts.at[p * XN + q, s], lambda p, q: whole.at[p, s, q], spot)
+        for s in range(2)
+    ]
+    for copy in copies:
+        copy.start()
+    for copy in copies:
+        copy.finish()
+
+
+def last(
+    hidden_part, grad_qkv_part, grad_proj_part, result,
+    hidden, grad_qkv, grad_proj, outputs,
+    l1, s1, a1, l2, a2, l3, a3, pm, pk, px, sems,
+):
+    spot = y, c, z, x = here()
+    wires = Wires(sems)
+    meet_tokens(team_peers(*spot) + grid_peers(*spot), spot, True)
+    first = TeamScatter(wires, hidden_part, l1, s1, a1, spot)
+    qkv = Scatter(wires, grad_qkv_part, l2, a2, spot)
+    to_mate = wires.far(grad_proj_part.at[1 - c], pm, device(y, 1 - c, z, x))
+    to_side = wires.far(pm.at[1 - x], px, device(y, c, z, 1 - x))
+    proj = Scatter(wires, pk, l3, a3, spot)
+    move = Tokens(wires, result, outputs, spot, True)
+    qkv.start()
+    to_mate.start()
+    first.start()
+    to_mate.wait_recv()
+    pm[1 - x] = (pm[1 - x].astype(F32) + grad_proj_part[c, 1 - x].astype(F32)).astype(LOW)
+    to_side.start()
+    first.step(0)
+    first.step(1)
+    qkv.step(0)
+    qkv.step(1)
+    qkv.step(2)
+    to_side.wait_recv()
+    pk[...] = (pm[x].astype(F32) + grad_proj_part[c, x].astype(F32) + px[...].astype(F32)).astype(LOW)
+    proj.start()
+    move.start()
+    first.finish(hidden)
+    qkv.finish(grad_qkv)
+    proj.step(0)
+    proj.step(1)
+    proj.step(2)
+    proj.finish(grad_proj)
+    move.finish()
+    to_mate.wait_send()
+    to_side.wait_send()
+
+
+def epilogue(
+    grads, units_qkv, units_fc, small, grad_in, got_qkv, got_fc, total, by_y, by_z, by_team, sems
+):
+    spot = y, c, z, x = here()
+    wires = Wires(sems)
+    meet_tokens(team_peers(*spot) + grid_peers(*spot), spot, True)
+    move = Tokens(wires, grads, grad_in, spot, True)
+    qkv = TeamSwap(
+        wires, lambda p, q: units_qkv.at[p * XN + q], lambda p, q: got_qkv.at[p * XN + q], spot
+    )
+    fc = TeamSwap(
+        wires, lambda p, q: units_fc.at[p * XN + q], lambda p, q: got_fc.at[p * XN + q], spot
+    )
+    over = wires.far(small.at[1 - y], by_y, device(1 - y, c, z, x))
+    over.start()
+    move.start()
+    qkv.start()
+    fc.start()
+    over.wait()
+    by_y[...] = by_y[...] + small[y]
+    column = [
+        wires.far(by_y.at[lax.rem(z + k, ZN)], by_z.at[k - 1], device(y, c, lax.rem(z + k, ZN), x))
+        for k in range(1, ZN)
+    ]
+    for copy in column:
+        copy.start()
+    for copy in column:
+        copy.wait()
+    by_z[3] = by_y[z] + by_z[0] + by_z[1] + by_z[2]
+    team = [
+        wires.far(by_z.at[3, p * XN + q], by_team.at[i], device(y, p, z, q))
+        for i, (p, q) in enumerate(((c, 1 - x), (1 - c, 1 - x), (1 - c, x)))
+    ]
+    for copy in team:
+        copy.start()
+    for copy in team:
+        copy.wait()
+    total[...] = by_z[3, c * XN + x] + by_team[0] + by_team[1] + by_team[2]
+    qkv.finish()
+    fc.finish()
+    move.finish()
+
+
+QB = 256
+
+
+def attend(mixed, context, totals):
+    for head in range(SLOTS):
+        lanes = slice(head * HEAD, (head + 1) * HEAD)
+        keys = mixed[:, HW + head * HEAD : HW + (head + 1) * HEAD]
+        values = mixed[:, 2 * HW + head * HEAD : 2 * HW + (head + 1) * HEAD]
+        for block in range(SEQ // QB):
+            rows = slice(block * QB, (block + 1) * QB)
+            upto = (block + 1) * QB
+            scores = (
+                lax.dot_general(
+                    mixed[rows, lanes], keys[:upto], (((1,), (1,)), ((), ())), preferred_element_type=F32
+                )
+                * 0.125
+            )
+            row = lax.broadcasted_iota(jnp.int32, (QB, upto), 0) + block * QB
+            col = lax.broadcasted_iota(jnp.int32, (QB, upto), 1)
+            scores = jnp.where(row >= col, scores, -1e30)
+            peak = jnp.max(scores, axis=1, keepdims=True)
+            weights = jnp.exp(scores - peak)
+            total = jnp.sum(weights, axis=1, keepdims=True)
+            prob = (weights * (1.0 / total)).astype(LOW)
+            context[rows, lanes] = jnp.dot(
+                prob, values[:upto], preferred_element_type=F32
+            ).astype(LOW)
+            totals[rows, head : head + 1] = peak + jnp.log(total)
+
+
+def attend_back(mixed, totals, grads, out, acc_k, acc_v):
+    for head in range(SLOTS):
+        lanes = slice(head * HEAD, (head + 1) * HEAD)
+        lanes_k = slice(HW + head * HEAD, HW + (head + 1) * HEAD)
+        lanes_v = slice(2 * HW + head * HEAD, 2 * HW + (head + 1) * HEAD)
+        keys = mixed[:, lanes_k]
+        values = mixed[:, lanes_v]
+        acc_k[...] = jnp.zeros_like(acc_k)
+        acc_v[...] = jnp.zeros_like(acc_v)
+        for block in range(SEQ // QB):
+            rows = slice(block * QB, (block + 1) * QB)
+            upto = (block + 1) * QB
+            queries = mixed[rows, lanes]
+            outer = grads[rows, lanes]
+            scores = (
+                lax.dot_general(
+                    queries, keys[:upto], (((1,), (1,)), ((), ())), preferred_element_type=F32
+                )
+                * 0.125
+            )
+            row = lax.broadcasted_iota(jnp.int32, (QB, upto), 0) + block * QB
+            col = lax.broadcasted_iota(jnp.int32, (QB, upto), 1)
+            scores = jnp.where(row >= col, scores, -1e30)
+            prob = jnp.exp(scores - totals[rows, head : head + 1])
+            dprob = lax.dot_general(
+                outer, values[:upto], (((1,), (1,)), ((), ())), preferred_element_type=F32
+            )
+            delta = jnp.sum(prob * dprob, axis=1, keepdims=True)
+            ds = (prob * (dprob - delta)).astype(LOW)
+            out[rows, lanes] = (
+                jnp.dot(ds, keys[:upto], preferred_element_type=F32) * 0.125
+            ).astype(LOW)
+            acc_k[:upto] += outer_sum(ds, queries)
+            acc_v[:upto] += outer_sum(prob.astype(LOW), outer)
+        out[:, lanes_k] = (acc_k[...] * 0.125).astype(LOW)
+        out[:, lanes_v] = acc_v[...].astype(LOW)
+
+
+def plain(body, name, ins, outs, scratch=()):
+    return pl.pallas_call(
+        body,
+        out_shape=[jax.ShapeDtypeStruct(s, d) for s, d in outs],
+        in_specs=[VM] * len(ins),
+        out_specs=[VM] * len(outs),
+        scratch_shapes=list(scratch),
+        compiler_params=pltpu.CompilerParams(vmem_limit_bytes=VMEM_BYTES),
+        name=name,
+    )(*ins)
+
+
+def pick(values, index):
+    return lax.dynamic_index_in_dim(values, index, 0, keepdims=False)
+
+
+def pad_to(values, axis, size):
+    widths = [(0, 0)] * values.ndim
+    widths[axis] = (0, size - values.shape[axis])
+    return jnp.pad(values, widths)
+
+
+def head_parts(columns):
+    return jnp.stack(
+        [
+            pad_to(columns[:, start * HEAD : (start + count) * HEAD], 1, HW)
+            for start, count in zip(STARTS, COUNTS)
+        ]
+    )
+
+
+def head_join(parts):
+    return jnp.concatenate([parts[r][:, : COUNTS[r] * HEAD] for r in range(4)], axis=1)
+
+
+def feature_order():
+    order = -np.ones((YN, ZN, PIECE), np.int32)
+    grid = np.arange(D).reshape(YN, CN, ZN, XN, 50).transpose(0, 2, 1, 3, 4)
+    order[:, :, :200] = grid.reshape(YN, ZN, 200)
+    return order.reshape(-1)
+
+
+def context_order():
+    natural = -np.ones(D, np.int32)
+    grid = np.arange(D).reshape(YN, CN, ZN, XN, 50).transpose(1, 3, 0, 2, 4).reshape(32, 50)
+    for block in range(32):
+        natural[grid[block]] = block * PB + np.arange(50)
+    order = -np.ones((4, HW), np.int32)
+    for r in range(4):
+        width = COUNTS[r] * HEAD
+        order[r, :width] = natural[STARTS[r] * HEAD : STARTS[r] * HEAD + width]
+    return order.reshape(-1)
+
+
+def one_hot(order, size):
+    rows = lax.broadcasted_iota(jnp.int32, (size, order.shape[0]), 0)
+    return (rows == jnp.asarray(order)[None, :]).astype(LOW)
+
+
+def dot(left, right):
+    return jnp.dot(left, right, preferred_element_type=F32)
+
+
+def ones_row(values):
+    return jnp.sum(values.astype(F32), axis=0)
+
+
+def fast_shards(inputs, grad_out, w_qkv, w_proj, w_fc, w_out, smalls):
+    y, c, z, x = here()
+    rank = c * XN + x
+    to_wide = one_hot(feature_order(), D)
+    to_heads = one_hot(context_order(), PROJ)
+
+    rows = w_qkv.reshape(50, 3, D)
+    units_qkv = jnp.stack([head_parts(rows[:, i]) for i in range(3)], axis=2).reshape(4, 50, QW)
+    units_qkv = pad_to(units_qkv, 1, 64)
+    units_fc = w_fc.reshape(50, YN, CN, ZN, XN, 200).transpose(2, 4, 0, 1, 3, 5)
+    units_fc = pad_to(pad_to(units_fc, 5, PIECE).reshape(4, 50, WIDE), 1, 64)
+    small = pad_to(smalls, 0, 2048).reshape(16, 128)
+    tokens, got_qkv, got_fc, smalls_all = call(
+        prologue, "prologue", 1,
+        (inputs.reshape(MICRO, BLK, D), units_qkv, units_fc, small),
+        [((2, BLK, D), LOW), ((4, 64, QW), LOW), ((4, 64, WIDE), LOW), ((YN, ZN, 4, 16, 128), LOW)],
+        [ANY] * 4, [ANY] * 4, [], 3 * TEAM_SWAP_SEMS + TOKENS_SEMS + 8,
+    )
+    small = smalls_all.reshape(YN, ZN, CN, XN, 2048)[..., :600].transpose(0, 2, 1, 3, 4)
+    small = small.reshape(-1).astype(F32)
+    gain1, shift1, bias_q, bias_v, bias_proj, gain2, shift2 = [segment(small, i) for i in range(7)]
+    bias_fc = small[7 * D : 7 * D + FF].reshape(YN, CN, ZN, XN, 200)
+    bias_fc = lax.dynamic_index_in_dim(bias_fc, c, 1, keepdims=False)
+    bias_fc = lax.dynamic_index_in_dim(bias_fc, x, 2, keepdims=False)
+    bias_fc = pad_to(bias_fc, 2, PIECE).reshape(WIDE)
+    bias_out = small[7 * D + FF :]
+    bias_qkv = jnp.stack(
+        [head_parts(bias_q[None]), jnp.zeros((4, 1, HW)), head_parts(bias_v[None])], axis=1
+    )
+    bias_qkv = pick(bias_qkv, rank).reshape(QW)
+
+    tokens = tokens.reshape(2 * BLK, D).astype(F32)
+    hidden_one, ln1_pull = jax.vjp(layer_norm, tokens, gain1, shift1)
+    hidden_one = dot(hidden_one.astype(LOW), to_wide).astype(LOW)
+    piece_qkv = pad_to(got_qkv[:, :50].reshape(200, QW), 0, PIECE)
+    piece_fc = pad_to(got_fc[:, :50].reshape(200, WIDE), 0, PIECE)
+    piece_out = pad_to(w_out.reshape(200, D), 0, PIECE)
+    piece_proj = pad_to(w_proj.reshape(50, D), 0, PB)
+    hidden_one, cotangent, mat_qkv, mat_fc, mat_out, mat_proj = call(
+        gather_all, "gather_all", 2,
+        (
+            hidden_one.reshape(2, BLK, WIDE), grad_out.reshape(MICRO, BLK, D),
+            piece_qkv, piece_fc, piece_out, piece_proj,
+        ),
+        [
+            ((2, 2, 2, BLK, WIDE), LOW), ((2, BLK, D), LOW), ((YN, ZN, PIECE, QW), LOW),
+            ((YN, ZN, PIECE, WIDE), LOW), ((YN, ZN, PIECE, D), LOW), ((4, YN, ZN, PB, D), LOW),
+        ],
+        [ANY] * 6, [ANY] * 6, [], TEAM_GATHER_SEMS + TOKENS_SEMS + 4 * GATHER_SEMS + 6,
+    )
+    hidden_one = hidden_one.reshape(SEQ, WIDE)
+    mat_qkv = mat_qkv.reshape(WIDE, QW)
+    mat_fc = mat_fc.reshape(WIDE, WIDE)
+    mat_out = mat_out.reshape(WIDE, D)
+    mat_proj = mat_proj.reshape(PROJ, D)
+
+    mixed = (dot(hidden_one, mat_qkv) + bias_qkv).astype(LOW)
+    context, totals = plain(
+        attend, "attend", (mixed,), [((SEQ, HW), LOW), ((SEQ, SLOTS), F32)]
+    )
+    (got,) = call(
+        swap_context, "swap_context", 3, (context.reshape(2, 2, 2, BLK, HW),),
+        [((4, 2, BLK, HW), LOW)], [ANY], [ANY], [], 2 * TEAM_SWAP_SEMS,
+    )
+    got = got.reshape(4, 2 * BLK, HW)
+    context = jnp.concatenate([got[r] for r in range(4)], axis=1)
+    context = back_product(context, to_heads).astype(LOW)
+    resid = tokens + dot(context, mat_proj) + bias_proj
+    hidden_two, ln2_pull = jax.vjp(layer_norm, resid, gain2, shift2)
+    hidden_two = dot(hidden_two.astype(LOW), to_wide).astype(LOW)
+    hidden_two, grad_all = call(
+        gather_two, "gather_two", 4, (hidden_two.reshape(2, BLK, WIDE), cotangent),
+        [((2, 2, 2, BLK, WIDE), LOW), ((2, 2, 2, BLK, D), LOW)],
+        [ANY] * 2, [ANY] * 2, [], 2 * TEAM_GATHER_SEMS,
+    )
+    hidden_two = hidden_two.reshape(SEQ, WIDE)
+    grad_all = grad_all.reshape(SEQ, D)
+    pre_act = dot(hidden_two, mat_fc) + bias_fc
+    activ, gelu_pull = jax.vjp(gelu_tanh, pre_act)
+    activ = activ.astype(LOW)
+    result_part = dot(activ, mat_out).astype(LOW)
+    (grad_pre,) = gelu_pull(back_product(grad_all, mat_out))
+    grad_pre = grad_pre.astype(LOW)
+    hidden_part = back_product(grad_pre, mat_fc).astype(LOW)
+    grad_out_part = outer_sum(activ, grad_all).astype(LOW)
+    grad_fc_part = outer_sum(hidden_two, grad_pre).astype(LOW)
+    result, grad_hidden_two, grad_out_w, grad_fc = call(
+        middle, "middle", 5,
+        (
+            result_part.reshape(2, 2, 2, BLK, D), hidden_part.reshape(2, 2, 2, BLK, WIDE),
+            grad_out_part.reshape(YN, ZN, PIECE, D), grad_fc_part.reshape(YN, ZN, PIECE, WIDE),
+        ),
+        [((2, BLK, D), F32), ((2, BLK, WIDE), F32), ((PIECE, D), F32), ((PIECE, WIDE), LOW)],
+        [VM] * 4, [VM] * 4,
+        team_scatter_scratch(D) + team_scatter_scratch(WIDE)
+        + scatter_scratch(PIECE, D) + scatter_scratch(PIECE, WIDE),
+        2 * TEAM_SCATTER_SEMS + 2 * SCATTER_SEMS,
+    )
+    result = (resid + result.reshape(2 * BLK, D) + bias_out).astype(LOW)
+    grad_out_w = grad_out_w[:200].reshape(-1)
+
+    grad_full = cotangent.reshape(2 * BLK, D).astype(F32)
+    grad_hidden_two = back_product(grad_hidden_two.reshape(2 * BLK, WIDE).astype(LOW), to_wide)
+    grad_ln_two, grad_gain_two, grad_shift_two = ln2_pull(grad_hidden_two)
+    grad_resid = grad_full + grad_ln_two
+    grad_branch = grad_resid.astype(LOW)
+    grad_context = back_product(grad_branch, mat_proj).astype(LOW)
+    grad_context = dot(grad_context, to_heads).astype(LOW)
+    grad_context = jnp.stack(
+        [grad_context[:, r * HW : (r + 1) * HW] for r in range(4)]
+    ).reshape(4, 2, BLK, HW)
+    (grad_context,) = call(
+        swap_grad_context, "swap_grad_context", 6, (grad_context,),
+        [((2, 2, 2, BLK, HW), LOW)], [ANY], [ANY], [], 2 * TEAM_SWAP_SEMS,
+    )
+    (grad_mixed,) = plain(
+        attend_back, "attend_back", (mixed, totals, grad_context.reshape(SEQ, HW)),
+        [((SEQ, QW), LOW)], [pltpu.VMEM((SEQ, HEAD), F32)] * 2,
+    )
+    hidden_part = back_product(grad_mixed, mat_qkv).astype(LOW)
+    grad_qkv_part = outer_sum(hidden_one, grad_mixed).astype(LOW)
+    grad_proj_part = outer_sum(context, grad_branch).astype(LOW)
+    grad_hidden_one, grad_qkv, grad_proj, outputs = call(
+        last, "last", 7,
+        (
+            hidden_part.reshape(2, 2, 2, BLK, WIDE), grad_qkv_part.reshape(YN, ZN, PIECE, QW),
+            grad_proj_part.reshape(CN, XN, YN, ZN, PB, D), result.reshape(2, BLK, D),
+        ),
+        [((2, BLK, WIDE), F32), ((PIECE, QW), LOW), ((PB, D), F32), ((2, BLK, D), LOW)],
+        [VM, VM, VM, ANY], [VM, VM, VM, ANY],
+        team_scatter_scratch(WIDE) + scatter_scratch(PIECE, QW) + scatter_scratch(PB, D)
+        + [
+            pltpu.VMEM((XN, YN, ZN, PB, D), LOW),
+            pltpu.VMEM((YN, ZN, PB, D), LOW),
+            pltpu.VMEM((YN, ZN, PB, D), LOW),
+        ],
+        TEAM_SCATTER_SEMS + 2 * SCATTER_SEMS + TOKENS_SEMS + 4,
+    )
+    grad_hidden_one = back_product(grad_hidden_one.reshape(2 * BLK, WIDE).astype(LOW), to_wide)
+    grad_ln_one, grad_gain_one, grad_shift_one = ln1_pull(grad_hidden_one)
+    grad_in = (grad_resid + grad_ln_one).astype(LOW)
+    grad_proj = grad_proj[:50].reshape(-1)
+
+    terms = ones_row(grad_mixed).reshape(3, HW)
+    mine = (jnp.arange(4) == rank).astype(F32)[:, None, None]
+    grad_bq = head_join(mine * terms[0][None, None])[0]
+    grad_bv = head_join(mine * terms[2][None, None])[0]
+    fc_terms = ones_row(grad_pre).reshape(YN, 1, ZN, 1, PIECE)[..., :200]
+    spot = (jnp.arange(CN) == c)[None, :, None, None, None] & (jnp.arange(XN) == x)[
+        None, None, None, :, None
+    ]
+    grad_fc_bias = jnp.where(spot, fc_terms, 0.0).reshape(-1)
+    front = jnp.concatenate([grad_gain_one, grad_shift_one, grad_bq, grad_bv])
+    tail = jnp.concatenate(
+        [
+            ones_row(grad_branch), grad_gain_two, grad_shift_two, grad_fc_bias,
+            jnp.sum(grad_full, axis=0),
+        ]
+    )
+    small = jnp.concatenate([front.reshape(32, 200), tail.reshape(32, 400)], axis=1)
+    small = pad_to(small, 1, 1024).reshape(YN, CN, ZN, XN, 8, 128).transpose(0, 2, 1, 3, 4, 5)
+    units_qkv = pad_to(grad_qkv[:200].reshape(4, 50, QW), 1, 64)
+    units_fc = pad_to(grad_fc[:200].reshape(4, 50, WIDE), 1, 64)
+    grad_in, got_qkv, got_fc, total = call(
+        epilogue, "epilogue", 8,
+        (grad_in.reshape(2, BLK, D), units_qkv, units_fc, small.reshape(YN, ZN, 4, 8, 128)),
+        [((MICRO, BLK, D), LOW), ((4, 64, QW), LOW), ((4, 64, WIDE), LOW), ((8, 128), F32)],
+        [ANY, ANY, ANY, VM], [ANY, ANY, ANY, VM],
+        [pltpu.VMEM((ZN, 4, 8, 128), F32), pltpu.VMEM((4, 4, 8, 128), F32), pltpu.VMEM((3, 8, 128), F32)],
+        2 * TEAM_SWAP_SEMS + TOKENS_SEMS + 14,
+    )
+    parts = got_qkv[:, :50].reshape(4, 50, 3, HW)
+    grad_qkv = jnp.stack([head_join(parts[:, :, i]) for i in range(3)], axis=1)
+    grad_qkv = grad_qkv.astype(F32).reshape(-1)
+    grad_fc = got_fc[:, :50].reshape(CN, XN, 50, YN, ZN, PIECE)[..., :200]
+    grad_fc = grad_fc.transpose(2, 3, 0, 4, 1, 5).astype(F32).reshape(-1)
+    total = total.reshape(-1)
+    return (
+        outputs[:, None],
+        grad_in.astype(F32)[:, None],
+        grad_qkv,
+        grad_proj,
+        grad_fc,
+        grad_out_w,
+        total[:200],
+        total[200:600],
+    )
+
+
 def solution(mesh):
     placed = (
         P(None, "dp", "ctx", None),
@@ -322,8 +1231,9 @@
         P(("dp", "ctx")),
         P(("dp", "ctx")),
     )
+    fast = dict(mesh.shape) == {"dp": DP, "ctx": CTX}
     return jax.shard_map(
-        shards,
+        fast_shards if fast else shards,
         mesh=mesh,
         in_specs=placed,
         out_specs=(

time: 3790 us -> 926 us (0.24)
  waiting for transfers between devices: 2330 us -> 0 us
  Pallas kernels: 0 us -> 650 us
  other arithmetic: 616 us -> 19.4 us
  matrix products: 345 us -> 135 us
  local copies, waits for them, and re-layouts: 304 us -> 111 us
  blocking collectives: 168 us -> 0 us
    unnamed x16 -> x0, waiting for transfers between devices: 1770 us -> none
    pallas_call x0 -> x10, Pallas kernels: none -> 650 us  [the longest x8 606 us: call(): pl.pallas_call(body, out_shape=[jax.ShapeDtypeStruct(s, d) for s, d in ou...]
    all_gather x4 -> x0, other arithmetic: 595 us -> none  [the longest x1 316 us: fetch(): lax.all_gather(w_qkv, ('dp', 'ctx'), axis=0, tiled=True)]
    all_gather x12 -> x0, waiting for transfers between devices: 565 us -> none  [the longest x1 220 us: fetch(): lax.all_gather(w_fc, ('dp', 'ctx'), axis=0, tiled=True)]
    dot_general x22 -> x7, matrix products: 213 us -> 56.1 us  [dot(): return jnp.dot(left, right, preferred_element_type=F32)]
    dynamic_slice x4 -> x1, local copies, waits for them, and re-layouts: 138 us -> 0.02 us  [fast_shards(): bias_fc = lax.dynamic_index_in_dim(bias_fc, x, 2, keepdims=False)]
    all_gather x4 -> x0, blocking collectives: 124 us -> none  [the longest x2 62.5 us: shards(): lax.all_gather(jnp.transpose(log_total[..., 0], (0, 2, 1)), 'ctx', axis=1...]
    reshape x4 -> x23, local copies, waits for them, and re-layouts: 113 us -> 28.6 us  [the longest x2 4.56 us: fast_shards(): grad_fc = grad_fc.transpose(2, 3, 0, 4, 1, 5).astype(F32).reshape(-1)]
  transfers between devices with their start and end apart: 14 -> 0, of which waited for: 8 -> 0; matrix products, arithmetic and copies ran while one was open for 32% -> 0% of each run, Pallas kernels for 0% -> 0%
where the time goes in v2:
time: 926 us; the launch traced here: 918 us
  Pallas kernels  650 us (70%)
  matrix products  135 us (15%)
  local copies, waits for them, and re-layouts  111 us (12%)
  other arithmetic  19.4 us (2%)
    pallas_call x8, Pallas kernels, call(): pl.pallas_call(body, out_shape=[jax.ShapeDtypeStruct(s, d) for s, d in ou...  606 us
    dot_general x7, matrix products, dot(): return jnp.dot(left, right, preferred_element_type=F32)  56.1 us
    pallas_call x2, Pallas kernels, plain(): pl.pallas_call(body, out_shape=[jax.ShapeDtypeStruct(s, d) for s, d in ou...  43.6 us
    dot_general x6, matrix products, back_product(): lax.dot_general(grad, weight, (((1,), (1,)), ((), ())), preferred_element...  41.4 us
    dot_general x4, matrix products, outer_sum(): lax.dot_general(left, right, (((0,), (0,)), ((), ())), preferred_element_...  37.7 us

profile of v2, /device:TPU:0, one launch (start us, length us, event | category | flops | bytes accessed | tf_op | source)
XLA Modules:
  0.0 918.2 jit_solution(11867799264526227744)
XLA Ops:
  1.9 1.3 pad_bitcast_fusion.9.small
  5.0 1.9 reshape.465
  12.1 2.4 reshape.467
  18.5 31.5 %prologue.1 = (bf16[2,128,1600]{2,1,0:T(8,128)(2,1)}, bf16[4,64,1344]{2,1,0:T(8,128)(2,1)}, bf16[4,64,1664]{2,1,0:T(8,128)(2,1)}, bf16[2,4,4,16,128]{4,3,2,1,0:T(8,128)(2,1)}) custom-call(bf16[2,128,1600]{2,1,0:T(8,128)(2,1)} %bitcast.224, bf16[4,64,1344]{2,1,0:T(8,128)(2,1)} %pad.102.units_qkv, bf16[4,64,1664]{2,1,0:T(8,128)(2,1)} %pad.104.units_fc, ...), custom_call_target="tpu_custom_call" | custom-call | tf_op jit(solution)/shard_map/prologue/pallas_call | solution.py:393
  51.2 1.4 convert_reduce_fusion.3
  52.5 1.5 multiply_reduce_fusion
  61.2 1.2 copy.110
  63.0 3.7 fusion.20
  66.7 200.1 %gather_all.1 = (bf16[2,2,2,128,1664]{4,3,2,1,0:T(8,128)(2,1)}, bf16[2,128,1600]{2,1,0:T(8,128)(2,1)}, bf16[2,4,208,1344]{3,2,1,0:T(8,128)(2,1)}, bf16[2,4,208,1...) custom-call(bf16[2,128,1664]{2,1,0:T(8,128)(2,1)} %bitcast.242, ...), custom_call_target="tpu_custom_call" | custom-call | tf_op jit(solution)/shard_map/gather_all/pallas_call | solution.py:393
  266.8 1.3 convert_reduce_fusion.4
  268.1 1.4 copy.115
  269.5 10.3 %add_convert_fusion.mixed = bf16[1024,1344]{1,0:T(8,128)(2,1)} fusion(bf16[1024,1664]{1,0:T(8,128)(2,1)} %bitcast.278, bf16[1664,1344]{1,0:T(8,128)(2,1)} %bitcast.276, f32[1344]{0:T(1024)S(1)} %add.183), kind=kOutput, calls=%fused_computation.26 | convolution fusion | flops 4582932480 | bytes 10638592 | tf_op jit(solution)/shard_map/dot_general | solution.py:1028
  279.8 17.7 %attend.1 = (bf16[1024,448]{1,0:T(8,128)(2,1)}, f32[1024,7]{1,0:T(8,128)}) custom-call(bf16[1024,1344]{1,0:T(8,128)(2,1)} %add_convert_fusion.mixed), custom_call_target="tpu_custom_call" | custom-call | tf_op jit(solution)/shard_map/attend/pallas_call | solution.py:969
  297.5 14.2 %swap_context.1 = bf16[4,2,128,448]{3,2,1,0:T(8,128)(2,1)} custom-call(bf16[2,2,2,128,448]{4,3,2,1,0:T(8,128)(2,1)} %bitcast.230), custom_call_target="tpu_custom_call" | custom-call | tf_op jit(solution)/shard_map/swap_context/pallas_call | solution.py:393
  311.8 2.1 fusion.42
  313.9 2.2 concatenate.37
  316.1 4.3 fusion.22
  320.5 6.3 fusion.53
  327.1 3.7 fusion.21
  330.8 54.1 %gather_two.1 = (bf16[2,2,2,128,1664]{4,3,2,1,0:T(8,128)(2,1)}, bf16[2,2,2,128,1600]{4,3,2,1,0:T(8,128)(2,1)}) custom-call(bf16[2,128,1664]{2,1,0:T(8,128)(2,1)} %bitcast.243, bf16[2,128,1600]{2,1,0:T(8,128)(2,1)} %get-tuple-element.41.right), custom_call_target="tpu_custom_call" | custom-call | tf_op jit(solution)/shard_map/gather_two/pallas_call | solution.py:393
  385.0 12.2 %fusion.54 = f32[1024,1664]{1,0:T(8,128)} fusion(bf16[1024,1664]{1,0:T(8,128)(2,1)} %bitcast.280, bf16[1664,1664]{1,0:T(8,128)(2,1)} %bitcast.268), kind=kOutput, calls=%fused_computation.167 | convolution fusion | flops 5670699008 | bytes 15761408 | tf_op jit(solution)/shard_map/dot_general | solution.py:1028
  397.2 11.8 %convolution_convert_fusion.6 = bf16[1024,1600]{0,1:T(8,128)(2,1)} fusion(bf16[1664,1600]{1,0:T(8,128)(2,1)} %bitcast.272, f32[1024,1664]{1,0:T(8,128)} %fusion.54, f32[1664]{0:T(1024)S(1)} %copy-done.29), kind=kOutput, calls=%fused_computation.33 | convolution fusion | flops 5471272960 | bytes 15424000 | tf_op jit(solution)/shard_map/dot_general | solution.py:1028
  409.1 12.8 %convert_reduce_fusion = (f32[1664]{0:T(1024)S(1)}, bf16[1024,1664]{1,0:T(8,128)(2,1)}) fusion(f32[1024,1664]{1,0:T(8,128)} %fusion.54, f32[1664]{0:T(1024)S(1)} %copy-done.29, bf16[1024,1600]{1,0:T(8,128)(2,1)S(1)} %bitcast.282, bf16[1664,1600]{1,0:T(8,128)(2,1)S(1)} %bitcast.275), kind=kOutput, calls=%fused_computation.23 | convolution fusion | flops 5491784192 | bytes 18838528 | tf_op jit(solution)/shard_map/dot_general | solution.py:73
  421.9 12.8 %convolution_convert_fusion.3 = bf16[1664,1600]{0,1:T(8,128)(2,1)} fusion(bf16[1024,1600]{1,0:T(8,128)(2,1)S(1)} %bitcast.283, f32[1024,1664]{1,0:T(8,128)} %fusion.54, f32[1664]{0:T(1024)S(1)} %copy-done.29), kind=kOutput, calls=%fused_computation.13 | convolution fusion | flops 5472296960 | bytes 15424000 | tf_op jit(solution)/shard_map/dot_general | solution.py:67
  434.7 8.2 convolution_convert_fusion.5
  443.2 5.5 copy.113
  448.7 9.3 %copy.114 = bf16[1664,1600]{1,0:T(8,128)(2,1)} copy(bf16[1664,1600]{0,1:T(8,128)(2,1)} %convolution_convert_fusion.3) | data formatting | bytes 10649600 | tf_op jit(solution)/shard_map/convert_element_type | solution.py:1119
  458.0 11.2 %convolution_convert_fusion.2 = bf16[1664,1664]{1,0:T(8,128)(2,1)} fusion(bf16[1024,1664]{1,0:T(8,128)(2,1)} %bitcast.281, bf16[1024,1664]{1,0:T(8,128)(2,1)} %get-tuple-element.99), kind=kOutput, calls=%fused_computation.12 | convolution fusion | flops 5673467904 | bytes 12353536 | tf_op jit(solution)/shard_map/dot_general | solution.py:67
  469.3 147.5 %middle.1 = (f32[2,128,1600]{2,1,0:T(8,128)}, f32[2,128,1664]{2,1,0:T(8,128)}, f32[208,1600]{1,0:T(8,128)}, bf16[208,1664]{1,0:T(8,128)(2,1)}) custom-call(bf16[2,2,2,128,1600]{4,3,2,1,0:T(8,128)(2,1)} %bitcast.217, bf16[2,2,2,128,1664]{4,3,2,1,0:T(8,128)(2,1)} %bitcast.225, bf16[2,4,208,1600]{3,2,1,0:T(8,128)(2,1)} %bitcast.215, ...), custom_call_target="tpu_custom_call" | custom-call | tf_op jit(solution)/shard_map/middle/pallas_call | solution.py:393
  616.8 2.4 convert_element_type.189
  619.2 2.8 copy.118
  622.0 2.0 slice.347
  624.0 2.1 reshape.499
  626.1 2.1 pad.118.units_fc
  628.2 3.7 multiply_reduce_fusion.1
  632.0 2.1 fusion.41
  635.7 8.0 fusion.23
  645.3 14.2 %swap_grad_context.1 = bf16[2,2,2,128,448]{4,3,2,1,0:T(8,128)(2,1)} custom-call(bf16[4,2,128,448]{3,2,1,0:T(8,128)(2,1)} %pad_maximum_fusion.parts), custom_call_target="tpu_custom_call" | custom-call | tf_op jit(solution)/shard_map/swap_grad_context/pallas_call | solution.py:393
  659.6 25.9 %attend_back.1 = bf16[1024,1344]{1,0:T(8,128)(2,1)} custom-call(bf16[1024,1344]{1,0:T(8,128)(2,1)} %add_convert_fusion.mixed, f32[1024,7]{1,0:T(8,128)} %get-tuple-element.40.totals, bf16[1024,448]{1,0:T(8,128)(2,1)} %bitcast.221), custom_call_target="tpu_custom_call" | custom-call | tf_op jit(solution)/shard_map/attend_back/pallas_call | solution.py:969
  685.5 10.2 %convolution_convert_fusion.4 = bf16[1024,1664]{1,0:T(8,128)(2,1)} fusion(bf16[1024,1344]{1,0:T(8,128)(2,1)} %attend_back.1, bf16[1664,1344]{1,0:T(8,128)(2,1)} %bitcast.277), kind=kOutput, calls=%fused_computation.31 | convolution fusion | flops 4581883904 | bytes 10633216 | tf_op jit(solution)/shard_map/dot_general | solution.py:73
  696.2 7.6 convolution_convert_fusion
  704.4 7.5 copy.116
  711.9 1.3 copy.119
  713.2 1.4 slice.390
  714.7 1.7 reshape.509
  716.4 6.1 convolution_convert_fusion.1
  722.5 9.6 %copy.117 = bf16[2048,1600]{1,0:T(8,128)(2,1)} copy(bf16[2048,1600]{0,1:T(8,128)(2,1)} %convolution_convert_fusion.1) | data formatting | bytes 13107200 | tf_op jit(solution)/shard_map/convert_element_type | solution.py:1156
  732.1 113.8 %last.1 = (f32[2,128,1664]{2,1,0:T(8,128)}, bf16[208,1344]{1,0:T(8,128)(2,1)}, f32[64,1600]{1,0:T(8,128)}, bf16[2,128,1600]{2,1,0:T(8,128)(2,1)}) custom-call(bf16[2,2,2,128,1664]{4,3,2,1,0:T(8,128)(2,1)} %bitcast.226, bf16[2,4,208,1344]{3,2,1,0:T(8,128)(2,1)} %bitcast.216, bf16[2,2,2,4,64,1600]{5,4,3,2,1,0:T(8,128)(2,1)} %bitcast.214, ...), custom_call_target="tpu_custom_call" | custom-call | tf_op jit(solution)/shard_map/last/pallas_call | solution.py:393
  845.9 2.1 copy.126
  848.1 1.8 slice.387
  849.8 2.0 reshape.505
  851.8 1.9 slice.346
  853.7 2.0 reshape.498
  855.8 2.0 pad.117.units_qkv
  857.8 1.5 convert_element_type.198
  859.4 2.2 multiply_reduce_fusion.3
  863.8 3.4 add_convert_fusion.1
  868.1 2.2 copy.120
  870.3 30.5 %epilogue.1 = (bf16[2,128,1600]{2,1,0:T(8,128)(2,1)}, bf16[4,64,1344]{2,1,0:T(8,128)(2,1)}, bf16[4,64,1664]{2,1,0:T(8,128)(2,1)}, f32[8,128]{1,0:T(8,128)}) custom-call(bf16[2,128,1600]{2,1,0:T(8,128)(2,1)} %bitcast.222, bf16[4,64,1344]{2,1,0:T(8,128)(2,1)} %pad.117.units_qkv, bf16[4,64,1664]{2,1,0:T(8,128)(2,1)} %pad.118.units_fc, ...), custom_call_target="tpu_custom_call" | custom-call | tf_op jit(solution)/shard_map/epilogue/pallas_call | solution.py:393
  902.1 1.3 slice.392
  907.7 1.8 reshape.515
  909.6 1.4 reshape.521
  912.3 3.7 reshape.517
  916.1 1.6 copy.127
  (231 shorter events, 35.4 us)
Async XLA Ops:
  8.1 2.5 copy-start.16
  8.5 3.6 copy-start.17
  14.5 2.8 copy-start.13
  52.5 10.5 %copy-start.21 = (f32[256]{0:T(256)}, f32[256]{0:T(256)S(1)}, u32[]{:S(2)}) copy-start(f32[256]{0:T(256)S(1)} %get-tuple-element.161) | copy-start | bytes 3076
  54.1 0.6 copy-start.25
  54.7 8.3 copy-start.23
  55.4 7.6 copy-start.18
  57.8 3.4 copy-start.14
  58.1 4.4 copy-start.4
  60.1 2.9 copy-start.34
  63.0 257.4 %copy-start = (f32[256,1600]{0,1:T(8,128)}, f32[256,1600]{0,1:T(8,128)S(1)}, u32[]{:S(2)}) copy-start(f32[256,1600]{0,1:T(8,128)S(1)} %copy.108) | copy-start | bytes 4915204
  316.1 4.3 copy-start.28
  320.4 6.4 copy-start.11
  320.4 6.6 copy-start.20
  320.4 6.6 copy-start.27
  320.4 6.6 copy-start.35
  326.8 4.0 copy-start.5
  384.9 12.3 %copy-start.29 = (f32[1664]{0:T(1024)S(1)}, f32[1664]{0:T(1024)}, u32[]{:S(2)}) copy-start(f32[1664]{0:T(1024)} %add.194) | copy-start | bytes 19972
  385.0 24.1 %slice-start.2 = ((s8[5537792]{0:T(1024)(128)(4,1)}), s8[4194304]{0:T(1024)(128)(4,1)S(1)}, s32[]{:S(2)}) async-start(s8[5537792]{0:T(1024)(128)(4,1)} %bitcast.273), calls=%async_computation.2 | async-start | bytes 8388608
  397.2 11.9 %slice-start.3 = ((s8[5537792]{0:T(1024)(128)(4,1)}), s8[1343488]{0:T(1024)(128)(4,1)S(1)}, s32[]{:S(2)}) async-start(s8[5537792]{0:T(1024)(128)(4,1)} %bitcast.273), calls=%async_computation.3 | async-start | bytes 2686976
  397.2 11.9 %copy-start.33 = (bf16[2,2,2,128,1600]{4,3,2,1,0:T(8,128)(2,1)S(1)}, bf16[2,2,2,128,1600]{4,3,2,1,0:T(8,128)(2,1)}, u32[]{:S(2)}) copy-start(bf16[2,2,2,128,1600]{4,3,2,1,0:T(8,128)(2,1)} %get-tuple-element.47) | copy-start | bytes 9830404
  397.2 37.4 %slice-start = ((s8[5537792]{0:T(1024)(128)(4,1)}), s8[4194304]{0:T(1024)(128)(4,1)S(1)}, s32[]{:S(2)}) async-start(s8[5537792]{0:T(1024)(128)(4,1)} %bitcast.269), calls=%async_computation | async-start | bytes 8388608
  409.1 25.6 %slice-start.1 = ((s8[5537792]{0:T(1024)(128)(4,1)}), s8[1343488]{0:T(1024)(128)(4,1)S(1)}, s32[]{:S(2)}) async-start(s8[5537792]{0:T(1024)(128)(4,1)} %bitcast.269), calls=%async_computation.1 | async-start | bytes 2686976
  421.9 12.8 %copy-start.37 = (bf16[1024,1664]{1,0:T(8,128)(2,1)S(1)}, bf16[1024,1664]{1,0:T(8,128)(2,1)}, u32[]{:S(2)}) copy-start(bf16[1024,1664]{1,0:T(8,128)(2,1)} %get-tuple-element.99) | copy-start | bytes 10223620
  434.7 8.3 copy-start.31
  619.2 9.0 copy-start.6
  628.2 3.8 copy-start.7
  634.1 1.2 copy-start.2
  634.1 1.6 copy-start.36
  635.7 8.0 copy-start.9
  685.5 10.2 %copy-start.3 = (bf16[1024,1344]{1,0:T(8,128)(2,1)S(1)}, bf16[1024,1344]{1,0:T(8,128)(2,1)}, u32[]{:S(2)}) copy-start(bf16[1024,1344]{1,0:T(8,128)(2,1)} %attend_back.1) | copy-start | bytes 8257540
  685.5 10.7 %copy-start.32 = (bf16[2,2,2,128,1664]{4,3,2,1,0:T(8,128)(2,1)S(1)}, bf16[2,2,2,128,1664]{4,3,2,1,0:T(8,128)(2,1)}, u32[]{:S(2)}) copy-start(bf16[2,2,2,128,1664]{4,3,2,1,0:T(8,128)(2,1)} %get-tuple-element.38) | copy-start | bytes 10223620
  696.2 7.6 copy-start.30
  704.4 7.5 copy-start.10
  849.8 9.5 %copy-start.1 = (f32[256,1600]{0,1:T(8,128)S(1)}, f32[256,1600]{0,1:T(8,128)}, u32[]{:S(2)}) copy-start(f32[256,1600]{0,1:T(8,128)} %copy-done) | copy-start | bytes 4915204
  849.8 9.5 %copy-start.19 = (f32[1600]{0:T(1024)S(1)}, f32[1600]{0:T(1024)}, u32[]{:S(2)}) copy-start(f32[1600]{0:T(1024)} %copy-done.18) | copy-start | bytes 19204
  849.8 9.6 %copy-start.22 = (f32[256]{0:T(256)S(1)}, f32[256]{0:T(256)}, u32[]{:S(2)}) copy-start(f32[256]{0:T(256)} %copy-done.21) | copy-start | bytes 3076
  859.4 2.2 copy-start.26
  859.4 3.4 copy-start.24
  861.6 1.2 copy-start.8
  907.0 2.5 copy-start.15
  911.4 4.6 copy-start.12

commit v3 on v2

--- a/solution.py
+++ b/solution.py
@@ -468,16 +468,21 @@
 class Scatter:
     def __init__(self, wires, parts, landed, arrived, spot):
         y, c, z, x = spot
-        self.y, self.z = y, z
+        self.y, self.z, self.size = y, z, landed.shape[1]
         self.parts, self.landed, self.arrived = parts, landed, arrived
         across = device(1 - y, c, z, x)
         self.order = [lax.rem(z + k, ZN) for k in (1, 2, 3, 0)]
-        self.over = [wires.far(parts.at[1 - y, o], landed.at[o], across) for o in self.order]
+        self.over = [
+            wires.far(parts.at[self.rows(1 - y, o)], landed.at[o], across) for o in self.order
+        ]
         self.along = [
             wires.far(landed.at[o], arrived.at[k], device(y, c, o, x))
             for k, o in enumerate(self.order[:3])
         ]
 
+    def rows(self, y, z):
+        return pl.ds(pl.multiple_of((y * ZN + z) * self.size, 16), self.size)
+
     def start(self):
         for copy in self.over:
             copy.start()
@@ -485,12 +490,12 @@
     def step(self, k):
         o = self.order[k]
         self.over[k].wait_recv()
-        self.landed[o] = (self.landed[o].astype(F32) + self.parts[self.y, o].astype(F32)).astype(LOW)
+        self.landed[o] = (self.landed[o].astype(F32) + self.parts[self.rows(self.y, o), :].astype(F32)).astype(LOW)
         self.along[k].start()
 
     def finish(self, total):
         self.over[3].wait_recv()
-        summed = self.landed[self.z].astype(F32) + self.parts[self.y, self.z].astype(F32)
+        summed = self.landed[self.z].astype(F32) + self.parts[self.rows(self.y, self.z), :].astype(F32)
         for k in range(3):
             self.along[k].wait_recv()
             summed = summed + self.arrived[k].astype(F32)
@@ -558,8 +563,11 @@
         self.c, self.x = c, x
         self.parts, self.landed, self.leaving, self.arrived = parts, landed, leaving, arrived
         mate, beside = device(y, 1 - c, z, x), device(y, c, z, 1 - x)
-        self.to_mate = [wires.far(parts.at[1 - c, s], landed.at[s], mate) for s in range(2)]
+        self.to_mate = [wires.far(parts.at[half_rows(1 - c, s)], landed.at[s], mate) for s in range(2)]
         self.to_side = [wires.far(leaving.at[s], arrived.at[s], beside) for s in range(2)]
+
+    def side(self, x):
+        return pl.ds(pl.multiple_of(x * BLK, BLK), BLK)
 
     def start(self):
         for copy in self.to_mate:
@@ -569,7 +577,8 @@
         self.to_mate[s].wait_recv()
         far = 1 - self.x
         self.leaving[s] = (
-            self.landed[s, far].astype(F32) + self.parts[self.c, s, far].astype(F32)
+            self.landed[s, self.side(far), :].astype(F32)
+            + self.parts[block_rows(self.c, s, far), :].astype(F32)
         ).astype(LOW)
         self.to_side[s].start()
 
@@ -577,20 +586,28 @@
         for s in range(2):
             self.to_side[s].wait_recv()
             total[s] = (
-                self.landed[s, self.x].astype(F32)
-                + self.parts[self.c, s, self.x].astype(F32)
+                self.landed[s, self.side(self.x), :].astype(F32)
+                + self.parts[block_rows(self.c, s, self.x), :].astype(F32)
                 + self.arrived[s].astype(F32)
             )
         for copy in self.to_mate + self.to_side:
             copy.wait_send()
 
 
+def block_rows(c, s, x):
+    return pl.ds(pl.multiple_of((c * 4 + s * 2 + x) * BLK, BLK), BLK)
+
+
+def half_rows(c, s):
+    return pl.ds(pl.multiple_of((c * 2 + s) * 2 * BLK, 2 * BLK), 2 * BLK)
+
+
 TEAM_SCATTER_SEMS = 2 * 4
 
 
 def team_scatter_scratch(width):
     return [
-        pltpu.VMEM((2, 2, BLK, width), LOW),
+        pltpu.VMEM((2, 2 * BLK, width), LOW),
         pltpu.VMEM((2, BLK, width), LOW),
         pltpu.VMEM((2, BLK, width), LOW),
     ]
@@ -658,7 +675,10 @@
     pl.semaphore_wait(pltpu.get_barrier_semaphore(), len(peers) + leaving)
 
 
-def prologue(inputs, units_qkv, units_fc, small, tokens, got_qkv, got_fc, smalls, sems):
+def prologue(
+    inputs, units_qkv, units_fc, small, piece_out,
+    tokens, got_qkv, got_fc, smalls, all_out, sems,
+):
     spot = y, c, z, x = here()
     wires = Wires(sems)
     meet_tokens(team_peers(*spot) + grid_peers(*spot), spot, False)
@@ -672,182 +692,319 @@
         wires, lambda p, q: units_fc.at[p * XN + q], lambda p, q: got_fc.at[p * XN + q], spot
     )
     move = Tokens(wires, inputs, tokens, spot, False)
+    out = Gather(wires, piece_out, all_out, spot)
+    column = [
+        wires.far(smalls.at[y, z], smalls.at[y, z], device(y, c, lax.rem(z + k, ZN), x))
+        for k in range(1, ZN)
+    ]
+    over = wires.far(smalls.at[y], smalls.at[y], device(1 - y, c, z, x))
     first.start()
     move.start()
     qkv.start()
     fc.start()
     first.finish()
-    column = [
-        wires.far(smalls.at[y, z], smalls.at[y, z], device(y, c, lax.rem(z + k, ZN), x))
-        for k in range(1, ZN)
-    ]
     for copy in column:
         copy.start()
+    out.start()
     for copy in column:
         copy.wait()
-    over = wires.far(smalls.at[y], smalls.at[y], device(1 - y, c, z, x))
     over.start()
     over.wait()
+    out.step(1)
+    move.finish()
     qkv.finish()
     fc.finish()
-    move.finish()
-
-
-def gather_all(
-    hidden, grads, piece_qkv, piece_fc, piece_out, piece_proj,
-    hidden_all, cotangent, all_qkv, all_fc, all_out, all_proj, sems,
+    out.step(2)
+    out.step(3)
+    out.finish()
+
+
+def gather_first(
+    hidden, grads, piece_qkv, piece_proj, hidden_all, cotangent, all_qkv, all_proj, sems,
 ):
     spot = y, c, z, x = here()
     wires = Wires(sems)
     rank = c * XN + x
     meet_tokens(team_peers(*spot) + grid_peers(*spot), spot, False)
     team = TeamGather(wires, hidden, hidden_all, spot)
+    bring = Tokens(wires, grads, cotangent, spot, False)
     qkv = Gather(wires, piece_qkv, all_qkv, spot)
     proj = Gather(wires, piece_proj, all_proj.at[rank], spot)
-    fc = Gather(wires, piece_fc, all_fc, spot)
-    out = Gather(wires, piece_out, all_out, spot)
-    move = Tokens(wires, grads, cotangent, spot, False)
     side = wires.far(all_proj.at[rank], all_proj.at[rank], device(y, c, z, 1 - x))
-    other = c * XN + 1 - x
     mate = device(y, 1 - c, z, x)
     relay = [
-        wires.far(all_proj.at[r], all_proj.at[r], mate) for r in (rank, other)
+        wires.far(all_proj.at[r], all_proj.at[r], mate) for r in (rank, c * XN + 1 - x)
     ]
+    proj.start()
+    qkv.start()
     team.start()
-    jobs = [qkv, proj, fc, out]
-    for job in jobs:
-        job.start()
-        if job is qkv:
-            team.step(0)
-            team.step(1)
-        for turn in range(1, ZN):
-            job.step(turn)
-        if job is fc:
-            proj.finish()
-            side.start()
-            relay[0].start()
-    move.start()
+    proj.step(1)
+    proj.step(2)
+    proj.step(3)
+    qkv.step(1)
+    team.step(0)
+    team.step(1)
+    proj.finish()
+    side.start()
+    relay[0].start()
+    bring.start()
+    qkv.step(2)
+    qkv.step(3)
     side.wait_recv()
     relay[1].start()
-    for job in (qkv, fc, out):
-        job.finish()
+    qkv.finish()
     team.finish()
-    move.finish()
+    bring.finish()
     side.wait_send()
     for copy in relay:
         copy.wait()
 
 
-def swap_context(context, got, sems):
+def attention(
+    hidden, mat_qkv, bias_qkv, piece_fc, cotangent, mixed, context, totals, got, all_fc, grad_all,
+    hidden_in, mat_in, sems,
+):
     spot = y, c, z, x = here()
     wires = Wires(sems)
-    meet(team_peers(*spot))
-    copies = [
-        TeamSwap(wires, lambda p, q: context.at[p, s, q], lambda p, q: got.at[p * XN + q, s], spot)
+    load = [wires.near(mat_qkv, mat_in), wires.near(hidden, hidden_in)]
+    for copy in load:
+        copy.start()
+    meet(team_peers(*spot) + grid_peers(*spot))
+    fc = Gather(wires, piece_fc, all_fc, spot)
+    fc.start()
+    team = TeamGather(wires, cotangent, grad_all, spot)
+    team.start()
+    swaps = [
+        TeamSwap(
+            wires,
+            lambda p, q, s=s: context.at[block_rows(p, s, q)],
+            lambda p, q, s=s: got.at[p * XN + q, s],
+            spot,
+        )
         for s in range(2)
     ]
-    for copy in copies:
+    for copy in load:
+        copy.wait()
+
+    @pl.loop(0, SEQ // QB)
+    def _(i):
+        rows = pl.ds(pl.multiple_of(i * QB, QB), QB)
+        mixed[rows, :] = (dot(hidden_in[rows, :], mat_in[...]) + bias_qkv[...]).astype(LOW)
+
+    for head in range(SLOTS):
+        attend(mixed, context, totals, head)
+        if head == 2:
+            fc.step(1)
+        if head == 4:
+            team.step(0)
+            team.step(1)
+    for copy in swaps:
         copy.start()
-    for copy in copies:
+    fc.step(2)
+    for copy in swaps:
         copy.finish()
-
-
-def gather_two(left, right, left_all, right_all, sems):
+    fc.step(3)
+    team.finish()
+    fc.finish()
+
+
+def gather_second(block, whole, sems):
     spot = here()
     wires = Wires(sems)
     meet(team_peers(*spot))
-    one = TeamGather(wires, left, left_all, spot)
-    two = TeamGather(wires, right, right_all, spot)
-    one.start()
-    one.step(0)
-    one.step(1)
-    two.start()
-    two.step(0)
-    two.step(1)
-    one.finish()
-    two.finish()
-
-
-def middle(
-    result_part, hidden_part, grad_out_part, grad_fc_part,
-    result, hidden, grad_out_w, grad_fc,
-    l1, s1, a1, l2, s2, a2, l3, a3, l4, a4, sems,
+    team = TeamGather(wires, block, whole, spot)
+    team.start()
+    team.step(0)
+    team.step(1)
+    team.finish()
+
+
+def gelu_both(f):
+    square = f * f
+    t = jnp.tanh(0.7978845608028654 * f * (1.0 + 0.044715 * square))
+    half = 0.5 * (1.0 + t)
+    slope = half + f * (0.5 * 0.7978845608028654) * (1.0 - t * t) * (1.0 + 3 * 0.044715 * square)
+    return f * half, slope
+
+
+def chunks(total, step):
+    return [(start, min(step, total - start)) for start in range(0, total, step)]
+
+
+def outer_into(target, left, right):
+    count = left.shape[1] // 256
+
+    @pl.loop(0, count)
+    def _(i):
+        at = pl.ds(pl.multiple_of(i * 256, 256), 256)
+        target[at, :] = outer_sum(left[:, at], right[...]).astype(LOW)
+
+    rest = left.shape[1] - count * 256
+    if rest:
+        target[count * 256 :, :] = outer_sum(left[:, count * 256 :], right[...]).astype(LOW)
+
+
+def feed_forward(
+    hidden_two, grad_all, mat_fc, mat_out, bias_fc,
+    result, hidden, grad_out_w, grad_pre, terms,
+    h2, dy, wf, wo, activ, part_r, part_h, part_o, l1, s1, a1, l2, s2, a2, l3, a3, sems,
 ):
-    spot = here()
+    spot = y, c, z, x = here()
     wires = Wires(sems)
+    load = [
+        wires.near(*both) for both in ((hidden_two, h2), (mat_fc, wf), (grad_all, dy), (mat_out, wo))
+    ]
+    for copy in load:
+        copy.start()
     meet(team_peers(*spot) + grid_peers(*spot))
-    second = TeamScatter(wires, hidden_part, l2, s2, a2, spot)
-    first = TeamScatter(wires, result_part, l1, s1, a1, spot)
-    out = Scatter(wires, grad_out_part, l3, a3, spot)
-    fc = Scatter(wires, grad_fc_part, l4, a4, spot)
+    second = TeamScatter(wires, part_h, l2, s2, a2, spot)
+    first = TeamScatter(wires, part_r, l1, s1, a1, spot)
+    out = Scatter(wires, part_o, l3, a3, spot)
+    load[0].wait()
+    load[1].wait()
+
+    @pl.loop(0, SEQ // QB)
+    def _(i):
+        rows = pl.ds(pl.multiple_of(i * QB, QB), QB)
+        f = dot(h2[rows, :], wf[...]) + bias_fc[...]
+        value, slope = gelu_both(f)
+        activ[rows, :] = value.astype(LOW)
+        grad_pre[rows, :] = slope.astype(LOW)
+
+    load[2].wait()
+    outer_into(part_o, activ, dy)
     out.start()
+    load[3].wait()
+    terms[...] = jnp.zeros_like(terms)
+
+    @pl.loop(0, SEQ // QB)
+    def _(i):
+        rows = pl.ds(pl.multiple_of(i * QB, QB), QB)
+        df = (back_product(dy[rows, :], wo[...]) * grad_pre[rows, :].astype(F32)).astype(LOW)
+        grad_pre[rows, :] = df
+        terms[...] += jnp.sum(df.astype(F32), axis=0, keepdims=True)
+
+    def into(target, make):
+        def half(which):
+            @pl.loop(0, 2)
+            def _(s):
+                rows = half_rows(which, s)
+                target[rows, :] = make(rows).astype(LOW)
+
+        return half
+
+    half = into(part_h, lambda rows: back_product(grad_pre[rows, :], wf[...]))
+    half(1 - c)
     second.start()
+    half(c)
+    out.step(0)
     second.step(0)
     second.step(1)
-    out.step(0)
+    half = into(part_r, lambda rows: dot(activ[rows, :], wo[...]))
+    half(1 - c)
     first.start()
+    half(c)
     out.step(1)
     first.step(0)
     first.step(1)
     second.finish(hidden)
     out.step(2)
-    fc.start()
     first.finish(result)
     out.finish(grad_out_w)
-    fc.step(0)
-    fc.step(1)
-    fc.step(2)
-    fc.finish(grad_fc)
-
-
-def swap_grad_context(parts, whole, sems):
-    spot = y, c, z, x = here()
-    wires = Wires(sems)
-    meet(team_peers(*spot))
-    copies = [
-        TeamSwap(wires, lambda p, q: parts.at[p * XN + q, s], lambda p, q: whole.at[p, s, q], spot)
-        for s in range(2)
-    ]
-    for copy in copies:
-        copy.start()
-    for copy in copies:
-        copy.finish()
-
-
-def last(
-    hidden_part, grad_qkv_part, grad_proj_part, result,
-    hidden, grad_qkv, grad_proj, outputs,
-    l1, s1, a1, l2, a2, l3, a3, pm, pk, px, sems,
+
+
+def backward(
+    hidden_one, hidden_two, grad_pre, mat_qkv, mixed, totals, swap_parts, context, branch, result,
+    hidden, grad_qkv, grad_fc, grad_proj, outputs, terms,
+    ha, hb, wq, part_f, part_h, grads, grad_mixed, acc_k, acc_v,
+    l1, s1, a1, l2, a2, l3, a3, l4, a4, pm, pk, px, sems,
 ):
     spot = y, c, z, x = here()
     wires = Wires(sems)
+    load = [wires.near(*both) for both in ((hidden_two, ha), (grad_pre, hb), (mat_qkv, wq))]
+    again = wires.near(hidden_one, ha)
+    for copy in load:
+        copy.start()
     meet_tokens(team_peers(*spot) + grid_peers(*spot), spot, True)
-    first = TeamScatter(wires, hidden_part, l1, s1, a1, spot)
-    qkv = Scatter(wires, grad_qkv_part, l2, a2, spot)
-    to_mate = wires.far(grad_proj_part.at[1 - c], pm, device(y, 1 - c, z, x))
-    to_side = wires.far(pm.at[1 - x], px, device(y, c, z, 1 - x))
-    proj = Scatter(wires, pk, l3, a3, spot)
+    swaps = [
+        TeamSwap(
+            wires,
+            lambda p, q, s=s: swap_parts.at[p * XN + q, s],
+            lambda p, q, s=s: grads.at[block_rows(p, s, q)],
+            spot,
+        )
+        for s in range(2)
+    ]
+    for copy in swaps:
+        copy.start()
+    fc = Scatter(wires, part_f, l2, a2, spot)
+    first = TeamScatter(wires, part_h, l1, s1, a1, spot)
+    qkv = Scatter(wires, wq, l3, a3, spot)
+    quarter = PROJ // 4
+    to_mate = wires.far(hb, pm, device(y, 1 - c, z, x))
+
+    def side(q):
+        return pl.ds(pl.multiple_of(q * quarter, 16), quarter)
+
+    def term(p, q):
+        at = pl.ds(pl.multiple_of((p * 2 + q) * quarter, quarter), quarter)
+        return outer_sum(context[:, at], branch[...])
+
+    to_side = wires.far(pm.at[side(1 - x)], px, device(y, c, z, 1 - x))
+    proj = Scatter(wires, pk, l4, a4, spot)
     move = Tokens(wires, result, outputs, spot, True)
-    qkv.start()
+    load[0].wait()
+    load[1].wait()
+    outer_into(part_f, ha, hb)
+    fc.start()
+    again.start()
+    for q in range(2):
+        hb[side(q), :D] = term(1 - c, q).astype(LOW)
     to_mate.start()
+    for copy in swaps:
+        copy.finish()
+    for head in range(SLOTS):
+        attend_back(mixed, totals, grads, grad_mixed, acc_k, acc_v, head)
+        if head == 1:
+            fc.step(0)
+            to_mate.wait_recv()
+            pm[side(1 - x), :D] = (pm[side(1 - x), :D].astype(F32) + term(c, 1 - x)).astype(LOW)
+        if head == 5:
+            fc.step(1)
+    load[2].wait()
+
+    def half(which):
+        @pl.loop(0, 2)
+        def _(s):
+            rows = half_rows(which, s)
+            part_h[rows, :] = back_product(grad_mixed[rows, :], wq[...]).astype(LOW)
+
+    half(1 - c)
     first.start()
-    to_mate.wait_recv()
-    pm[1 - x] = (pm[1 - x].astype(F32) + grad_proj_part[c, 1 - x].astype(F32)).astype(LOW)
-    to_side.start()
+    half(c)
+    again.wait()
     first.step(0)
     first.step(1)
+    to_side.start()
+    outer_into(wq, ha, grad_mixed)
+    qkv.start()
+    fc.step(2)
+    terms[...] = jnp.sum(grad_mixed[...].astype(F32), axis=0, keepdims=True)
+    move.start()
+    first.finish(hidden)
+    to_side.wait_recv()
+    pk[...] = (
+        pm[side(x), :D].astype(F32) + term(c, x) + px[:, :D].astype(F32)
+    ).astype(LOW)
+    proj.start()
+    fc.finish(grad_fc)
     qkv.step(0)
     qkv.step(1)
     qkv.step(2)
-    to_side.wait_recv()
-    pk[...] = (pm[x].astype(F32) + grad_proj_part[c, x].astype(F32) + px[...].astype(F32)).astype(LOW)
-    proj.start()
-    move.start()
-    first.finish(hidden)
-    qkv.finish(grad_qkv)
     proj.step(0)
     proj.step(1)
     proj.step(2)
+    qkv.finish(grad_qkv)
     proj.finish(grad_proj)
     move.finish()
     to_mate.wait_send()
@@ -900,69 +1057,66 @@
 QB = 256
 
 
-def attend(mixed, context, totals):
-    for head in range(SLOTS):
-        lanes = slice(head * HEAD, (head + 1) * HEAD)
-        keys = mixed[:, HW + head * HEAD : HW + (head + 1) * HEAD]
-        values = mixed[:, 2 * HW + head * HEAD : 2 * HW + (head + 1) * HEAD]
-        for block in range(SEQ // QB):
-            rows = slice(block * QB, (block + 1) * QB)
-            upto = (block + 1) * QB
-            scores = (
-                lax.dot_general(
-                    mixed[rows, lanes], keys[:upto], (((1,), (1,)), ((), ())), preferred_element_type=F32
-                )
-                * 0.125
+def attend(mixed, context, totals, head):
+    lanes = slice(head * HEAD, (head + 1) * HEAD)
+    keys = mixed[:, HW + head * HEAD : HW + (head + 1) * HEAD]
+    values = mixed[:, 2 * HW + head * HEAD : 2 * HW + (head + 1) * HEAD]
+    for block in range(SEQ // QB):
+        rows = slice(block * QB, (block + 1) * QB)
+        upto = (block + 1) * QB
+        scores = (
+            lax.dot_general(
+                mixed[rows, lanes], keys[:upto], (((1,), (1,)), ((), ())), preferred_element_type=F32
             )
-            row = lax.broadcasted_iota(jnp.int32, (QB, upto), 0) + block * QB
-            col = lax.broadcasted_iota(jnp.int32, (QB, upto), 1)
-            scores = jnp.where(row >= col, scores, -1e30)
-            peak = jnp.max(scores, axis=1, keepdims=True)
-            weights = jnp.exp(scores - peak)
-            total = jnp.sum(weights, axis=1, keepdims=True)
-            prob = (weights * (1.0 / total)).astype(LOW)
-            context[rows, lanes] = jnp.dot(
-                prob, values[:upto], preferred_element_type=F32
-            ).astype(LOW)
-            totals[rows, head : head + 1] = peak + jnp.log(total)
-
-
-def attend_back(mixed, totals, grads, out, acc_k, acc_v):
-    for head in range(SLOTS):
-        lanes = slice(head * HEAD, (head + 1) * HEAD)
-        lanes_k = slice(HW + head * HEAD, HW + (head + 1) * HEAD)
-        lanes_v = slice(2 * HW + head * HEAD, 2 * HW + (head + 1) * HEAD)
-        keys = mixed[:, lanes_k]
-        values = mixed[:, lanes_v]
-        acc_k[...] = jnp.zeros_like(acc_k)
-        acc_v[...] = jnp.zeros_like(acc_v)
-        for block in range(SEQ // QB):
-            rows = slice(block * QB, (block + 1) * QB)
-            upto = (block + 1) * QB
-            queries = mixed[rows, lanes]
-            outer = grads[rows, lanes]
-            scores = (
-                lax.dot_general(
-                    queries, keys[:upto], (((1,), (1,)), ((), ())), preferred_element_type=F32
-                )
-                * 0.125
+            * 0.125
+        )
+        row = lax.broadcasted_iota(jnp.int32, (QB, upto), 0) + block * QB
+        col = lax.broadcasted_iota(jnp.int32, (QB, upto), 1)
+        scores = jnp.where(row >= col, scores, -1e30)
+        peak = jnp.max(scores, axis=1, keepdims=True)
+        weights = jnp.exp(scores - peak)
+        total = jnp.sum(weights, axis=1, keepdims=True)
+        prob = (weights * (1.0 / total)).astype(LOW)
+        found = jnp.dot(prob, values[:upto], preferred_element_type=F32).astype(LOW)
+        context[rows, lanes] = found
+        totals[rows, head : head + 1] = peak + jnp.log(total)
+
+
+def attend_back(mixed, totals, grads, out, acc_k, acc_v, head):
+    lanes = slice(head * HEAD, (head + 1) * HEAD)
+    lanes_k = slice(HW + head * HEAD, HW + (head + 1) * HEAD)
+    lanes_v = slice(2 * HW + head * HEAD, 2 * HW + (head + 1) * HEAD)
+    keys = mixed[:, lanes_k]
+    values = mixed[:, lanes_v]
+    acc_k[...] = jnp.zeros_like(acc_k)
+    acc_v[...] = jnp.zeros_like(acc_v)
+    for block in range(SEQ // QB):
+        rows = slice(block * QB, (block + 1) * QB)
+        upto = (block + 1) * QB
+        queries = mixed[rows, lanes]
+        outer = grads[rows, lanes]
+        scores = (
+            lax.dot_general(
+                queries, keys[:upto], (((1,), (1,)), ((), ())), preferred_element_type=F32
             )
-            row = lax.broadcasted_iota(jnp.int32, (QB, upto), 0) + block * QB
-            col = lax.broadcasted_iota(jnp.int32, (QB, upto), 1)
-            scores = jnp.where(row >= col, scores, -1e30)
-            prob = jnp.exp(scores - totals[rows, head : head + 1])
-            dprob = lax.dot_general(
-                outer, values[:upto], (((1,), (1,)), ((), ())), preferred_element_type=F32
-            )
-            delta = jnp.sum(prob * dprob, axis=1, keepdims=True)
-            ds = (prob * (dprob - delta)).astype(LOW)
-            out[rows, lanes] = (
-                jnp.dot(ds, keys[:upto], preferred_element_type=F32) * 0.125
-            ).astype(LOW)
-            acc_k[:upto] += outer_sum(ds, queries)
-            acc_v[:upto] += outer_sum(prob.astype(LOW), outer)
-        out[:, lanes_k] = (acc_k[...] * 0.125).astype(LOW)
-        out[:, lanes_v] = acc_v[...].astype(LOW)
+            * 0.125
+        )
+        row = lax.broadcasted_iota(jnp.int32, (QB, upto), 0) + block * QB
+        col = lax.broadcasted_iota(jnp.int32, (QB, upto), 1)
+        scores = jnp.where(row >= col, scores, -1e30)
+        prob = jnp.exp(scores - totals[rows, head : head + 1])
+        dprob = lax.dot_general(
+            outer, values[:upto], (((1,), (1,)), ((), ())), preferred_element_type=F32
+        )
+        delta = jnp.sum(prob * dprob, axis=1, keepdims=True)
+        ds = (prob * (dprob - delta)).astype(LOW)
+        out[rows, lanes] = (
+            jnp.dot(ds, keys[:upto], preferred_element_type=F32) * 0.125
+        ).astype(LOW)
+        acc_k[:upto] += outer_sum(ds, queries)
+        acc_v[:upto] += outer_sum(prob.astype(LOW), outer)
+    out[:, lanes_k] = (acc_k[...] * 0.125).astype(LOW)
+    out[:, lanes_v] = acc_v[...].astype(LOW)
 
 
 def plain(body, name, ins, outs, scratch=()):
@@ -1044,11 +1198,14 @@
     units_fc = w_fc.reshape(50, YN, CN, ZN, XN, 200).transpose(2, 4, 0, 1, 3, 5)
     units_fc = pad_to(pad_to(units_fc, 5, PIECE).reshape(4, 50, WIDE), 1, 64)
     small = pad_to(smalls, 0, 2048).reshape(16, 128)
-    tokens, got_qkv, got_fc, smalls_all = call(
+    piece_out = pad_to(w_out.reshape(200, D), 0, PIECE)
+    tokens, got_qkv, got_fc, smalls_all, mat_out = call(
         prologue, "prologue", 1,
-        (inputs.reshape(MICRO, BLK, D), units_qkv, units_fc, small),
-        [((2, BLK, D), LOW), ((4, 64, QW), LOW), ((4, 64, WIDE), LOW), ((YN, ZN, 4, 16, 128), LOW)],
-        [ANY] * 4, [ANY] * 4, [], 3 * TEAM_SWAP_SEMS + TOKENS_SEMS + 8,
+        (inputs.reshape(MICRO, BLK, D), units_qkv, units_fc, small, piece_out),
+        [
+            ((2, BLK, D), LOW), ((4, 64, QW), LOW), ((4, 64, WIDE), LOW), ((YN, ZN, 4, 16, 128), LOW), ((YN, ZN, PIECE, D), LOW),
+        ],
+        [ANY] * 5, [ANY] * 5, [], 3 * TEAM_SWAP_SEMS + TOKENS_SEMS + GATHER_SEMS + 8,
     )
     small = smalls_all.reshape(YN, ZN, CN, XN, 2048)[..., :600].transpose(0, 2, 1, 3, 4)
     small = small.reshape(-1).astype(F32)
@@ -1068,67 +1225,63 @@
     hidden_one = dot(hidden_one.astype(LOW), to_wide).astype(LOW)
     piece_qkv = pad_to(got_qkv[:, :50].reshape(200, QW), 0, PIECE)
     piece_fc = pad_to(got_fc[:, :50].reshape(200, WIDE), 0, PIECE)
-    piece_out = pad_to(w_out.reshape(200, D), 0, PIECE)
     piece_proj = pad_to(w_proj.reshape(50, D), 0, PB)
-    hidden_one, cotangent, mat_qkv, mat_fc, mat_out, mat_proj = call(
-        gather_all, "gather_all", 2,
+    hidden_one, cotangent, mat_qkv, mat_proj = call(
+        gather_first, "gather_first", 2,
         (
             hidden_one.reshape(2, BLK, WIDE), grad_out.reshape(MICRO, BLK, D),
-            piece_qkv, piece_fc, piece_out, piece_proj,
+            piece_qkv, piece_proj,
         ),
         [
             ((2, 2, 2, BLK, WIDE), LOW), ((2, BLK, D), LOW), ((YN, ZN, PIECE, QW), LOW),
-            ((YN, ZN, PIECE, WIDE), LOW), ((YN, ZN, PIECE, D), LOW), ((4, YN, ZN, PB, D), LOW),
+            ((4, YN, ZN, PB, D), LOW),
         ],
-        [ANY] * 6, [ANY] * 6, [], TEAM_GATHER_SEMS + TOKENS_SEMS + 4 * GATHER_SEMS + 6,
+        [ANY] * 4, [ANY] * 4, [], TEAM_GATHER_SEMS + TOKENS_SEMS + 2 * GATHER_SEMS + 6,
     )
     hidden_one = hidden_one.reshape(SEQ, WIDE)
     mat_qkv = mat_qkv.reshape(WIDE, QW)
-    mat_fc = mat_fc.reshape(WIDE, WIDE)
     mat_out = mat_out.reshape(WIDE, D)
     mat_proj = mat_proj.reshape(PROJ, D)
 
-    mixed = (dot(hidden_one, mat_qkv) + bias_qkv).astype(LOW)
-    context, totals = plain(
-        attend, "attend", (mixed,), [((SEQ, HW), LOW), ((SEQ, SLOTS), F32)]
-    )
-    (got,) = call(
-        swap_context, "swap_context", 3, (context.reshape(2, 2, 2, BLK, HW),),
-        [((4, 2, BLK, HW), LOW)], [ANY], [ANY], [], 2 * TEAM_SWAP_SEMS,
-    )
+    mixed, context, totals, got, mat_fc, grad_all = call(
+        attention, "attention", 3,
+        (hidden_one, mat_qkv, bias_qkv.reshape(1, QW), piece_fc, cotangent),
+        [
+            ((SEQ, QW), LOW), ((SEQ, HW), LOW), ((SEQ, SLOTS), F32), ((4, 2, BLK, HW), LOW),
+            ((YN, ZN, PIECE, WIDE), LOW), ((2, 2, 2, BLK, D), LOW),
+        ],
+        [ANY, ANY, VM, ANY, ANY], [VM, VM, VM, VM, ANY, ANY],
+        [pltpu.VMEM((SEQ, WIDE), LOW), pltpu.VMEM((WIDE, QW), LOW)],
+        2 * TEAM_SWAP_SEMS + GATHER_SEMS + TEAM_GATHER_SEMS + 2,
+    )
+    mat_fc = mat_fc.reshape(WIDE, WIDE)
+    grad_all = grad_all.reshape(SEQ, D)
     got = got.reshape(4, 2 * BLK, HW)
     context = jnp.concatenate([got[r] for r in range(4)], axis=1)
     context = back_product(context, to_heads).astype(LOW)
     resid = tokens + dot(context, mat_proj) + bias_proj
     hidden_two, ln2_pull = jax.vjp(layer_norm, resid, gain2, shift2)
     hidden_two = dot(hidden_two.astype(LOW), to_wide).astype(LOW)
-    hidden_two, grad_all = call(
-        gather_two, "gather_two", 4, (hidden_two.reshape(2, BLK, WIDE), cotangent),
-        [((2, 2, 2, BLK, WIDE), LOW), ((2, 2, 2, BLK, D), LOW)],
-        [ANY] * 2, [ANY] * 2, [], 2 * TEAM_GATHER_SEMS,
+    (hidden_two,) = call(
+        gather_second, "gather_second", 4, (hidden_two.reshape(2, BLK, WIDE),),
+        [((2, 2, 2, BLK, WIDE), LOW)], [ANY], [ANY], [], TEAM_GATHER_SEMS,
     )
     hidden_two = hidden_two.reshape(SEQ, WIDE)
-    grad_all = grad_all.reshape(SEQ, D)
-    pre_act = dot(hidden_two, mat_fc) + bias_fc
-    activ, gelu_pull = jax.vjp(gelu_tanh, pre_act)
-    activ = activ.astype(LOW)
-    result_part = dot(activ, mat_out).astype(LOW)
-    (grad_pre,) = gelu_pull(back_product(grad_all, mat_out))
-    grad_pre = grad_pre.astype(LOW)
-    hidden_part = back_product(grad_pre, mat_fc).astype(LOW)
-    grad_out_part = outer_sum(activ, grad_all).astype(LOW)
-    grad_fc_part = outer_sum(hidden_two, grad_pre).astype(LOW)
-    result, grad_hidden_two, grad_out_w, grad_fc = call(
-        middle, "middle", 5,
-        (
-            result_part.reshape(2, 2, 2, BLK, D), hidden_part.reshape(2, 2, 2, BLK, WIDE),
-            grad_out_part.reshape(YN, ZN, PIECE, D), grad_fc_part.reshape(YN, ZN, PIECE, WIDE),
-        ),
-        [((2, BLK, D), F32), ((2, BLK, WIDE), F32), ((PIECE, D), F32), ((PIECE, WIDE), LOW)],
-        [VM] * 4, [VM] * 4,
-        team_scatter_scratch(D) + team_scatter_scratch(WIDE)
-        + scatter_scratch(PIECE, D) + scatter_scratch(PIECE, WIDE),
-        2 * TEAM_SCATTER_SEMS + 2 * SCATTER_SEMS,
+    result, grad_hidden_two, grad_out_w, grad_pre, fc_terms = call(
+        feed_forward, "feed_forward", 5,
+        (hidden_two, grad_all, mat_fc, mat_out, bias_fc.reshape(1, WIDE)),
+        [
+            ((2, BLK, D), F32), ((2, BLK, WIDE), F32), ((PIECE, D), F32), ((SEQ, WIDE), LOW),
+            ((1, WIDE), F32),
+        ],
+        [ANY] * 4 + [VM], [VM] * 5,
+        [
+            pltpu.VMEM((SEQ, WIDE), LOW), pltpu.VMEM((SEQ, D), LOW), pltpu.VMEM((WIDE, WIDE), LOW),
+            pltpu.VMEM((WIDE, D), LOW), pltpu.VMEM((SEQ, WIDE), LOW), pltpu.VMEM((SEQ, D), LOW),
+            pltpu.VMEM((SEQ, WIDE), LOW), pltpu.VMEM((WIDE, D), LOW),
+        ]
+        + team_scatter_scratch(D) + team_scatter_scratch(WIDE) + scatter_scratch(PIECE, D),
+        2 * TEAM_SCATTER_SEMS + SCATTER_SEMS + 4,
     )
     result = (resid + result.reshape(2 * BLK, D) + bias_out).astype(LOW)
     grad_out_w = grad_out_w[:200].reshape(-1)
@@ -1143,43 +1296,40 @@
     grad_context = jnp.stack(
         [grad_context[:, r * HW : (r + 1) * HW] for r in range(4)]
     ).reshape(4, 2, BLK, HW)
-    (grad_context,) = call(
-        swap_grad_context, "swap_grad_context", 6, (grad_context,),
-        [((2, 2, 2, BLK, HW), LOW)], [ANY], [ANY], [], 2 * TEAM_SWAP_SEMS,
-    )
-    (grad_mixed,) = plain(
-        attend_back, "attend_back", (mixed, totals, grad_context.reshape(SEQ, HW)),
-        [((SEQ, QW), LOW)], [pltpu.VMEM((SEQ, HEAD), F32)] * 2,
-    )
-    hidden_part = back_product(grad_mixed, mat_qkv).astype(LOW)
-    grad_qkv_part = outer_sum(hidden_one, grad_mixed).astype(LOW)
-    grad_proj_part = outer_sum(context, grad_branch).astype(LOW)
-    grad_hidden_one, grad_qkv, grad_proj, outputs = call(
-        last, "last", 7,
+    grad_hidden_one, grad_qkv, grad_fc, grad_proj, outputs, terms = call(
+        backward, "backward", 7,
         (
-            hidden_part.reshape(2, 2, 2, BLK, WIDE), grad_qkv_part.reshape(YN, ZN, PIECE, QW),
-            grad_proj_part.reshape(CN, XN, YN, ZN, PB, D), result.reshape(2, BLK, D),
+            hidden_one, hidden_two, grad_pre, mat_qkv, mixed, totals, grad_context, context,
+            grad_branch, result.reshape(2, BLK, D),
         ),
-        [((2, BLK, WIDE), F32), ((PIECE, QW), LOW), ((PB, D), F32), ((2, BLK, D), LOW)],
-        [VM, VM, VM, ANY], [VM, VM, VM, ANY],
-        team_scatter_scratch(WIDE) + scatter_scratch(PIECE, QW) + scatter_scratch(PB, D)
+        [
+            ((2, BLK, WIDE), F32), ((PIECE, QW), LOW), ((PIECE, WIDE), LOW), ((PB, D), F32),
+            ((2, BLK, D), LOW), ((1, QW), F32),
+        ],
+        [ANY] * 4 + [VM, VM, ANY, VM, VM, ANY], [VM, VM, VM, VM, ANY, VM],
+        [
+            pltpu.VMEM((SEQ, WIDE), LOW), pltpu.VMEM((SEQ, WIDE), LOW), pltpu.VMEM((WIDE, QW), LOW),
+            pltpu.VMEM((WIDE, WIDE), LOW), pltpu.VMEM((SEQ, WIDE), LOW), pltpu.VMEM((SEQ, HW), LOW), pltpu.VMEM((SEQ, QW), LOW),
+            pltpu.VMEM((SEQ, HEAD), F32), pltpu.VMEM((SEQ, HEAD), F32),
+        ]
+        + team_scatter_scratch(WIDE) + scatter_scratch(PIECE, WIDE) + scatter_scratch(PIECE, QW)
+        + scatter_scratch(PB, D)
         + [
-            pltpu.VMEM((XN, YN, ZN, PB, D), LOW),
-            pltpu.VMEM((YN, ZN, PB, D), LOW),
-            pltpu.VMEM((YN, ZN, PB, D), LOW),
+            pltpu.VMEM((PROJ // 2, WIDE), LOW), pltpu.VMEM((PROJ // 4, D), LOW),
+            pltpu.VMEM((PROJ // 4, WIDE), LOW),
         ],
-        TEAM_SCATTER_SEMS + 2 * SCATTER_SEMS + TOKENS_SEMS + 4,
+        TEAM_SCATTER_SEMS + 3 * SCATTER_SEMS + TOKENS_SEMS + 2 * TEAM_SWAP_SEMS + 8,
     )
     grad_hidden_one = back_product(grad_hidden_one.reshape(2 * BLK, WIDE).astype(LOW), to_wide)
     grad_ln_one, grad_gain_one, grad_shift_one = ln1_pull(grad_hidden_one)
     grad_in = (grad_resid + grad_ln_one).astype(LOW)
     grad_proj = grad_proj[:50].reshape(-1)
 
-    terms = ones_row(grad_mixed).reshape(3, HW)
+    terms = terms.reshape(3, HW)
     mine = (jnp.arange(4) == rank).astype(F32)[:, None, None]
     grad_bq = head_join(mine * terms[0][None, None])[0]
     grad_bv = head_join(mine * terms[2][None, None])[0]
-    fc_terms = ones_row(grad_pre).reshape(YN, 1, ZN, 1, PIECE)[..., :200]
+    fc_terms = fc_terms.reshape(YN, 1, ZN, 1, PIECE)[..., :200]
     spot = (jnp.arange(CN) == c)[None, :, None, None, None] & (jnp.arange(XN) == x)[
         None, None, None, :, None
     ]

time: 926 us -> 700 us (0.76)
  matrix products: 135 us -> 29.4 us
  local copies, waits for them, and re-layouts: 111 us -> 52.9 us
  Pallas kernels: 650 us -> 592 us
    pallas_call x2 -> x0, Pallas kernels: 43.6 us -> none  [plain(): pl.pallas_call(body, out_shape=[jax.ShapeDtypeStruct(s, d) for s, d in ou...]
    dot_general x4 -> x0, matrix products: 37.7 us -> none  [outer_sum(): lax.dot_general(left, right, (((0,), (0,)), ((), ())), preferred_element_...]
    convert_element_type x8 -> x0, local copies, waits for them, and re-layouts: 37.3 us -> none  [the longest x1 9.58 us: fast_shards(): grad_proj_part = outer_sum(context, grad_branch).astype(LOW)]
    dot_general x7 -> x4, matrix products: 56.1 us -> 20 us  [dot(): return jnp.dot(left, right, preferred_element_type=F32)]
    dot_general x6 -> x3, matrix products: 41.4 us -> 9.43 us  [back_product(): lax.dot_general(grad, weight, (((1,), (1,)), ((), ())), preferred_element...]
    pallas_call x8 -> x7, Pallas kernels: 606 us -> 592 us  [call(): pl.pallas_call(body, out_shape=[jax.ShapeDtypeStruct(s, d) for s, d in ou...]
where the time goes in v3:
time: 700 us; the launch traced here: 693 us
  Pallas kernels  592 us (85%)
  local copies, waits for them, and re-layouts  52.9 us (8%)
  matrix products  29.4 us (4%)
  other arithmetic  16.7 us (2%)
    pallas_call x7, Pallas kernels, call(): pl.pallas_call(body, out_shape=[jax.ShapeDtypeStruct(s, d) for s, d in ou...  592 us
    dot_general x4, matrix products, dot(): return jnp.dot(left, right, preferred_element_type=F32)  20 us

profile of v3, /device:TPU:0, one launch (start us, length us, event | category | flops | bytes accessed | tf_op | source)
XLA Modules:
  0.0 693.2 jit_solution(3215474741867892280)
XLA Ops:
  0.6 1.9 reshape.450
  2.6 0.7 fusion.35
  4.1 0.5 copy.106
  4.7 0.7 reshape.495
  5.4 0.9 pad.102.units_qkv
  6.3 2.4 reshape.452
  9.5 1.1 reshape.496
  10.5 1.0 pad.104.units_fc
  11.5 0.5 reshape.455
  12.1 0.9 pad.106.piece_out
  13.0 1.2 copy.83
  14.2 0.6 pad_bitcast_fusion.9.small
  14.8 89.6 %prologue.1 = (bf16[2,128,1600]{2,1,0:T(8,128)(2,1)}, bf16[4,64,1344]{2,1,0:T(8,128)(2,1)}, bf16[4,64,1664]{2,1,0:T(8,128)(2,1)}, bf16[2,4,4,16,128]{4,3,2,1,0:T(8,128)(2,1)}, bf16[2,4,208,1600]{3,2,1,0:T(8,128)(2,1)}) custom-call(bf16[2,128,1600]{2,1,0:T(8,128)(2,1)} %bitcast.224, bf16[4,64,1344]{2,1,0:T(8,128)(2,1)} %pad.102.units_qkv, ...), custom_call_target="tpu_custom_call" | custom-call | tf_op jit(solution)/shard_map/prologue/pallas_call | solution.py:393
  104.4 1.0 reshape.456
  106.1 0.7 reshape_reshape.6.bias_qkv
  106.8 1.4 convert_reduce_fusion.1
  109.0 3.2 fusion.13
  112.5 0.9 pad.107.piece_qkv
  113.4 1.2 copy.91
  114.8 0.7 pad.108.piece_proj
  115.5 82.9 %gather_first.1 = (bf16[2,2,2,128,1664]{4,3,2,1,0:T(8,128)(2,1)}, bf16[2,128,1600]{2,1,0:T(8,128)(2,1)}, bf16[2,4,208,1344]{3,2,1,0:T(8,128)(2,1)}, bf16[4,2,4,64,1600]{4,3,2,1,0:T(8,128)(2,1)}) custom-call(bf16[2,128,1664]{2,1,0:T(8,128)(2,1)} %bitcast.239, bf16[2,128,1600]{2,1,0:T(8,128)(2,1)} %bitcast.225, bf16[208,1344]{1,0:T(8,128)(2,1)} %pad.107.piece_qkv, ...), custom_call_target="tpu_custom_call" | custom-call | tf_op jit(solution)/shard_map/gather_first/pallas_call | solution.py:393
  198.7 0.9 pad.115.piece_fc
  199.6 71.7 %attention.1 = (bf16[1024,1344]{1,0:T(8,128)(2,1)}, bf16[1024,448]{1,0:T(8,128)(2,1)}, f32[1024,7]{1,0:T(8,128)}, bf16[4,2,128,448]{3,2,1,0:T(8,128)(2,1)}, bf16...) custom-call(bf16[1024,1664]{1,0:T(8,128)(2,1)} %bitcast.218, bf16[1664,1344]{1,0:T(8,128)(2,1)} %bitcast.216, ...), custom_call_target="tpu_custom_call" | custom-call | tf_op jit(solution)/shard_map/attention/pallas_call | solution.py:393
  271.3 1.3 fusion.32
  272.6 0.5 concatenate.37
  273.2 3.1 fusion.15.context
  276.3 5.5 fusion.43
  282.1 3.4 fusion.14
  285.5 29.5 %gather_second.1 = bf16[2,2,2,128,1664]{4,3,2,1,0:T(8,128)(2,1)} custom-call(bf16[2,128,1664]{2,1,0:T(8,128)(2,1)} %bitcast.240), custom_call_target="tpu_custom_call" | custom-call | tf_op jit(solution)/shard_map/gather_second/pallas_call | solution.py:393
  315.3 0.7 reshape_reshape.7.bias_fc
  316.0 100.8 %feed_forward.1 = (f32[2,128,1600]{2,1,0:T(8,128)}, f32[2,128,1664]{2,1,0:T(8,128)}, f32[208,1600]{1,0:T(8,128)}, bf16[1024,1664]{1,0:T(8,128)(2,1)}, f32[1,1664]{1,0:T(1,128)}) custom-call(bf16[1024,1664]{1,0:T(8,128)(2,1)} %bitcast.213, bf16[1024,1600]{1,0:T(8,128)(2,1)} %bitcast.222, bf16[1664,1664]{1,0:T(8,128)(2,1)} %bitcast.221, ...), custom_call_target="tpu_custom_call" | custom-call | tf_op jit(solution)/shard_map/feed_forward/pallas_call | solution.py:393
  416.8 1.5 convert_element_type.146
  418.3 3.2 fusion.44
  421.5 1.8 copy.93
  423.3 2.1 multiply_reduce_fusion
  425.7 1.5 fusion.31
  427.6 0.8 copy-done.1
  428.4 8.0 %fusion.16 = bf16[256,1792]{1,0:T(8,128)(2,1)S(1)} fusion(s32[1792]{0:T(1024)S(1)} %copy-done.25, bf16[256,1600]{1,0:T(8,128)(2,1)S(1)} %get-tuple-element.103.branch, bf16[2048,1600]{1,0:T(8,128)(2,1)} %bitcast.266), kind=kOutput, calls=%fused_computation.20 | convolution fusion | flops 3561422848 | bytes 8297472 | tf_op jit(solution)/shard_map/dot_general | solution.py:1182
  436.7 1.1 pad_maximum_fusion.swap_parts
  437.8 182.4 %backward.1 = (f32[2,128,1664]{2,1,0:T(8,128)}, bf16[208,1344]{1,0:T(8,128)(2,1)}, bf16[208,1664]{1,0:T(8,128)(2,1)}, f32[64,1600]{1,0:T(8,128)}, bf16[2,128,1600]{2,1,0:T(8,128)(2,1)}, /*index=5*/f32[1,1344]{1,0:T(1,128)}) custom-call(bf16[1024,1664]{1,0:T(8,128)(2,1)} %bitcast.219, bf16[1024,1664]{1,0:T(8,128)(2,1)} %bitcast.214, ...), custom_call_target="tpu_custom_call" | custom-call | tf_op jit(solution)/shard_map/backward/pallas_call | solution.py:393
  620.3 0.7 fusion.42
  622.4 1.5 convert_element_type.152
  623.9 3.2 fusion.45
  627.1 2.0 copy.94
  629.5 0.8 multiply_reduce_fusion.1
  630.6 0.7 copy.97
  631.3 3.2 add_convert_fusion
  634.7 1.0 pad.118.units_fc
  635.9 0.9 pad.117.units_qkv
  636.8 35.0 %epilogue.1 = (bf16[2,128,1600]{2,1,0:T(8,128)(2,1)}, bf16[4,64,1344]{2,1,0:T(8,128)(2,1)}, bf16[4,64,1664]{2,1,0:T(8,128)(2,1)}, f32[8,128]{1,0:T(8,128)}) custom-call(bf16[2,128,1600]{2,1,0:T(8,128)(2,1)} %bitcast.223, bf16[4,64,1344]{2,1,0:T(8,128)(2,1)} %pad.117.units_qkv, bf16[4,64,1664]{2,1,0:T(8,128)(2,1)} %pad.118.units_fc, ...), custom_call_target="tpu_custom_call" | custom-call | tf_op jit(solution)/shard_map/epilogue/pallas_call | solution.py:393
  671.9 1.1 slice.371
  673.2 0.8 reshape.480
  674.0 0.8 fusion.34
  676.2 1.8 reshape.491
  678.1 1.4 reshape.497
  679.9 0.9 copy.101
  680.8 3.7 reshape.493
  684.6 1.6 copy.103
  686.2 0.6 slice.398
  686.9 0.6 slice.397
  687.5 1.2 copy.102
  688.7 0.9 reshape.481
  689.6 1.4 slice.396
  691.0 1.7 reshape.485
  (180 shorter events, 9.5 us)
Async XLA Ops:
  4.7 1.7 copy-start.15
  9.5 2.1 copy-start.14
  11.5 1.4 copy-start.10
  12.1 2.2 copy-start.23
  104.4 3.8 copy-start
  106.8 2.2 copy-start.24
  109.0 3.2 copy-start.17
  112.2 1.2 copy-start.11
  112.5 2.1 copy-start.20
  114.6 83.8 %copy-start.12 = (bf16[4,64,1664]{2,1,0:T(8,128)(2,1)S(1)}, bf16[4,64,1664]{2,1,0:T(8,128)(2,1)}, u32[]{:S(2)}) copy-start(bf16[4,64,1664]{2,1,0:T(8,128)(2,1)} %get-tuple-element.42) | copy-start | bytes 2555908
  271.3 1.9 copy-start.25
  276.3 5.5 copy-start.7
  281.8 3.8 copy-start.2
  423.3 2.1 copy-start.3
  423.3 2.5 copy-start.6
  425.7 1.5 copy-start.4
  427.3 1.2 copy-start.1
  428.4 8.0 %copy-start.5 = (bf16[256,1600]{1,0:T(8,128)(2,1)}, bf16[256,1600]{1,0:T(8,128)(2,1)S(1)}, u32[]{:S(2)}) copy-start(bf16[256,1600]{1,0:T(8,128)(2,1)S(1)} %get-tuple-element.103.branch) | copy-start | bytes 2457604
  437.8 183.7 %copy-start.21 = (f32[1,1664]{1,0:T(1,128)S(1)}, f32[1,1664]{1,0:T(1,128)}, u32[]{:S(2)}) copy-start(f32[1,1664]{1,0:T(1,128)} %get-tuple-element.59) | copy-start | bytes 19972
  631.3 3.2 copy-start.16
  634.5 1.2 copy-start.18
  676.2 1.9 copy-start.13
  680.8 3.7 copy-start.8
  684.6 1.6 copy-start.22
  684.6 2.8 copy-start.9
  684.6 4.0 copy-start.19

commit v4 on v3

--- a/solution.py
+++ b/solution.py
@@ -352,6 +352,7 @@
 
     def one(self):
         self.used += 1
+        assert self.used <= self.sems.shape[0]
         return self.sems.at[self.used - 1]
 
     def far(self, source, target, where):
@@ -471,40 +472,104 @@
         self.y, self.z, self.size = y, z, landed.shape[1]
         self.parts, self.landed, self.arrived = parts, landed, arrived
         across = device(1 - y, c, z, x)
-        self.order = [lax.rem(z + k, ZN) for k in (1, 2, 3, 0)]
-        self.over = [
-            wires.far(parts.at[self.rows(1 - y, o)], landed.at[o], across) for o in self.order
-        ]
-        self.along = [
-            wires.far(landed.at[o], arrived.at[k], device(y, c, o, x))
-            for k, o in enumerate(self.order[:3])
-        ]
+        up = device(y, c, lax.min(z + 1, ZN - 1), x)
+        down = device(y, c, lax.max(z - 1, 0), x)
+        base = wires.used
+        wires.used += 2 * ZN
+        self.over = lambda o: pltpu.make_async_remote_copy(
+            src_ref=parts.at[self.rows(1 - y, o)],
+            dst_ref=landed.at[o],
+            send_sem=wires.sems.at[base + o],
+            recv_sem=wires.sems.at[base + ZN + o],
+            device_id=across,
+            device_id_type=pl.DeviceIdType.MESH,
+        )
+        self.ups, self.downs = [], []
+        for turn in range(1, ZN):
+            high = lax.min(z + ZN - turn, ZN - 1)
+            low = lax.max(z - ZN + turn, 0)
+            slot = self.slot(0, turn, z + 1)
+            self.ups.append((high, wires.far(landed.at[high], arrived.at[slot], up)))
+            slot = self.slot(1, turn, z - 1)
+            self.downs.append((low, wires.far(landed.at[low], arrived.at[slot], down)))
 
     def rows(self, y, z):
         return pl.ds(pl.multiple_of((y * ZN + z) * self.size, 16), self.size)
 
+    @staticmethod
+    def slot(side, turn, z):
+        return jnp.where(z == 1 + side, turn - 1, turn + 1)
+
     def start(self):
-        for copy in self.over:
-            copy.start()
-
-    def step(self, k):
-        o = self.order[k]
-        self.over[k].wait_recv()
-        self.landed[o] = (self.landed[o].astype(F32) + self.parts[self.rows(self.y, o), :].astype(F32)).astype(LOW)
-        self.along[k].start()
+        z = self.z
+        first = jnp.where(z < 2, 3, 0)
+        second = jnp.where(z < 2, 2, 1)
+        third = jnp.where(z == 0, 1, jnp.where(z == 1, 0, jnp.where(z == 2, 3, 2)))
+        for o in (first, second, third, z):
+            self.over(o).start()
+
+    def goes_up(self, turn):
+        return (self.z <= turn - 1) & (self.z < ZN - 1)
+
+    def goes_down(self, turn):
+        return (self.z >= ZN - turn) & (self.z > 0)
+
+    def add(self, o, side, turn, more):
+        total = self.landed[o].astype(F32) + self.parts[self.rows(self.y, o), :].astype(F32)
+        if more:
+            total = total + self.arrived[self.slot(side, turn - 1, self.z)].astype(F32)
+        self.landed[o] = total.astype(LOW)
+
+    def step(self, turn):
+        for side, goes, jobs, inner in (
+            (0, self.goes_up, self.ups, self.z > 0),
+            (1, self.goes_down, self.downs, self.z < ZN - 1),
+        ):
+            o, copy = jobs[turn - 1]
+
+            @pl.when(goes(turn))
+            def _(side=side, jobs=jobs, inner=inner, o=o, copy=copy):
+                self.over(o).wait_recv()
+                if turn == 1:
+                    self.add(o, side, turn, False)
+                else:
+
+                    @pl.when(inner)
+                    def _():
+                        jobs[turn - 2][1].wait_recv()
+                        self.add(o, side, turn, True)
+
+                    @pl.when(jnp.logical_not(inner))
+                    def _():
+                        self.add(o, side, turn, False)
+
+                copy.start()
 
     def finish(self, total):
-        self.over[3].wait_recv()
-        summed = self.landed[self.z].astype(F32) + self.parts[self.rows(self.y, self.z), :].astype(F32)
-        for k in range(3):
-            self.along[k].wait_recv()
-            summed = summed + self.arrived[k].astype(F32)
-        total[...] = summed.astype(total.dtype)
-        for copy in self.over + self.along:
-            copy.wait_send()
-
-
-SCATTER_SEMS = 2 * 7
+        self.over(self.z).wait_recv()
+        total[...] = (
+            self.landed[self.z].astype(F32) + self.parts[self.rows(self.y, self.z), :].astype(F32)
+        ).astype(total.dtype)
+        last = ZN - 1
+
+        @pl.when(self.z > 0)
+        def _():
+            self.ups[last - 1][1].wait_recv()
+            total[...] = (total[...].astype(F32) + self.arrived[self.slot(0, last, self.z)].astype(F32)).astype(total.dtype)
+
+        @pl.when(self.z < ZN - 1)
+        def _():
+            self.downs[last - 1][1].wait_recv()
+            total[...] = (total[...].astype(F32) + self.arrived[self.slot(1, last, self.z)].astype(F32)).astype(total.dtype)
+
+        for o in range(ZN):
+            self.over(o).wait_send()
+        for turn in range(1, ZN):
+            pl.when(self.goes_up(turn))(self.ups[turn - 1][1].wait_send)
+            pl.when(self.goes_down(turn))(self.downs[turn - 1][1].wait_send)
+
+
+SCATTER_SEMS = 2 * (ZN + 6)
 
 
 class TeamGather:
@@ -614,7 +679,7 @@
 
 
 def scatter_scratch(rows, width):
-    return [pltpu.VMEM((ZN, rows, width), LOW), pltpu.VMEM((ZN - 1, rows, width), LOW)]
+    return [pltpu.VMEM((ZN, rows, width), LOW), pltpu.VMEM((5, rows, width), LOW)]
 
 
 class Tokens:
@@ -676,8 +741,8 @@
 
 
 def prologue(
-    inputs, units_qkv, units_fc, small, piece_out,
-    tokens, got_qkv, got_fc, smalls, all_out, sems,
+    inputs, units_qkv, units_fc, small, piece_out, piece_proj,
+    tokens, got_qkv, got_fc, smalls, all_out, all_proj, sems,
 ):
     spot = y, c, z, x = here()
     wires = Wires(sems)
@@ -693,6 +758,13 @@
     )
     move = Tokens(wires, inputs, tokens, spot, False)
     out = Gather(wires, piece_out, all_out, spot)
+    rank = c * XN + x
+    proj = Gather(wires, piece_proj, all_proj.at[rank], spot)
+    side = wires.far(all_proj.at[rank], all_proj.at[rank], device(y, c, z, 1 - x))
+    mate = device(y, 1 - c, z, x)
+    relay = [
+        wires.far(all_proj.at[r], all_proj.at[r], mate) for r in (rank, c * XN + 1 - x)
+    ]
     column = [
         wires.far(smalls.at[y, z], smalls.at[y, z], device(y, c, lax.rem(z + k, ZN), x))
         for k in range(1, ZN)
@@ -705,75 +777,52 @@
     first.finish()
     for copy in column:
         copy.start()
+    proj.start()
     out.start()
     for copy in column:
         copy.wait()
     over.start()
+    proj.step(1)
     over.wait()
+    proj.step(2)
+    proj.step(3)
     out.step(1)
+    proj.finish()
+    side.start()
+    relay[0].start()
     move.finish()
     qkv.finish()
     fc.finish()
     out.step(2)
     out.step(3)
+    side.wait_recv()
+    relay[1].start()
     out.finish()
-
-
-def gather_first(
-    hidden, grads, piece_qkv, piece_proj, hidden_all, cotangent, all_qkv, all_proj, sems,
+    side.wait_send()
+    for copy in relay:
+        copy.wait()
+
+
+def forward(
+    hidden, grads, piece_qkv, piece_fc, mat_proj, to_proj, to_wide,
+    tokens, bias_qkv, bias_proj, gain2, shift2,
+    hidden_all, cotangent, grad_all, all_qkv, all_fc, second_all, mixed, totals, context_out, resid,
+    hidden_in, mat_in, proj_in, to_proj_in, to_wide_in, context, got, second, sems,
 ):
     spot = y, c, z, x = here()
     wires = Wires(sems)
-    rank = c * XN + x
+    load = [
+        wires.near(*both)
+        for both in ((mat_proj, proj_in), (to_proj, to_proj_in), (to_wide, to_wide_in))
+    ]
+    load_hidden, load_qkv = wires.near(hidden_all, hidden_in), wires.near(all_qkv, mat_in)
     meet_tokens(team_peers(*spot) + grid_peers(*spot), spot, False)
     team = TeamGather(wires, hidden, hidden_all, spot)
+    qkv = Gather(wires, piece_qkv, all_qkv, spot)
+    fc = Gather(wires, piece_fc, all_fc, spot)
     bring = Tokens(wires, grads, cotangent, spot, False)
-    qkv = Gather(wires, piece_qkv, all_qkv, spot)
-    proj = Gather(wires, piece_proj, all_proj.at[rank], spot)
-    side = wires.far(all_proj.at[rank], all_proj.at[rank], device(y, c, z, 1 - x))
-    mate = device(y, 1 - c, z, x)
-    relay = [
-        wires.far(all_proj.at[r], all_proj.at[r], mate) for r in (rank, c * XN + 1 - x)
-    ]
-    proj.start()
-    qkv.start()
-    team.start()
-    proj.step(1)
-    proj.step(2)
-    proj.step(3)
-    qkv.step(1)
-    team.step(0)
-    team.step(1)
-    proj.finish()
-    side.start()
-    relay[0].start()
-    bring.start()
-    qkv.step(2)
-    qkv.step(3)
-    side.wait_recv()
-    relay[1].start()
-    qkv.finish()
-    team.finish()
-    bring.finish()
-    side.wait_send()
-    for copy in relay:
-        copy.wait()
-
-
-def attention(
-    hidden, mat_qkv, bias_qkv, piece_fc, cotangent, mixed, context, totals, got, all_fc, grad_all,
-    hidden_in, mat_in, sems,
-):
-    spot = y, c, z, x = here()
-    wires = Wires(sems)
-    load = [wires.near(mat_qkv, mat_in), wires.near(hidden, hidden_in)]
-    for copy in load:
-        copy.start()
-    meet(team_peers(*spot) + grid_peers(*spot))
-    fc = Gather(wires, piece_fc, all_fc, spot)
-    fc.start()
-    team = TeamGather(wires, cotangent, grad_all, spot)
-    team.start()
+    team_two = TeamGather(wires, cotangent, grad_all, spot)
+    team_three = TeamGather(wires, second, second_all, spot)
     swaps = [
         TeamSwap(
             wires,
@@ -783,40 +832,63 @@
         )
         for s in range(2)
     ]
+    qkv.start()
+    team.start()
+    qkv.step(1)
+    team.step(0)
+    team.step(1)
+    qkv.step(2)
+    qkv.step(3)
+    fc.start()
     for copy in load:
-        copy.wait()
+        copy.start()
+    team.finish()
+    load_hidden.start()
+    qkv.finish()
+    load_qkv.start()
+    bring.start()
+    load_hidden.wait()
+    load_qkv.wait()
 
     @pl.loop(0, SEQ // QB)
     def _(i):
         rows = pl.ds(pl.multiple_of(i * QB, QB), QB)
-        mixed[rows, :] = (dot(hidden_in[rows, :], mat_in[...]) + bias_qkv[...]).astype(LOW)
-
+        flat = hidden_in[i // 2, i % 2].reshape(QB, WIDE)
+        mixed[rows, :] = (dot(flat, mat_in[...].reshape(WIDE, QW)) + bias_qkv[...]).astype(LOW)
+
+    fc.step(1)
     for head in range(SLOTS):
         attend(mixed, context, totals, head)
         if head == 2:
-            fc.step(1)
-        if head == 4:
-            team.step(0)
-            team.step(1)
+            fc.step(2)
+    bring.finish()
     for copy in swaps:
         copy.start()
-    fc.step(2)
+    team_two.start()
+    fc.step(3)
+    for copy in load:
+        copy.wait()
     for copy in swaps:
         copy.finish()
-    fc.step(3)
-    team.finish()
+    placed = 0.0
+    for r in range(4):
+        placed = placed + dot(
+            got[r].reshape(2 * BLK, HW), to_proj_in[r * HW : (r + 1) * HW, :]
+        )
+    placed = placed.astype(LOW)
+    context_out[...] = placed
+    found = tokens[...].astype(F32) + dot(placed, proj_in[...]) + bias_proj[...]
+    resid[...] = found
+    normed = layer_norm(found, gain2[...], shift2[...]).astype(LOW)
+    second[...] = dot(normed, to_wide_in[...]).astype(LOW).reshape(2, BLK, WIDE)
+    team_three.start()
+    team_two.step(0)
+    team_two.step(1)
+    team_three.step(0)
+    team_three.step(1)
+    team_two.finish()
+    team_three.finish()
     fc.finish()
-
-
-def gather_second(block, whole, sems):
-    spot = here()
-    wires = Wires(sems)
-    meet(team_peers(*spot))
-    team = TeamGather(wires, block, whole, spot)
-    team.start()
-    team.step(0)
-    team.step(1)
-    team.finish()
 
 
 def gelu_both(f):
@@ -897,31 +969,31 @@
     half(1 - c)
     second.start()
     half(c)
-    out.step(0)
+    out.step(1)
     second.step(0)
     second.step(1)
     half = into(part_r, lambda rows: dot(activ[rows, :], wo[...]))
     half(1 - c)
     first.start()
     half(c)
-    out.step(1)
+    out.step(2)
     first.step(0)
     first.step(1)
     second.finish(hidden)
-    out.step(2)
+    out.step(3)
     first.finish(result)
     out.finish(grad_out_w)
 
 
 def backward(
-    hidden_one, hidden_two, grad_pre, mat_qkv, mixed, totals, swap_parts, context, branch, result,
+    hidden_one, hidden_two, grad_pre, mat_qkv, mixed_all, totals, swap_parts, context, branch, result,
     hidden, grad_qkv, grad_fc, grad_proj, outputs, terms,
-    ha, hb, wq, part_f, part_h, grads, grad_mixed, acc_k, acc_v,
+    ha, hb, wq, part_f, part_h, grads, mixed, acc_k, acc_v,
     l1, s1, a1, l2, a2, l3, a3, l4, a4, pm, pk, px, sems,
 ):
     spot = y, c, z, x = here()
     wires = Wires(sems)
-    load = [wires.near(*both) for both in ((hidden_two, ha), (grad_pre, hb), (mat_qkv, wq))]
+    load = [wires.near(*both) for both in ((hidden_two, ha), (grad_pre, hb), (mixed_all, mixed), (mat_qkv, wq))]
     again = wires.near(hidden_one, ha)
     for copy in load:
         copy.start()
@@ -961,23 +1033,24 @@
     for q in range(2):
         hb[side(q), :D] = term(1 - c, q).astype(LOW)
     to_mate.start()
+    load[2].wait()
     for copy in swaps:
         copy.finish()
     for head in range(SLOTS):
-        attend_back(mixed, totals, grads, grad_mixed, acc_k, acc_v, head)
+        attend_back(mixed, totals, grads, acc_k, acc_v, head)
         if head == 1:
-            fc.step(0)
+            fc.step(1)
             to_mate.wait_recv()
             pm[side(1 - x), :D] = (pm[side(1 - x), :D].astype(F32) + term(c, 1 - x)).astype(LOW)
         if head == 5:
-            fc.step(1)
-    load[2].wait()
+            fc.step(2)
+    load[3].wait()
 
     def half(which):
         @pl.loop(0, 2)
         def _(s):
             rows = half_rows(which, s)
-            part_h[rows, :] = back_product(grad_mixed[rows, :], wq[...]).astype(LOW)
+            part_h[rows, :] = back_product(mixed[rows, :], wq[...]).astype(LOW)
 
     half(1 - c)
     first.start()
@@ -986,10 +1059,10 @@
     first.step(0)
     first.step(1)
     to_side.start()
-    outer_into(wq, ha, grad_mixed)
+    outer_into(wq, ha, mixed)
     qkv.start()
-    fc.step(2)
-    terms[...] = jnp.sum(grad_mixed[...].astype(F32), axis=0, keepdims=True)
+    fc.step(3)
+    terms[...] = jnp.sum(mixed[...].astype(F32), axis=0, keepdims=True)
     move.start()
     first.finish(hidden)
     to_side.wait_recv()
@@ -998,12 +1071,12 @@
     ).astype(LOW)
     proj.start()
     fc.finish(grad_fc)
-    qkv.step(0)
     qkv.step(1)
     qkv.step(2)
-    proj.step(0)
+    qkv.step(3)
     proj.step(1)
     proj.step(2)
+    proj.step(3)
     qkv.finish(grad_qkv)
     proj.finish(grad_proj)
     move.finish()
@@ -1082,7 +1155,7 @@
         totals[rows, head : head + 1] = peak + jnp.log(total)
 
 
-def attend_back(mixed, totals, grads, out, acc_k, acc_v, head):
+def attend_back(mixed, totals, grads, acc_k, acc_v, head):
     lanes = slice(head * HEAD, (head + 1) * HEAD)
     lanes_k = slice(HW + head * HEAD, HW + (head + 1) * HEAD)
     lanes_v = slice(2 * HW + head * HEAD, 2 * HW + (head + 1) * HEAD)
@@ -1110,13 +1183,13 @@
         )
         delta = jnp.sum(prob * dprob, axis=1, keepdims=True)
         ds = (prob * (dprob - delta)).astype(LOW)
-        out[rows, lanes] = (
+        mixed[rows, lanes] = (
             jnp.dot(ds, keys[:upto], preferred_element_type=F32) * 0.125
         ).astype(LOW)
         acc_k[:upto] += outer_sum(ds, queries)
         acc_v[:upto] += outer_sum(prob.astype(LOW), outer)
-    out[:, lanes_k] = (acc_k[...] * 0.125).astype(LOW)
-    out[:, lanes_v] = acc_v[...].astype(LOW)
+    mixed[:, lanes_k] = (acc_k[...] * 0.125).astype(LOW)
+    mixed[:, lanes_v] = acc_v[...].astype(LOW)
 
 
 def plain(body, name, ins, outs, scratch=()):
@@ -1199,14 +1272,18 @@
     units_fc = pad_to(pad_to(units_fc, 5, PIECE).reshape(4, 50, WIDE), 1, 64)
     small = pad_to(smalls, 0, 2048).reshape(16, 128)
     piece_out = pad_to(w_out.reshape(200, D), 0, PIECE)
-    tokens, got_qkv, got_fc, smalls_all, mat_out = call(
+    piece_proj = pad_to(w_proj.reshape(50, D), 0, PB)
+    tokens, got_qkv, got_fc, smalls_all, mat_out, mat_proj = call(
         prologue, "prologue", 1,
-        (inputs.reshape(MICRO, BLK, D), units_qkv, units_fc, small, piece_out),
+        (inputs.reshape(MICRO, BLK, D), units_qkv, units_fc, small, piece_out, piece_proj),
         [
-            ((2, BLK, D), LOW), ((4, 64, QW), LOW), ((4, 64, WIDE), LOW), ((YN, ZN, 4, 16, 128), LOW), ((YN, ZN, PIECE, D), LOW),
+            ((2, BLK, D), LOW), ((4, 64, QW), LOW), ((4, 64, WIDE), LOW),
+            ((YN, ZN, 4, 16, 128), LOW), ((YN, ZN, PIECE, D), LOW), ((4, YN, ZN, PB, D), LOW),
         ],
-        [ANY] * 5, [ANY] * 5, [], 3 * TEAM_SWAP_SEMS + TOKENS_SEMS + GATHER_SEMS + 8,
-    )
+        [ANY] * 6, [ANY] * 6, [], 3 * TEAM_SWAP_SEMS + TOKENS_SEMS + 2 * GATHER_SEMS + 14,
+    )
+    mat_out = mat_out.reshape(WIDE, D)
+    mat_proj = mat_proj.reshape(PROJ, D)
     small = smalls_all.reshape(YN, ZN, CN, XN, 2048)[..., :600].transpose(0, 2, 1, 3, 4)
     small = small.reshape(-1).astype(F32)
     gain1, shift1, bias_q, bias_v, bias_proj, gain2, shift2 = [segment(small, i) for i in range(7)]
@@ -1220,53 +1297,40 @@
     )
     bias_qkv = pick(bias_qkv, rank).reshape(QW)
 
-    tokens = tokens.reshape(2 * BLK, D).astype(F32)
+    tokens_low = tokens.reshape(2 * BLK, D)
+    tokens = tokens_low.astype(F32)
     hidden_one, ln1_pull = jax.vjp(layer_norm, tokens, gain1, shift1)
     hidden_one = dot(hidden_one.astype(LOW), to_wide).astype(LOW)
     piece_qkv = pad_to(got_qkv[:, :50].reshape(200, QW), 0, PIECE)
     piece_fc = pad_to(got_fc[:, :50].reshape(200, WIDE), 0, PIECE)
-    piece_proj = pad_to(w_proj.reshape(50, D), 0, PB)
-    hidden_one, cotangent, mat_qkv, mat_proj = call(
-        gather_first, "gather_first", 2,
+    (
+        hidden_one, cotangent, grad_all, mat_qkv, mat_fc, hidden_two, mixed, totals, context, resid,
+    ) = call(
+        forward, "forward", 2,
         (
-            hidden_one.reshape(2, BLK, WIDE), grad_out.reshape(MICRO, BLK, D),
-            piece_qkv, piece_proj,
+            hidden_one.reshape(2, BLK, WIDE), grad_out.reshape(MICRO, BLK, D), piece_qkv, piece_fc,
+            mat_proj, to_heads.T, to_wide, tokens_low, bias_qkv.reshape(1, QW),
+            bias_proj.reshape(1, D), gain2.reshape(1, D), shift2.reshape(1, D),
         ),
         [
-            ((2, 2, 2, BLK, WIDE), LOW), ((2, BLK, D), LOW), ((YN, ZN, PIECE, QW), LOW),
-            ((4, YN, ZN, PB, D), LOW),
+            ((2, 2, 2, BLK, WIDE), LOW), ((2, BLK, D), LOW), ((2, 2, 2, BLK, D), LOW),
+            ((YN, ZN, PIECE, QW), LOW), ((YN, ZN, PIECE, WIDE), LOW), ((2, 2, 2, BLK, WIDE), LOW),
+            ((SEQ, QW), LOW), ((SEQ, SLOTS), F32), ((2 * BLK, PROJ), LOW), ((2 * BLK, D), F32),
         ],
-        [ANY] * 4, [ANY] * 4, [], TEAM_GATHER_SEMS + TOKENS_SEMS + 2 * GATHER_SEMS + 6,
+        [ANY] * 7 + [VM] * 5, [ANY] * 6 + [VM] * 4,
+        [
+            pltpu.VMEM((2, 2, 2, BLK, WIDE), LOW), pltpu.VMEM((YN, ZN, PIECE, QW), LOW),
+            pltpu.VMEM((PROJ, D), LOW), pltpu.VMEM((4 * HW, PROJ), LOW), pltpu.VMEM((D, WIDE), LOW),
+            pltpu.VMEM((SEQ, HW), LOW), pltpu.VMEM((4, 2, BLK, HW), LOW), pltpu.VMEM((2, BLK, WIDE), LOW),
+        ],
+        3 * TEAM_GATHER_SEMS + TOKENS_SEMS + 2 * GATHER_SEMS + 2 * TEAM_SWAP_SEMS + 5,
     )
     hidden_one = hidden_one.reshape(SEQ, WIDE)
+    hidden_two = hidden_two.reshape(SEQ, WIDE)
+    grad_all = grad_all.reshape(SEQ, D)
     mat_qkv = mat_qkv.reshape(WIDE, QW)
-    mat_out = mat_out.reshape(WIDE, D)
-    mat_proj = mat_proj.reshape(PROJ, D)
-
-    mixed, context, totals, got, mat_fc, grad_all = call(
-        attention, "attention", 3,
-        (hidden_one, mat_qkv, bias_qkv.reshape(1, QW), piece_fc, cotangent),
-        [
-            ((SEQ, QW), LOW), ((SEQ, HW), LOW), ((SEQ, SLOTS), F32), ((4, 2, BLK, HW), LOW),
-            ((YN, ZN, PIECE, WIDE), LOW), ((2, 2, 2, BLK, D), LOW),
-        ],
-        [ANY, ANY, VM, ANY, ANY], [VM, VM, VM, VM, ANY, ANY],
-        [pltpu.VMEM((SEQ, WIDE), LOW), pltpu.VMEM((WIDE, QW), LOW)],
-        2 * TEAM_SWAP_SEMS + GATHER_SEMS + TEAM_GATHER_SEMS + 2,
-    )
     mat_fc = mat_fc.reshape(WIDE, WIDE)
-    grad_all = grad_all.reshape(SEQ, D)
-    got = got.reshape(4, 2 * BLK, HW)
-    context = jnp.concatenate([got[r] for r in range(4)], axis=1)
-    context = back_product(context, to_heads).astype(LOW)
-    resid = tokens + dot(context, mat_proj) + bias_proj
-    hidden_two, ln2_pull = jax.vjp(layer_norm, resid, gain2, shift2)
-    hidden_two = dot(hidden_two.astype(LOW), to_wide).astype(LOW)
-    (hidden_two,) = call(
-        gather_second, "gather_second", 4, (hidden_two.reshape(2, BLK, WIDE),),
-        [((2, 2, 2, BLK, WIDE), LOW)], [ANY], [ANY], [], TEAM_GATHER_SEMS,
-    )
-    hidden_two = hidden_two.reshape(SEQ, WIDE)
+    _, ln2_pull = jax.vjp(layer_norm, resid, gain2, shift2)
     result, grad_hidden_two, grad_out_w, grad_pre, fc_terms = call(
         feed_forward, "feed_forward", 5,
         (hidden_two, grad_all, mat_fc, mat_out, bias_fc.reshape(1, WIDE)),
@@ -1306,7 +1370,7 @@
             ((2, BLK, WIDE), F32), ((PIECE, QW), LOW), ((PIECE, WIDE), LOW), ((PB, D), F32),
             ((2, BLK, D), LOW), ((1, QW), F32),
         ],
-        [ANY] * 4 + [VM, VM, ANY, VM, VM, ANY], [VM, VM, VM, VM, ANY, VM],
+        [ANY] * 5 + [VM, ANY, VM, VM, ANY], [VM, VM, VM, VM, ANY, VM],
         [
             pltpu.VMEM((SEQ, WIDE), LOW), pltpu.VMEM((SEQ, WIDE), LOW), pltpu.VMEM((WIDE, QW), LOW),
             pltpu.VMEM((WIDE, WIDE), LOW), pltpu.VMEM((SEQ, WIDE), LOW), pltpu.VMEM((SEQ, HW), LOW), pltpu.VMEM((SEQ, QW), LOW),
@@ -1318,7 +1382,7 @@
             pltpu.VMEM((PROJ // 2, WIDE), LOW), pltpu.VMEM((PROJ // 4, D), LOW),
             pltpu.VMEM((PROJ // 4, WIDE), LOW),
         ],
-        TEAM_SCATTER_SEMS + 3 * SCATTER_SEMS + TOKENS_SEMS + 2 * TEAM_SWAP_SEMS + 8,
+        TEAM_SCATTER_SEMS + 3 * SCATTER_SEMS + TOKENS_SEMS + 2 * TEAM_SWAP_SEMS + 9,
     )
     grad_hidden_one = back_product(grad_hidden_one.reshape(2 * BLK, WIDE).astype(LOW), to_wide)
     grad_ln_one, grad_gain_one, grad_shift_one = ln1_pull(grad_hidden_one)

time: 700 us -> 662 us (0.946)
  Pallas kernels: 592 us -> 552 us
  matrix products: 29.4 us -> 17.8 us
    pallas_call x7 -> x5, Pallas kernels: 592 us -> 552 us  [call(): pl.pallas_call(body, out_shape=[jax.ShapeDtypeStruct(s, d) for s, d in ou...]
    convert_element_type x1 -> x2, other arithmetic: 0.4 us -> 8.96 us  [one_hot(): return (rows == jnp.asarray(order)[None, :]).astype(LOW)]
    dot_general x4 -> x2, matrix products: 20 us -> 11.4 us  [dot(): return jnp.dot(left, right, preferred_element_type=F32)]
where the time goes in v4:
time: 662 us; the launch traced here: 653 us
  Pallas kernels  552 us (83%)
  local copies, waits for them, and re-layouts  58.9 us (9%)
  other arithmetic  22.8 us (3%)
  matrix products  17.8 us (3%)
    pallas_call x5, Pallas kernels, call(): pl.pallas_call(body, out_shape=[jax.ShapeDtypeStruct(s, d) for s, d in ou...  552 us

profile of v4, /device:TPU:0, one launch (start us, length us, event | category | flops | bytes accessed | tf_op | source)
XLA Modules:
  0.0 653.0 jit_solution(11504424336492469696)
XLA Ops:
  0.7 0.5 compare_convert_fusion
  1.3 1.3 pad_bitcast_fusion.9.small
  2.6 1.1 reshape.451
  3.7 0.7 pad.107.piece_proj
  4.4 1.9 reshape.445
  6.3 0.7 fusion.32
  7.9 0.5 copy.101
  8.5 0.7 reshape.492
  9.2 0.9 pad.102.units_qkv
  10.1 0.5 reshape.450
  10.7 0.9 pad.106.piece_out
  11.6 2.4 reshape.447
  14.7 1.1 reshape.493
  15.8 1.0 pad.104.units_fc
  16.8 1.2 copy.80
  18.0 1.2 copy.88
  19.3 4.8 fusion.4.to_wide
  24.0 4.2 fusion.to_proj
  28.2 107.8 %prologue.1 = (bf16[2,128,1600]{2,1,0:T(8,128)(2,1)}, bf16[4,64,1344]{2,1,0:T(8,128)(2,1)}, bf16[4,64,1664]{2,1,0:T(8,128)(2,1)}, bf16[2,4,4,16,128]{4,3,2,1,0:T...) custom-call(bf16[2,128,1600]{2,1,0:T(8,128)(2,1)} %bitcast.208, ...), custom_call_target="tpu_custom_call" | custom-call | tf_op jit(solution)/shard_map/prologue/pallas_call | solution.py:394
  136.1 1.0 reshape.453
  137.3 1.4 convert_reduce_fusion
  139.4 0.7 reshape_reshape.7.bias_fc
  140.4 0.7 reshape_reshape.6.bias_qkv
  141.1 0.6 reshape.461.shift2
  141.7 0.6 reshape.459.bias_proj
  142.3 0.6 reshape.460.gain2
  142.9 1.2 slice.309
  144.4 0.9 pad.108.piece_qkv
  145.5 0.9 pad.109.piece_fc
  146.4 3.5 fusion.10
  149.9 153.4 %forward.1 = (bf16[2,2,2,128,1664]{4,3,2,1,0:T(8,128)(2,1)}, bf16[2,128,1600]{2,1,0:T(8,128)(2,1)}, bf16[2,2,2,128,1600]{4,3,2,1,0:T(8,128)(2,1)}, bf16[2,4,208,...) custom-call(bf16[2,128,1664]{2,1,0:T(8,128)(2,1)} %bitcast.220, ...), custom_call_target="tpu_custom_call" | custom-call | tf_op jit(solution)/shard_map/forward/pallas_call | solution.py:394
  303.3 90.3 %feed_forward.1 = (f32[2,128,1600]{2,1,0:T(8,128)}, f32[2,128,1664]{2,1,0:T(8,128)}, f32[208,1600]{1,0:T(8,128)}, bf16[1024,1664]{1,0:T(8,128)(2,1)}, f32[1,1664]{1,0:T(1,128)}) custom-call(bf16[1024,1664]{1,0:T(8,128)(2,1)} %bitcast.199, bf16[1024,1600]{1,0:T(8,128)(2,1)} %bitcast.206, bf16[1664,1664]{1,0:T(8,128)(2,1)} %bitcast.204, ...), custom_call_target="tpu_custom_call" | custom-call | tf_op jit(solution)/shard_map/feed_forward/pallas_call | solution.py:394
  395.1 1.5 convert_element_type.137
  396.7 3.2 fusion.40
  400.0 1.7 reshape.483
  401.7 2.1 copy.89
  404.4 0.9 copy-done.9
  405.3 1.5 fusion.29
  407.2 0.9 copy-done.3
  408.1 8.0 %fusion.11 = bf16[256,1792]{1,0:T(8,128)(2,1)S(1)} fusion(s32[1792]{0:T(1024)S(1)} %copy-done.22, bf16[256,1600]{1,0:T(8,128)(2,1)S(1)} %get-tuple-element.107.branch, bf16[2048,1600]{1,0:T(8,128)(2,1)} %bitcast.202), kind=kOutput, calls=%fused_computation.15 | convolution fusion | flops 3561422848 | bytes 8297472 | tf_op jit(solution)/shard_map/dot_general | solution.py:1255
  416.6 1.1 pad_maximum_fusion.swap_parts
  417.7 170.8 %backward.1 = (f32[2,128,1664]{2,1,0:T(8,128)}, bf16[208,1344]{1,0:T(8,128)(2,1)}, bf16[208,1664]{1,0:T(8,128)(2,1)}, f32[64,1600]{1,0:T(8,128)}, bf16[2,128,1600]{2,1,0:T(8,128)(2,1)}, /*index=5*/f32[1,1344]{1,0:T(1,128)}) custom-call(bf16[1024,1664]{1,0:T(8,128)(2,1)} %bitcast.209, bf16[1024,1664]{1,0:T(8,128)(2,1)} %bitcast.200, ...), custom_call_target="tpu_custom_call" | custom-call | tf_op jit(solution)/shard_map/backward/pallas_call | solution.py:394
  588.5 2.2 copy.98
  590.8 0.7 fusion.39
  592.1 0.9 reshape.479
  593.2 0.9 pad.117.units_qkv
  594.4 1.0 pad.118.units_fc
  595.4 0.6 copy-done.8
  596.1 3.2 fusion.41
  599.3 1.8 copy.90
  601.6 0.8 multiply_reduce_fusion.1
  602.8 3.1 add_convert_fusion
  606.0 0.7 copy.93
  606.7 29.2 %epilogue.1 = (bf16[2,128,1600]{2,1,0:T(8,128)(2,1)}, bf16[4,64,1344]{2,1,0:T(8,128)(2,1)}, bf16[4,64,1664]{2,1,0:T(8,128)(2,1)}, f32[8,128]{1,0:T(8,128)}) custom-call(bf16[2,128,1600]{2,1,0:T(8,128)(2,1)} %bitcast.207, bf16[4,64,1344]{2,1,0:T(8,128)(2,1)} %pad.117.units_qkv, bf16[4,64,1664]{2,1,0:T(8,128)(2,1)} %pad.118.units_fc, ...), custom_call_target="tpu_custom_call" | custom-call | tf_op jit(solution)/shard_map/epilogue/pallas_call | solution.py:394
  635.9 1.2 slice.377
  637.1 1.3 slice.378
  638.4 1.1 slice.351
  639.8 0.8 reshape.478
  640.5 0.8 fusion.31
  642.7 1.8 reshape.488
  644.6 1.4 reshape.494
  646.5 0.9 copy.97
  647.4 3.7 reshape.490
  651.2 1.6 copy.99
  (176 shorter events, 10.2 us)
Async XLA Ops:
  8.4 1.7 copy-start.16
  9.2 2.4 copy-start.17
  14.7 2.1 copy-start.12
  15.8 2.2 copy-start.13
  16.8 2.5 copy-start.21
  19.3 4.8 copy-start.22
  136.1 2.6 copy-start
  142.9 2.3 copy-start.14
  303.3 90.3 %copy-start.2 = (f32[256,1600]{1,0:T(8,128)S(1)}, f32[256,1600]{1,0:T(8,128)}, u32[]{:S(2)}) copy-start(f32[256,1600]{1,0:T(8,128)} %get-tuple-element.55) | copy-start | bytes 4915204
  393.6 0.7 copy-start.23
  393.6 1.2 copy-start.4
  396.7 3.2 copy-start.10
  403.8 1.5 copy-start.9
  405.3 1.5 copy-start.5
  406.8 1.3 copy-start.3
  408.1 8.0 %copy-start.7 = (bf16[256,1600]{1,0:T(8,128)(2,1)}, bf16[256,1600]{1,0:T(8,128)(2,1)S(1)}, u32[]{:S(2)}) copy-start(bf16[256,1600]{1,0:T(8,128)(2,1)S(1)} %get-tuple-element.107.branch) | copy-start | bytes 2457604
  417.7 173.8 %copy-start.24 = (f32[4]{0:T(128)S(1)}, f32[4]{0:T(128)}, u32[]{:S(2)}) copy-start(f32[4]{0:T(128)} %compare_convert_fusion) | copy-start | bytes 52
  588.5 3.5 copy-start.20
  588.5 4.5 copy-start.19
  593.0 1.1 copy-start.18
  594.2 1.8 copy-start.8
  599.2 1.9 copy-start.1
  601.6 1.2 copy-start.6
  642.7 1.9 copy-start.15
  647.4 3.7 copy-start.11

commit v5 on v4

--- a/solution.py
+++ b/solution.py
@@ -318,7 +318,7 @@
 
 
 DP, CTX = 4, 8
-YN, CN, ZN, XN = 2, 2, 4, 2
+YN, CN, HN, LN, XN = 2, 2, 2, 2, 2
 SLOTS = 7
 HW = SLOTS * HEAD
 QW = 3 * HW
@@ -339,11 +339,15 @@
 
 def here():
     dp, ctx = lax.axis_index("dp"), lax.axis_index("ctx")
-    return dp // CN, dp % CN, ctx // XN, ctx % XN
-
-
-def device(y, c, z, x):
-    return (y * CN + c, z * XN + x)
+    return dp // CN, dp % CN, ctx // 4, (ctx // XN) % LN, ctx % XN
+
+
+def device(y, c, h, l, x):
+    return (y * CN + c, (h * LN + l) * XN + x)
+
+
+def team_number(y, h, x):
+    return y * 4 + h * 2 + x
 
 
 class Wires:
@@ -375,13 +379,16 @@
     )
 
 
-def team_peers(y, c, z, x):
-    return [device(y, 1 - c, z, x), device(y, c, z, 1 - x), device(y, 1 - c, z, 1 - x)]
-
-
-def grid_peers(y, c, z, x):
-    ring = [device(y, c, lax.rem(z + k, ZN), x) for k in range(1, ZN)]
-    return ring + [device(1 - y, c, z, x)]
+def team_peers(y, c, h, l, x):
+    return [
+        device(y, 1 - c, h, l, x), device(y, c, h, 1 - l, x), device(y, 1 - c, h, 1 - l, x)
+    ]
+
+
+def grid_peers(y, c, h, l, x):
+    return [
+        device(1 - y, c, h, l, x), device(y, c, 1 - h, l, x), device(y, c, h, l, 1 - x)
+    ]
 
 
 def meet(peers):
@@ -404,184 +411,162 @@
     )(*ins)
 
 
+class Routes:
+    def __init__(self, spot):
+        y, c, h, l, x = spot
+        self.place = (y, h, x)
+        self.peers = {
+            "y": device(1 - y, c, h, l, x),
+            "h": device(y, c, 1 - h, l, x),
+            "x": device(y, c, h, l, 1 - x),
+        }
+
+    def flipped(self, ways):
+        y, h, x = self.place
+        return team_number(
+            1 - y if "y" in ways else y, 1 - h if "h" in ways else h, 1 - x if "x" in ways else x
+        )
+
+
+def halves(rows):
+    cut = (rows // 2 + 15) // 16 * 16
+    return ((0, cut, "hxy"), (cut, rows - cut, "hyx"))
+
+
 class Gather:
     def __init__(self, wires, piece, whole, spot):
-        y, c, z, x = self.spot = spot
-        self.z = z
-        self.across = device(1 - y, c, z, x)
-        up = device(y, c, lax.min(z + 1, ZN - 1), x)
-        down = device(y, c, lax.max(z - 1, 0), x)
-        self.local = wires.near(piece, whole.at[y, z])
-        self.mine = wires.far(piece, whole.at[y, z], self.across)
-        self.ups, self.downs, self.from_low, self.from_high = [], [], [], []
-        for turn in range(1, ZN):
-            low = lax.max(z - (turn - 1), 0)
-            high = lax.min(z + (turn - 1), ZN - 1)
-            source = piece if turn == 1 else whole.at[y, low]
-            self.ups.append(wires.far(source, whole.at[y, low], up))
-            source = piece if turn == 1 else whole.at[y, high]
-            self.downs.append(wires.far(source, whole.at[y, high], down))
-            low = lax.max(z - turn, 0)
-            high = lax.min(z + turn, ZN - 1)
-            self.from_low.append(wires.far(whole.at[y, low], whole.at[y, low], self.across))
-            self.from_high.append(wires.far(whole.at[y, high], whole.at[y, high], self.across))
-
-    def send_up(self, turn):
-        return (self.z >= turn - 1) & (self.z < ZN - 1)
-
-    def send_down(self, turn):
-        return (self.z <= ZN - turn) & (self.z > 0)
+        routes = Routes(spot)
+        self.local = wires.near(piece, whole.at[routes.flipped("")])
+        self.parts = []
+        for start, size, order in halves(piece.shape[0]):
+            at = pl.ds(start, size)
+            first, second, third = order
+
+            def copy(ways, way):
+                spot = whole.at[routes.flipped(ways), at]
+                source = piece.at[at] if not ways else spot
+                return wires.far(source, spot, routes.peers[way])
+
+            self.parts.append(
+                {
+                    "first": copy("", first),
+                    "second": [copy("", second), copy(first, second)],
+                    "third": [
+                        copy("", third), copy(second, third), copy(first, third),
+                        copy(first + second, third),
+                    ],
+                }
+            )
 
     def start(self):
         self.local.start()
-        self.mine.start()
-        pl.when(self.send_up(1))(self.ups[0].start)
-        pl.when(self.send_down(1))(self.downs[0].start)
+        for part in self.parts:
+            part["first"].start()
+            part["second"][0].start()
+            part["third"][0].start()
 
     def step(self, turn):
-        @pl.when(self.z >= turn)
-        def _():
-            self.ups[turn - 1].wait_recv()
-            if turn < ZN - 1:
-                pl.when(self.send_up(turn + 1))(self.ups[turn].start)
-            self.from_low[turn - 1].start()
-
-        @pl.when(self.z + turn <= ZN - 1)
-        def _():
-            self.downs[turn - 1].wait_recv()
-            if turn < ZN - 1:
-                pl.when(self.send_down(turn + 1))(self.downs[turn].start)
-            self.from_high[turn - 1].start()
+        for part in self.parts:
+            if turn == 1:
+                part["second"][0].wait_recv()
+                part["third"][1].start()
+            elif turn == 2:
+                part["first"].wait_recv()
+                part["second"][1].start()
+                part["third"][2].start()
+            else:
+                part["second"][1].wait_recv()
+                part["third"][3].start()
 
     def finish(self):
         self.local.wait()
-        self.mine.wait()
-        for turn in range(1, ZN):
-            pl.when(self.send_up(turn))(self.ups[turn - 1].wait_send)
-            pl.when(self.send_down(turn))(self.downs[turn - 1].wait_send)
-            pl.when(self.z >= turn)(self.from_low[turn - 1].wait)
-            pl.when(self.z + turn <= ZN - 1)(self.from_high[turn - 1].wait)
-
-
-GATHER_SEMS = 1 + 2 + 2 * 4 * 3
+        for part in self.parts:
+            for copy in [part["first"]] + part["second"]:
+                copy.wait_send()
+            for copy in part["third"]:
+                copy.wait()
+
+
+GATHER_SEMS = 1 + 2 * 2 * 7
 
 
 class Scatter:
-    def __init__(self, wires, parts, landed, arrived, spot):
-        y, c, z, x = spot
-        self.y, self.z, self.size = y, z, landed.shape[1]
-        self.parts, self.landed, self.arrived = parts, landed, arrived
-        across = device(1 - y, c, z, x)
-        up = device(y, c, lax.min(z + 1, ZN - 1), x)
-        down = device(y, c, lax.max(z - 1, 0), x)
-        base = wires.used
-        wires.used += 2 * ZN
-        self.over = lambda o: pltpu.make_async_remote_copy(
-            src_ref=parts.at[self.rows(1 - y, o)],
-            dst_ref=landed.at[o],
-            send_sem=wires.sems.at[base + o],
-            recv_sem=wires.sems.at[base + ZN + o],
-            device_id=across,
-            device_id_type=pl.DeviceIdType.MESH,
-        )
-        self.ups, self.downs = [], []
-        for turn in range(1, ZN):
-            high = lax.min(z + ZN - turn, ZN - 1)
-            low = lax.max(z - ZN + turn, 0)
-            slot = self.slot(0, turn, z + 1)
-            self.ups.append((high, wires.far(landed.at[high], arrived.at[slot], up)))
-            slot = self.slot(1, turn, z - 1)
-            self.downs.append((low, wires.far(landed.at[low], arrived.at[slot], down)))
-
-    def rows(self, y, z):
-        return pl.ds(pl.multiple_of((y * ZN + z) * self.size, 16), self.size)
-
-    @staticmethod
-    def slot(side, turn, z):
-        return jnp.where(z == 1 + side, turn - 1, turn + 1)
+    def __init__(self, wires, parts, landed, spot):
+        routes = Routes(spot)
+        self.rows = landed.shape[1]
+        self.parts, self.landed = parts, landed
+        self.jobs = []
+        for start, size, order in halves(self.rows):
+            first, second, third = order
+            at = pl.ds(start, size)
+
+            def term(ways):
+                base = routes.flipped(ways) * self.rows + start
+                return parts.at[pl.ds(pl.multiple_of(base, 16), size)]
+
+            stay = [second + first, second, first, ""]
+            job = {
+                "terms": [term(ways) for ways in stay],
+                "spots": [landed.at[k, at] for k in range(7)],
+                "over": [
+                    wires.far(term(third + ways), landed.at[k, at], routes.peers[third])
+                    for k, ways in enumerate(stay)
+                ],
+                "along": [
+                    wires.far(landed.at[k, at], landed.at[4 + k, at], routes.peers[second])
+                    for k in range(2)
+                ],
+                "last": wires.far(landed.at[2, at], landed.at[6, at], routes.peers[first]),
+                "at": slice(start, start + size),
+            }
+            self.jobs.append(job)
 
     def start(self):
-        z = self.z
-        first = jnp.where(z < 2, 3, 0)
-        second = jnp.where(z < 2, 2, 1)
-        third = jnp.where(z == 0, 1, jnp.where(z == 1, 0, jnp.where(z == 2, 3, 2)))
-        for o in (first, second, third, z):
-            self.over(o).start()
-
-    def goes_up(self, turn):
-        return (self.z <= turn - 1) & (self.z < ZN - 1)
-
-    def goes_down(self, turn):
-        return (self.z >= ZN - turn) & (self.z > 0)
-
-    def add(self, o, side, turn, more):
-        total = self.landed[o].astype(F32) + self.parts[self.rows(self.y, o), :].astype(F32)
-        if more:
-            total = total + self.arrived[self.slot(side, turn - 1, self.z)].astype(F32)
-        self.landed[o] = total.astype(LOW)
+        for k in (0, 2):
+            for job in self.jobs:
+                job["over"][k].start()
 
     def step(self, turn):
-        for side, goes, jobs, inner in (
-            (0, self.goes_up, self.ups, self.z > 0),
-            (1, self.goes_down, self.downs, self.z < ZN - 1),
-        ):
-            o, copy = jobs[turn - 1]
-
-            @pl.when(goes(turn))
-            def _(side=side, jobs=jobs, inner=inner, o=o, copy=copy):
-                self.over(o).wait_recv()
-                if turn == 1:
-                    self.add(o, side, turn, False)
-                else:
-
-                    @pl.when(inner)
-                    def _():
-                        jobs[turn - 2][1].wait_recv()
-                        self.add(o, side, turn, True)
-
-                    @pl.when(jnp.logical_not(inner))
-                    def _():
-                        self.add(o, side, turn, False)
-
-                copy.start()
+        k = (0, 2, 1)[turn - 1]
+        for job in self.jobs:
+            job["over"][k].wait_recv()
+            if turn < 3:
+                job["over"][2 * turn - 1].start()
+            total = job["spots"][k][...].astype(F32) + job["terms"][k][...].astype(F32)
+            if turn == 2:
+                job["along"][0].wait_recv()
+                total = total + job["spots"][4][...].astype(F32)
+            job["spots"][k][...] = total.astype(LOW)
+            (job["along"] + [job["last"]])[k].start()
 
     def finish(self, total):
-        self.over(self.z).wait_recv()
-        total[...] = (
-            self.landed[self.z].astype(F32) + self.parts[self.rows(self.y, self.z), :].astype(F32)
-        ).astype(total.dtype)
-        last = ZN - 1
-
-        @pl.when(self.z > 0)
-        def _():
-            self.ups[last - 1][1].wait_recv()
-            total[...] = (total[...].astype(F32) + self.arrived[self.slot(0, last, self.z)].astype(F32)).astype(total.dtype)
-
-        @pl.when(self.z < ZN - 1)
-        def _():
-            self.downs[last - 1][1].wait_recv()
-            total[...] = (total[...].astype(F32) + self.arrived[self.slot(1, last, self.z)].astype(F32)).astype(total.dtype)
-
-        for o in range(ZN):
-            self.over(o).wait_send()
-        for turn in range(1, ZN):
-            pl.when(self.goes_up(turn))(self.ups[turn - 1][1].wait_send)
-            pl.when(self.goes_down(turn))(self.downs[turn - 1][1].wait_send)
-
-
-SCATTER_SEMS = 2 * (ZN + 6)
+        for job in self.jobs:
+            job["over"][3].wait_recv()
+            job["along"][1].wait_recv()
+            job["last"].wait_recv()
+            summed = job["terms"][3][...].astype(F32)
+            for k in (3, 5, 6):
+                summed = summed + job["spots"][k][...].astype(F32)
+            total[job["at"], :] = summed.astype(total.dtype)
+            for copy in job["over"] + job["along"] + [job["last"]]:
+                copy.wait_send()
+
+
+SCATTER_SEMS = 2 * 2 * 7
 
 
 class TeamGather:
     def __init__(self, wires, block, whole, spot):
-        y, c, z, x = spot
-        mate, beside = device(y, 1 - c, z, x), device(y, c, z, 1 - x)
-        self.local = [wires.near(block.at[s], whole.at[c, s, x]) for s in range(2)]
-        self.to_mate = [wires.far(block.at[s], whole.at[c, s, x], mate) for s in range(2)]
-        self.to_side = [wires.far(block.at[s], whole.at[c, s, x], beside) for s in range(2)]
-        self.relay = [
-            wires.far(whole.at[c, s, 1 - x], whole.at[c, s, 1 - x], mate) for s in range(2)
-        ]
+        y, c, h, l, x = spot
+        mate, beside = device(y, 1 - c, h, l, x), device(y, c, h, 1 - l, x)
+
+        def at(l, s):
+            return whole.at[c * 4 + l * 2 + s]
+
+        self.local = [wires.near(block.at[s], at(l, s)) for s in range(2)]
+        self.to_mate = [wires.far(block.at[s], at(l, s), mate) for s in range(2)]
+        self.to_side = [wires.far(block.at[s], at(l, s), beside) for s in range(2)]
+        self.relay = [wires.far(at(1 - l, s), at(1 - l, s), mate) for s in range(2)]
 
     def start(self):
         for copy in self.to_side + self.to_mate + self.local:
@@ -603,11 +588,11 @@
 
 class TeamSwap:
     def __init__(self, wires, source, target, spot):
-        y, c, z, x = spot
-        self.local = wires.near(source(c, x), target(c, x))
+        y, c, h, l, x = spot
+        self.local = wires.near(source(c, l), target(c, l))
         self.copies = [
-            wires.far(source(p, q), target(c, x), device(y, p, z, q))
-            for p, q in ((c, 1 - x), (1 - c, 1 - x), (1 - c, x))
+            wires.far(source(p, q), target(c, l), device(y, p, h, q, x))
+            for p, q in ((c, 1 - l), (1 - c, 1 - l), (1 - c, l))
         ]
 
     def start(self):
@@ -622,49 +607,51 @@
 TEAM_SWAP_SEMS = 1 + 2 * 3
 
 
+def pair_rows(c, l):
+    return pl.ds(pl.multiple_of((c * 2 + l) * 2 * BLK, 2 * BLK), 2 * BLK)
+
+
+def block_rows(c, l, s):
+    return pl.ds(pl.multiple_of((c * 4 + l * 2 + s) * BLK, BLK), BLK)
+
+
 class TeamScatter:
     def __init__(self, wires, parts, landed, leaving, arrived, spot):
-        y, c, z, x = spot
-        self.c, self.x = c, x
+        y, c, h, l, x = spot
+        self.c, self.l = c, l
         self.parts, self.landed, self.leaving, self.arrived = parts, landed, leaving, arrived
-        mate, beside = device(y, 1 - c, z, x), device(y, c, z, 1 - x)
-        self.to_mate = [wires.far(parts.at[half_rows(1 - c, s)], landed.at[s], mate) for s in range(2)]
+        mate, beside = device(y, 1 - c, h, l, x), device(y, c, h, 1 - l, x)
+        self.to_mate = [
+            wires.far(parts.at[pair_rows(1 - c, q)], landed.at[k], mate)
+            for k, q in enumerate((1 - l, l))
+        ]
         self.to_side = [wires.far(leaving.at[s], arrived.at[s], beside) for s in range(2)]
-
-    def side(self, x):
-        return pl.ds(pl.multiple_of(x * BLK, BLK), BLK)
 
     def start(self):
         for copy in self.to_mate:
             copy.start()
 
     def step(self, s):
-        self.to_mate[s].wait_recv()
-        far = 1 - self.x
+        if s == 0:
+            self.to_mate[0].wait_recv()
+        rows = slice(s * BLK, (s + 1) * BLK)
         self.leaving[s] = (
-            self.landed[s, self.side(far), :].astype(F32)
-            + self.parts[block_rows(self.c, s, far), :].astype(F32)
+            self.landed[0, rows, :].astype(F32)
+            + self.parts[block_rows(self.c, 1 - self.l, s), :].astype(F32)
         ).astype(LOW)
         self.to_side[s].start()
 
     def finish(self, total):
+        self.to_mate[1].wait_recv()
         for s in range(2):
             self.to_side[s].wait_recv()
             total[s] = (
-                self.landed[s, self.side(self.x), :].astype(F32)
-                + self.parts[block_rows(self.c, s, self.x), :].astype(F32)
+                self.landed[1, s * BLK : (s + 1) * BLK, :].astype(F32)
+                + self.parts[block_rows(self.c, self.l, s), :].astype(F32)
                 + self.arrived[s].astype(F32)
             )
         for copy in self.to_mate + self.to_side:
             copy.wait_send()
-
-
-def block_rows(c, s, x):
-    return pl.ds(pl.multiple_of((c * 4 + s * 2 + x) * BLK, BLK), BLK)
-
-
-def half_rows(c, s):
-    return pl.ds(pl.multiple_of((c * 2 + s) * 2 * BLK, 2 * BLK), 2 * BLK)
 
 
 TEAM_SCATTER_SEMS = 2 * 4
@@ -679,197 +666,218 @@
 
 
 def scatter_scratch(rows, width):
-    return [pltpu.VMEM((ZN, rows, width), LOW), pltpu.VMEM((5, rows, width), LOW)]
+    return [pltpu.VMEM((7, rows, width), LOW)]
 
 
 class Tokens:
-    def __init__(self, wires, source, target, spot, back):
-        y, c, z, x = spot
-        self.own, self.local, self.copies, self.peers = [], [], [], []
+    def __init__(self, wires, source, target, spot):
+        y, c, h, l, x = spot
+        self.stays = h == c
+        goals = token_goals(spot)
+        pairs = []
         for k in range(2):
-            if not back:
-                m = lax.rem(z + k, 2)
-                goal_c, goal_z = z // 2, 2 * m + c
-                block, landing = source.at[m], target.at[lax.rem(z, 2)]
-            else:
-                m = z // 2
-                s = lax.rem(m + k, 2)
-                goal_c, goal_z = lax.rem(z, 2), 2 * c + s
-                block, landing = source.at[s], target.at[m]
-            goal = device(y, goal_c, goal_z, x)
-            stays = (goal_c == c) & (goal_z == z)
-            self.own.append(stays)
-            self.peers.append(goal)
-            self.local.append(wires.near(block, landing))
-            self.copies.append(wires.far(block, landing, goal))
+            other = lax.rem(x + k, 2)
+            pairs.append((source.at[other], target.at[x]))
+        self.local = wires.near(*pairs[0])
+        self.copies = [wires.far(*pair, goal) for pair, goal in zip(pairs, goals)]
 
     def start(self):
-        for stays, local, copy in zip(self.own, self.local, self.copies):
-            pl.when(stays)(local.start)
-            pl.when(jnp.logical_not(stays))(copy.start)
+        pl.when(self.stays)(self.local.start)
+        pl.when(jnp.logical_not(self.stays))(self.copies[0].start)
+        self.copies[1].start()
 
     def finish(self):
-        for stays, local, copy in zip(self.own, self.local, self.copies):
-            pl.when(stays)(local.wait)
-            pl.when(jnp.logical_not(stays))(copy.wait)
-
-
-TOKENS_SEMS = 2 * 3
-
-
-def token_sources(spot, back):
-    y, c, z, x = spot
-    found = []
-    for k in range(2):
-        if back:
-            m = lax.rem(z + k, 2)
-            goal = (z // 2, 2 * m + c)
-        else:
-            s = lax.rem(z // 2 + k, 2)
-            goal = (lax.rem(z, 2), 2 * c + s)
-        found.append((device(y, goal[0], goal[1], x), (goal[0] == c) & (goal[1] == z)))
-    return found
-
-
-def meet_tokens(peers, spot, back):
-    for peer in peers:
+        pl.when(self.stays)(self.local.wait)
+        pl.when(jnp.logical_not(self.stays))(self.copies[0].wait)
+        self.copies[1].wait()
+
+
+TOKENS_SEMS = 1 + 2 * 2
+
+
+def token_goals(spot):
+    y, c, h, l, x = spot
+    return [device(y, h, c, l, x), device(y, h, c, l, 1 - x)]
+
+
+def meet_tokens(peers, spot):
+    y, c, h, l, x = spot
+    same, other = token_goals(spot)
+    for peer in peers + [other]:
         signal(peer)
-    for source, stays in token_sources(spot, back):
-        pl.when(jnp.logical_not(stays))(functools.partial(signal, source))
-    leaving = sum(jnp.where(stays, 0, 1) for _, stays in token_sources(spot, not back))
-    pl.semaphore_wait(pltpu.get_barrier_semaphore(), len(peers) + leaving)
+    pl.when(h != c)(functools.partial(signal, same))
+    count = len(peers) + 1 + jnp.where(h == c, 0, 1)
+    pl.semaphore_wait(pltpu.get_barrier_semaphore(), count)
+
+
+class Smalls:
+    def __init__(self, wires, small, smalls, spot):
+        y, c, h, l, x = spot
+        own = team_number(y, h, x)
+        self.first = TeamSwap(
+            wires, lambda p, q: small, lambda p, q: smalls.at[own, p * LN + q], spot
+        )
+        self.second = [
+            wires.far(smalls.at[own], smalls.at[own], where) for where in team_twins(*spot)
+        ]
+
+    def start(self):
+        self.first.start()
+
+    def step(self):
+        self.first.finish()
+        for copy in self.second:
+            copy.start()
+
+    def finish(self):
+        for copy in self.second:
+            copy.wait()
+
+
+SMALLS_SEMS = TEAM_SWAP_SEMS + 2 * 7
+
+
+def team_twins(y, c, h, l, x):
+    ways = ((0, 0, 1), (1, 0, 0), (0, 1, 0), (1, 0, 1), (0, 1, 1), (1, 1, 0), (1, 1, 1))
+    return [
+        device(1 - y if a else y, c, 1 - h if b else h, l, 1 - x if d else x) for a, b, d in ways
+    ]
+
+
+def join_units(units, wide, piece):
+    for k in range(4):
+        wide[k * 50 : (k + 1) * 50, :] = units[k, :50, :].astype(F32)
+    wide[200:, :] = jnp.zeros((PIECE - 200, wide.shape[1]), F32)
+    piece[...] = wide[...].astype(LOW)
 
 
 def prologue(
-    inputs, units_qkv, units_fc, small, piece_out, piece_proj,
-    tokens, got_qkv, got_fc, smalls, all_out, all_proj, sems,
+    inputs, units_qkv, units_fc, small, piece_proj,
+    tokens, smalls, all_qkv, all_proj, piece_fc,
+    got_qkv, got_fc, wide_qkv, wide_fc, piece_qkv, beside_proj, sems,
 ):
-    spot = y, c, z, x = here()
+    spot = y, c, h, l, x = here()
     wires = Wires(sems)
-    meet_tokens(team_peers(*spot) + grid_peers(*spot), spot, False)
-    first = TeamSwap(
-        wires, lambda p, q: small, lambda p, q: smalls.at[y, z, p * XN + q], spot
-    )
-    qkv = TeamSwap(
-        wires, lambda p, q: units_qkv.at[p * XN + q], lambda p, q: got_qkv.at[p * XN + q], spot
-    )
-    fc = TeamSwap(
-        wires, lambda p, q: units_fc.at[p * XN + q], lambda p, q: got_fc.at[p * XN + q], spot
-    )
-    move = Tokens(wires, inputs, tokens, spot, False)
-    out = Gather(wires, piece_out, all_out, spot)
-    rank = c * XN + x
+    rank = c * LN + l
+    meet_tokens(team_peers(*spot) + team_twins(*spot), spot)
+    values = Smalls(wires, small, smalls, spot)
+    qkv_units = TeamSwap(
+        wires, lambda p, q: units_qkv.at[p * LN + q], lambda p, q: got_qkv.at[p * LN + q], spot
+    )
+    fc_units = TeamSwap(
+        wires, lambda p, q: units_fc.at[p * LN + q], lambda p, q: got_fc.at[p * LN + q], spot
+    )
+    move = Tokens(wires, inputs, tokens, spot)
+    qkv = Gather(wires, piece_qkv, all_qkv, spot)
+    other = c * LN + 1 - l
     proj = Gather(wires, piece_proj, all_proj.at[rank], spot)
-    side = wires.far(all_proj.at[rank], all_proj.at[rank], device(y, c, z, 1 - x))
-    mate = device(y, 1 - c, z, x)
+    side = wires.far(piece_proj, beside_proj, device(y, c, h, 1 - l, x))
+    beside = Gather(wires, beside_proj, all_proj.at[other], spot)
+    mate = device(y, 1 - c, h, l, x)
     relay = [
-        wires.far(all_proj.at[r], all_proj.at[r], mate) for r in (rank, c * XN + 1 - x)
+        wires.far(all_proj.at[r], all_proj.at[r], mate) for r in (rank, other)
     ]
-    column = [
-        wires.far(smalls.at[y, z], smalls.at[y, z], device(y, c, lax.rem(z + k, ZN), x))
-        for k in range(1, ZN)
-    ]
-    over = wires.far(smalls.at[y], smalls.at[y], device(1 - y, c, z, x))
-    first.start()
+    values.start()
+    qkv_units.start()
+    values.step()
+    side.start()
+    proj.start()
+    qkv_units.finish()
+    join_units(got_qkv, wide_qkv, piece_qkv)
+    qkv.start()
+    fc_units.start()
     move.start()
-    qkv.start()
-    fc.start()
-    first.finish()
-    for copy in column:
-        copy.start()
-    proj.start()
-    out.start()
-    for copy in column:
-        copy.wait()
-    over.start()
+    side.wait()
+    beside.start()
     proj.step(1)
-    over.wait()
     proj.step(2)
     proj.step(3)
-    out.step(1)
+    values.finish()
+    qkv.step(1)
     proj.finish()
-    side.start()
     relay[0].start()
+    beside.step(1)
+    qkv.step(2)
+    beside.step(2)
+    fc_units.finish()
+    join_units(got_fc, wide_fc, piece_fc)
+    qkv.step(3)
+    beside.step(3)
+    beside.finish()
+    relay[1].start()
     move.finish()
     qkv.finish()
-    fc.finish()
-    out.step(2)
-    out.step(3)
-    side.wait_recv()
-    relay[1].start()
-    out.finish()
-    side.wait_send()
     for copy in relay:
         copy.wait()
 
 
 def forward(
-    hidden, grads, piece_qkv, piece_fc, mat_proj, to_proj, to_wide,
+    hidden, grads, piece_fc, piece_out, mat_qkv, mat_proj, to_proj, to_wide,
     tokens, bias_qkv, bias_proj, gain2, shift2,
-    hidden_all, cotangent, grad_all, all_qkv, all_fc, second_all, mixed, totals, context_out, resid,
-    hidden_in, mat_in, proj_in, to_proj_in, to_wide_in, context, got, second, sems,
+    hidden_all, cotangent, grad_all, all_fc, all_out, second_all, mixed, totals, context_out, resid,
+    mat_in, proj_in, to_proj_in, to_wide_in, context, got, second, sems,
 ):
-    spot = y, c, z, x = here()
+    spot = y, c, h, l, x = here()
     wires = Wires(sems)
     load = [
         wires.near(*both)
-        for both in ((mat_proj, proj_in), (to_proj, to_proj_in), (to_wide, to_wide_in))
+        for both in (
+            (mat_qkv, mat_in), (mat_proj, proj_in), (to_proj, to_proj_in), (to_wide, to_wide_in)
+        )
     ]
-    load_hidden, load_qkv = wires.near(hidden_all, hidden_in), wires.near(all_qkv, mat_in)
-    meet_tokens(team_peers(*spot) + grid_peers(*spot), spot, False)
+    for copy in load:
+        copy.start()
+    meet_tokens(team_peers(*spot) + grid_peers(*spot), spot)
     team = TeamGather(wires, hidden, hidden_all, spot)
-    qkv = Gather(wires, piece_qkv, all_qkv, spot)
     fc = Gather(wires, piece_fc, all_fc, spot)
-    bring = Tokens(wires, grads, cotangent, spot, False)
+    out = Gather(wires, piece_out, all_out, spot)
+    bring = Tokens(wires, grads, cotangent, spot)
     team_two = TeamGather(wires, cotangent, grad_all, spot)
     team_three = TeamGather(wires, second, second_all, spot)
     swaps = [
         TeamSwap(
             wires,
-            lambda p, q, s=s: context.at[block_rows(p, s, q)],
-            lambda p, q, s=s: got.at[p * XN + q, s],
+            lambda p, q, s=s: context.at[block_rows(p, q, s)],
+            lambda p, q, s=s: got.at[p * LN + q, s],
             spot,
         )
         for s in range(2)
     ]
-    qkv.start()
     team.start()
-    qkv.step(1)
+    fc.start()
     team.step(0)
     team.step(1)
-    qkv.step(2)
-    qkv.step(3)
-    fc.start()
-    for copy in load:
-        copy.start()
+    load[0].wait()
     team.finish()
-    load_hidden.start()
-    qkv.finish()
-    load_qkv.start()
     bring.start()
-    load_hidden.wait()
-    load_qkv.wait()
+    fc.step(1)
 
     @pl.loop(0, SEQ // QB)
     def _(i):
         rows = pl.ds(pl.multiple_of(i * QB, QB), QB)
-        flat = hidden_in[i // 2, i % 2].reshape(QB, WIDE)
-        mixed[rows, :] = (dot(flat, mat_in[...].reshape(WIDE, QW)) + bias_qkv[...]).astype(LOW)
-
-    fc.step(1)
+        flat = hidden_all[pl.ds(pl.multiple_of(i * 2, 2), 2)].reshape(QB, WIDE)
+        mixed[rows, :] = (dot(flat, mat_in[...]) + bias_qkv[...]).astype(LOW)
+
+    fc.step(2)
     for head in range(SLOTS):
         attend(mixed, context, totals, head)
-        if head == 2:
-            fc.step(2)
-    bring.finish()
+        if head == 0:
+            fc.step(3)
+            out.start()
+            bring.finish()
+            team_two.start()
+        if head == 3:
+            team_two.step(0)
+        if head == 4:
+            out.step(1)
+    team_two.step(1)
     for copy in swaps:
         copy.start()
-    team_two.start()
-    fc.step(3)
-    for copy in load:
+    for copy in load[1:]:
         copy.wait()
     for copy in swaps:
         copy.finish()
+    out.step(2)
     placed = 0.0
     for r in range(4):
         placed = placed + dot(
@@ -882,13 +890,13 @@
     normed = layer_norm(found, gain2[...], shift2[...]).astype(LOW)
     second[...] = dot(normed, to_wide_in[...]).astype(LOW).reshape(2, BLK, WIDE)
     team_three.start()
-    team_two.step(0)
-    team_two.step(1)
+    fc.finish()
     team_three.step(0)
+    out.step(3)
     team_three.step(1)
     team_two.finish()
     team_three.finish()
-    fc.finish()
+    out.finish()
 
 
 def gelu_both(f):
@@ -909,19 +917,19 @@
     @pl.loop(0, count)
     def _(i):
         at = pl.ds(pl.multiple_of(i * 256, 256), 256)
-        target[at, :] = outer_sum(left[:, at], right[...]).astype(LOW)
+        target[at, :] = outer_sum(left[:, at], right()).astype(LOW)
 
     rest = left.shape[1] - count * 256
     if rest:
-        target[count * 256 :, :] = outer_sum(left[:, count * 256 :], right[...]).astype(LOW)
+        target[count * 256 :, :] = outer_sum(left[:, count * 256 :], right()).astype(LOW)
 
 
 def feed_forward(
     hidden_two, grad_all, mat_fc, mat_out, bias_fc,
     result, hidden, grad_out_w, grad_pre, terms,
-    h2, dy, wf, wo, activ, part_r, part_h, part_o, l1, s1, a1, l2, s2, a2, l3, a3, sems,
+    h2, dy, wf, wo, activ, part_r, part_h, part_o, l1, s1, a1, l2, s2, a2, l3, sems,
 ):
-    spot = y, c, z, x = here()
+    spot = y, c, h, l, x = here()
     wires = Wires(sems)
     load = [
         wires.near(*both) for both in ((hidden_two, h2), (mat_fc, wf), (grad_all, dy), (mat_out, wo))
@@ -931,7 +939,7 @@
     meet(team_peers(*spot) + grid_peers(*spot))
     second = TeamScatter(wires, part_h, l2, s2, a2, spot)
     first = TeamScatter(wires, part_r, l1, s1, a1, spot)
-    out = Scatter(wires, part_o, l3, a3, spot)
+    out = Scatter(wires, part_o, l3, spot)
     load[0].wait()
     load[1].wait()
 
@@ -944,7 +952,7 @@
         grad_pre[rows, :] = slope.astype(LOW)
 
     load[2].wait()
-    outer_into(part_o, activ, dy)
+    outer_into(part_o, activ, lambda: dy[...].reshape(SEQ, D))
     out.start()
     load[3].wait()
     terms[...] = jnp.zeros_like(terms)
@@ -952,7 +960,8 @@
     @pl.loop(0, SEQ // QB)
     def _(i):
         rows = pl.ds(pl.multiple_of(i * QB, QB), QB)
-        df = (back_product(dy[rows, :], wo[...]) * grad_pre[rows, :].astype(F32)).astype(LOW)
+        here_dy = dy[pl.ds(pl.multiple_of(i * 2, 2), 2)].reshape(QB, D)
+        df = (back_product(here_dy, wo[...]) * grad_pre[rows, :].astype(F32)).astype(LOW)
         grad_pre[rows, :] = df
         terms[...] += jnp.sum(df.astype(F32), axis=0, keepdims=True)
 
@@ -960,7 +969,7 @@
         def half(which):
             @pl.loop(0, 2)
             def _(s):
-                rows = half_rows(which, s)
+                rows = pair_rows(which, s)
                 target[rows, :] = make(rows).astype(LOW)
 
         return half
@@ -989,31 +998,31 @@
     hidden_one, hidden_two, grad_pre, mat_qkv, mixed_all, totals, swap_parts, context, branch, result,
     hidden, grad_qkv, grad_fc, grad_proj, outputs, terms,
     ha, hb, wq, part_f, part_h, grads, mixed, acc_k, acc_v,
-    l1, s1, a1, l2, a2, l3, a3, l4, a4, pm, pk, px, sems,
+    l1, s1, a1, l2, l3, l4, pm, pk, px, sems,
 ):
-    spot = y, c, z, x = here()
+    spot = y, c, h, l, x = here()
     wires = Wires(sems)
     load = [wires.near(*both) for both in ((hidden_two, ha), (grad_pre, hb), (mixed_all, mixed), (mat_qkv, wq))]
     again = wires.near(hidden_one, ha)
     for copy in load:
         copy.start()
-    meet_tokens(team_peers(*spot) + grid_peers(*spot), spot, True)
+    meet_tokens(team_peers(*spot) + grid_peers(*spot), spot)
     swaps = [
         TeamSwap(
             wires,
-            lambda p, q, s=s: swap_parts.at[p * XN + q, s],
-            lambda p, q, s=s: grads.at[block_rows(p, s, q)],
+            lambda p, q, s=s: swap_parts.at[p * LN + q, s],
+            lambda p, q, s=s: grads.at[block_rows(p, q, s)],
             spot,
         )
         for s in range(2)
     ]
     for copy in swaps:
         copy.start()
-    fc = Scatter(wires, part_f, l2, a2, spot)
+    fc = Scatter(wires, part_f, l2, spot)
     first = TeamScatter(wires, part_h, l1, s1, a1, spot)
-    qkv = Scatter(wires, wq, l3, a3, spot)
+    qkv = Scatter(wires, wq, l3, spot)
     quarter = PROJ // 4
-    to_mate = wires.far(hb, pm, device(y, 1 - c, z, x))
+    to_mate = wires.far(hb, pm, device(y, 1 - c, h, l, x))
 
     def side(q):
         return pl.ds(pl.multiple_of(q * quarter, 16), quarter)
@@ -1022,12 +1031,12 @@
         at = pl.ds(pl.multiple_of((p * 2 + q) * quarter, quarter), quarter)
         return outer_sum(context[:, at], branch[...])
 
-    to_side = wires.far(pm.at[side(1 - x)], px, device(y, c, z, 1 - x))
-    proj = Scatter(wires, pk, l4, a4, spot)
-    move = Tokens(wires, result, outputs, spot, True)
+    to_side = wires.far(pm.at[side(1 - l)], px, device(y, c, h, 1 - l, x))
+    proj = Scatter(wires, pk, l4, spot)
+    move = Tokens(wires, result, outputs, spot)
     load[0].wait()
     load[1].wait()
-    outer_into(part_f, ha, hb)
+    outer_into(part_f, ha, lambda: hb[...])
     fc.start()
     again.start()
     for q in range(2):
@@ -1038,45 +1047,47 @@
         copy.finish()
     for head in range(SLOTS):
         attend_back(mixed, totals, grads, acc_k, acc_v, head)
-        if head == 1:
+        if head == 0:
             fc.step(1)
             to_mate.wait_recv()
-            pm[side(1 - x), :D] = (pm[side(1 - x), :D].astype(F32) + term(c, 1 - x)).astype(LOW)
-        if head == 5:
+            pm[side(1 - l), :D] = (pm[side(1 - l), :D].astype(F32) + term(c, 1 - l)).astype(LOW)
+        if head == 1:
+            to_side.start()
+        if head == 2:
             fc.step(2)
+        if head == 4:
+            fc.step(3)
+            move.start()
     load[3].wait()
 
     def half(which):
         @pl.loop(0, 2)
         def _(s):
-            rows = half_rows(which, s)
+            rows = pair_rows(which, s)
             part_h[rows, :] = back_product(mixed[rows, :], wq[...]).astype(LOW)
 
     half(1 - c)
     first.start()
     half(c)
     again.wait()
+    outer_into(wq, ha, lambda: mixed[...])
+    qkv.start()
     first.step(0)
     first.step(1)
-    to_side.start()
-    outer_into(wq, ha, mixed)
-    qkv.start()
-    fc.step(3)
-    terms[...] = jnp.sum(mixed[...].astype(F32), axis=0, keepdims=True)
-    move.start()
-    first.finish(hidden)
+    fc.finish(grad_fc)
     to_side.wait_recv()
     pk[...] = (
-        pm[side(x), :D].astype(F32) + term(c, x) + px[:, :D].astype(F32)
+        pm[side(l), :D].astype(F32) + term(c, l) + px[:, :D].astype(F32)
     ).astype(LOW)
     proj.start()
-    fc.finish(grad_fc)
     qkv.step(1)
+    terms[...] = jnp.sum(mixed[...].astype(F32), axis=0, keepdims=True)
     qkv.step(2)
+    proj.step(1)
     qkv.step(3)
-    proj.step(1)
     proj.step(2)
     proj.step(3)
+    first.finish(hidden)
     qkv.finish(grad_qkv)
     proj.finish(grad_proj)
     move.finish()
@@ -1085,43 +1096,48 @@
 
 
 def epilogue(
-    grads, units_qkv, units_fc, small, grad_in, got_qkv, got_fc, total, by_y, by_z, by_team, sems
+    grads, units_qkv, units_fc, small, grad_in, got_qkv, got_fc, total, by_team, own, by_rank, sems
 ):
-    spot = y, c, z, x = here()
+    spot = y, c, h, l, x = here()
     wires = Wires(sems)
-    meet_tokens(team_peers(*spot) + grid_peers(*spot), spot, True)
-    move = Tokens(wires, grads, grad_in, spot, True)
+    meet_tokens(team_peers(*spot) + team_twins(*spot), spot)
+    move = Tokens(wires, grads, grad_in, spot)
     qkv = TeamSwap(
-        wires, lambda p, q: units_qkv.at[p * XN + q], lambda p, q: got_qkv.at[p * XN + q], spot
+        wires, lambda p, q: units_qkv.at[p * LN + q], lambda p, q: got_qkv.at[p * LN + q], spot
     )
     fc = TeamSwap(
-        wires, lambda p, q: units_fc.at[p * XN + q], lambda p, q: got_fc.at[p * XN + q], spot
-    )
-    over = wires.far(small.at[1 - y], by_y, device(1 - y, c, z, x))
-    over.start()
-    move.start()
+        wires, lambda p, q: units_fc.at[p * LN + q], lambda p, q: got_fc.at[p * LN + q], spot
+    )
+    here_team = team_number(y, h, x)
+    ways = ((0, 0, 1), (1, 0, 0), (0, 1, 0), (1, 0, 1), (0, 1, 1), (1, 1, 0), (1, 1, 1))
+    twins = [
+        wires.far(
+            small.at[team_number(1 - y if a else y, 1 - h if b else h, 1 - x if d else x)],
+            by_team.at[i],
+            where,
+        )
+        for i, ((a, b, d), where) in enumerate(zip(ways, team_twins(*spot)))
+    ]
+    for copy in twins:
+        copy.start()
     qkv.start()
     fc.start()
-    over.wait()
-    by_y[...] = by_y[...] + small[y]
-    column = [
-        wires.far(by_y.at[lax.rem(z + k, ZN)], by_z.at[k - 1], device(y, c, lax.rem(z + k, ZN), x))
-        for k in range(1, ZN)
-    ]
-    for copy in column:
-        copy.start()
-    for copy in column:
+    move.start()
+    for copy in twins:
         copy.wait()
-    by_z[3] = by_y[z] + by_z[0] + by_z[1] + by_z[2]
+    summed = small[here_team]
+    for i in range(7):
+        summed = summed + by_team[i]
+    own[...] = summed
     team = [
-        wires.far(by_z.at[3, p * XN + q], by_team.at[i], device(y, p, z, q))
-        for i, (p, q) in enumerate(((c, 1 - x), (1 - c, 1 - x), (1 - c, x)))
+        wires.far(own.at[p * LN + q], by_rank.at[i], device(y, p, h, q, x))
+        for i, (p, q) in enumerate(((c, 1 - l), (1 - c, 1 - l), (1 - c, l)))
     ]
     for copy in team:
         copy.start()
     for copy in team:
         copy.wait()
-    total[...] = by_z[3, c * XN + x] + by_team[0] + by_team[1] + by_team[2]
+    total[...] = own[c * LN + l] + by_rank[0] + by_rank[1] + by_rank[2]
     qkv.finish()
     fc.finish()
     move.finish()
@@ -1228,15 +1244,15 @@
 
 
 def feature_order():
-    order = -np.ones((YN, ZN, PIECE), np.int32)
-    grid = np.arange(D).reshape(YN, CN, ZN, XN, 50).transpose(0, 2, 1, 3, 4)
-    order[:, :, :200] = grid.reshape(YN, ZN, 200)
+    order = -np.ones((8, PIECE), np.int32)
+    grid = np.arange(D).reshape(YN, CN, HN, LN, XN, 50).transpose(0, 2, 4, 1, 3, 5)
+    order[:, :200] = grid.reshape(8, 200)
     return order.reshape(-1)
 
 
 def context_order():
     natural = -np.ones(D, np.int32)
-    grid = np.arange(D).reshape(YN, CN, ZN, XN, 50).transpose(1, 3, 0, 2, 4).reshape(32, 50)
+    grid = np.arange(D).reshape(YN, CN, HN, LN, XN, 50).transpose(1, 3, 0, 2, 4, 5).reshape(32, 50)
     for block in range(32):
         natural[grid[block]] = block * PB + np.arange(50)
     order = -np.ones((4, HW), np.int32)
@@ -1247,8 +1263,7 @@
 
 
 def one_hot(order, size):
-    rows = lax.broadcasted_iota(jnp.int32, (size, order.shape[0]), 0)
-    return (rows == jnp.asarray(order)[None, :]).astype(LOW)
+    return (np.arange(size)[:, None] == order[None, :]).astype(LOW)
 
 
 def dot(left, right):
@@ -1260,37 +1275,43 @@
 
 
 def fast_shards(inputs, grad_out, w_qkv, w_proj, w_fc, w_out, smalls):
-    y, c, z, x = here()
-    rank = c * XN + x
-    to_wide = one_hot(feature_order(), D)
-    to_heads = one_hot(context_order(), PROJ)
+    y, c, h, l, x = here()
+    rank = c * LN + l
+    to_wide = jnp.asarray(one_hot(feature_order(), D))
+    to_proj = jnp.asarray(one_hot(context_order(), PROJ).T.copy())
 
     rows = w_qkv.reshape(50, 3, D)
     units_qkv = jnp.stack([head_parts(rows[:, i]) for i in range(3)], axis=2).reshape(4, 50, QW)
     units_qkv = pad_to(units_qkv, 1, 64)
-    units_fc = w_fc.reshape(50, YN, CN, ZN, XN, 200).transpose(2, 4, 0, 1, 3, 5)
-    units_fc = pad_to(pad_to(units_fc, 5, PIECE).reshape(4, 50, WIDE), 1, 64)
+    units_fc = w_fc.reshape(50, YN, CN, HN, LN, XN, 200).transpose(2, 4, 0, 1, 3, 5, 6)
+    units_fc = pad_to(pad_to(units_fc, 6, PIECE).reshape(4, 50, WIDE), 1, 64)
     small = pad_to(smalls, 0, 2048).reshape(16, 128)
     piece_out = pad_to(w_out.reshape(200, D), 0, PIECE)
     piece_proj = pad_to(w_proj.reshape(50, D), 0, PB)
-    tokens, got_qkv, got_fc, smalls_all, mat_out, mat_proj = call(
+    tokens, smalls_all, mat_qkv, mat_proj, piece_fc = call(
         prologue, "prologue", 1,
-        (inputs.reshape(MICRO, BLK, D), units_qkv, units_fc, small, piece_out, piece_proj),
+        (inputs.reshape(MICRO, BLK, D), units_qkv, units_fc, small, piece_proj),
         [
-            ((2, BLK, D), LOW), ((4, 64, QW), LOW), ((4, 64, WIDE), LOW),
-            ((YN, ZN, 4, 16, 128), LOW), ((YN, ZN, PIECE, D), LOW), ((4, YN, ZN, PB, D), LOW),
+            ((2, BLK, D), LOW), ((8, 4, 16, 128), LOW), ((8, PIECE, QW), LOW), ((4, 8, PB, D), LOW),
+            ((PIECE, WIDE), LOW),
         ],
-        [ANY] * 6, [ANY] * 6, [], 3 * TEAM_SWAP_SEMS + TOKENS_SEMS + 2 * GATHER_SEMS + 14,
-    )
-    mat_out = mat_out.reshape(WIDE, D)
+        [VM] * 5, [ANY] * 4 + [VM],
+        [
+            pltpu.VMEM((4, 64, QW), LOW), pltpu.VMEM((4, 64, WIDE), LOW),
+            pltpu.VMEM((PIECE, QW), F32), pltpu.VMEM((PIECE, WIDE), F32), pltpu.VMEM((PIECE, QW), LOW),
+            pltpu.VMEM((PB, D), LOW),
+        ],
+        SMALLS_SEMS + 2 * TEAM_SWAP_SEMS + TOKENS_SEMS + 3 * GATHER_SEMS + 6,
+    )
+    mat_qkv = mat_qkv.reshape(WIDE, QW)
     mat_proj = mat_proj.reshape(PROJ, D)
-    small = smalls_all.reshape(YN, ZN, CN, XN, 2048)[..., :600].transpose(0, 2, 1, 3, 4)
+    small = smalls_all.reshape(YN, HN, XN, CN, LN, 2048)[..., :600].transpose(0, 3, 1, 4, 2, 5)
     small = small.reshape(-1).astype(F32)
     gain1, shift1, bias_q, bias_v, bias_proj, gain2, shift2 = [segment(small, i) for i in range(7)]
-    bias_fc = small[7 * D : 7 * D + FF].reshape(YN, CN, ZN, XN, 200)
+    bias_fc = small[7 * D : 7 * D + FF].reshape(YN, CN, HN, LN, XN, 200)
     bias_fc = lax.dynamic_index_in_dim(bias_fc, c, 1, keepdims=False)
-    bias_fc = lax.dynamic_index_in_dim(bias_fc, x, 2, keepdims=False)
-    bias_fc = pad_to(bias_fc, 2, PIECE).reshape(WIDE)
+    bias_fc = lax.dynamic_index_in_dim(bias_fc, l, 2, keepdims=False)
+    bias_fc = pad_to(bias_fc, 3, PIECE).reshape(WIDE)
     bias_out = small[7 * D + FF :]
     bias_qkv = jnp.stack(
         [head_parts(bias_q[None]), jnp.zeros((4, 1, HW)), head_parts(bias_v[None])], axis=1
@@ -1301,34 +1322,32 @@
     tokens = tokens_low.astype(F32)
     hidden_one, ln1_pull = jax.vjp(layer_norm, tokens, gain1, shift1)
     hidden_one = dot(hidden_one.astype(LOW), to_wide).astype(LOW)
-    piece_qkv = pad_to(got_qkv[:, :50].reshape(200, QW), 0, PIECE)
-    piece_fc = pad_to(got_fc[:, :50].reshape(200, WIDE), 0, PIECE)
     (
-        hidden_one, cotangent, grad_all, mat_qkv, mat_fc, hidden_two, mixed, totals, context, resid,
+        hidden_one, cotangent, grad_all, mat_fc, mat_out, hidden_two, mixed, totals, context, resid,
     ) = call(
         forward, "forward", 2,
         (
-            hidden_one.reshape(2, BLK, WIDE), grad_out.reshape(MICRO, BLK, D), piece_qkv, piece_fc,
-            mat_proj, to_heads.T, to_wide, tokens_low, bias_qkv.reshape(1, QW),
+            hidden_one.reshape(2, BLK, WIDE), grad_out.reshape(MICRO, BLK, D), piece_fc, piece_out,
+            mat_qkv, mat_proj, to_proj, to_wide, tokens_low, bias_qkv.reshape(1, QW),
             bias_proj.reshape(1, D), gain2.reshape(1, D), shift2.reshape(1, D),
         ),
         [
-            ((2, 2, 2, BLK, WIDE), LOW), ((2, BLK, D), LOW), ((2, 2, 2, BLK, D), LOW),
-            ((YN, ZN, PIECE, QW), LOW), ((YN, ZN, PIECE, WIDE), LOW), ((2, 2, 2, BLK, WIDE), LOW),
-            ((SEQ, QW), LOW), ((SEQ, SLOTS), F32), ((2 * BLK, PROJ), LOW), ((2 * BLK, D), F32),
+            ((8, BLK, WIDE), LOW), ((2, BLK, D), LOW), ((8, BLK, D), LOW),
+            ((8, PIECE, WIDE), LOW), ((8, PIECE, D), LOW),
+            ((8, BLK, WIDE), LOW), ((SEQ, QW), LOW), ((SEQ, SLOTS), F32), ((2 * BLK, PROJ), LOW),
+            ((2 * BLK, D), F32),
         ],
-        [ANY] * 7 + [VM] * 5, [ANY] * 6 + [VM] * 4,
+        [VM] * 4 + [ANY] * 4 + [VM] * 5, [VM, VM] + [ANY] * 4 + [VM] * 4,
         [
-            pltpu.VMEM((2, 2, 2, BLK, WIDE), LOW), pltpu.VMEM((YN, ZN, PIECE, QW), LOW),
-            pltpu.VMEM((PROJ, D), LOW), pltpu.VMEM((4 * HW, PROJ), LOW), pltpu.VMEM((D, WIDE), LOW),
-            pltpu.VMEM((SEQ, HW), LOW), pltpu.VMEM((4, 2, BLK, HW), LOW), pltpu.VMEM((2, BLK, WIDE), LOW),
+            pltpu.VMEM((WIDE, QW), LOW), pltpu.VMEM((PROJ, D), LOW), pltpu.VMEM((4 * HW, PROJ), LOW),
+            pltpu.VMEM((D, WIDE), LOW), pltpu.VMEM((SEQ, HW), LOW), pltpu.VMEM((4, 2, BLK, HW), LOW),
+            pltpu.VMEM((2, BLK, WIDE), LOW),
         ],
-        3 * TEAM_GATHER_SEMS + TOKENS_SEMS + 2 * GATHER_SEMS + 2 * TEAM_SWAP_SEMS + 5,
+        3 * TEAM_GATHER_SEMS + TOKENS_SEMS + 2 * GATHER_SEMS + 2 * TEAM_SWAP_SEMS + 4,
     )
     hidden_one = hidden_one.reshape(SEQ, WIDE)
     hidden_two = hidden_two.reshape(SEQ, WIDE)
-    grad_all = grad_all.reshape(SEQ, D)
-    mat_qkv = mat_qkv.reshape(WIDE, QW)
+    mat_out = mat_out.reshape(WIDE, D)
     mat_fc = mat_fc.reshape(WIDE, WIDE)
     _, ln2_pull = jax.vjp(layer_norm, resid, gain2, shift2)
     result, grad_hidden_two, grad_out_w, grad_pre, fc_terms = call(
@@ -1340,7 +1359,7 @@
         ],
         [ANY] * 4 + [VM], [VM] * 5,
         [
-            pltpu.VMEM((SEQ, WIDE), LOW), pltpu.VMEM((SEQ, D), LOW), pltpu.VMEM((WIDE, WIDE), LOW),
+            pltpu.VMEM((SEQ, WIDE), LOW), pltpu.VMEM((8, BLK, D), LOW), pltpu.VMEM((WIDE, WIDE), LOW),
             pltpu.VMEM((WIDE, D), LOW), pltpu.VMEM((SEQ, WIDE), LOW), pltpu.VMEM((SEQ, D), LOW),
             pltpu.VMEM((SEQ, WIDE), LOW), pltpu.VMEM((WIDE, D), LOW),
         ]
@@ -1356,7 +1375,7 @@
     grad_resid = grad_full + grad_ln_two
     grad_branch = grad_resid.astype(LOW)
     grad_context = back_product(grad_branch, mat_proj).astype(LOW)
-    grad_context = dot(grad_context, to_heads).astype(LOW)
+    grad_context = back_product(grad_context, to_proj).astype(LOW)
     grad_context = jnp.stack(
         [grad_context[:, r * HW : (r + 1) * HW] for r in range(4)]
     ).reshape(4, 2, BLK, HW)
@@ -1370,7 +1389,7 @@
             ((2, BLK, WIDE), F32), ((PIECE, QW), LOW), ((PIECE, WIDE), LOW), ((PB, D), F32),
             ((2, BLK, D), LOW), ((1, QW), F32),
         ],
-        [ANY] * 5 + [VM, ANY, VM, VM, ANY], [VM, VM, VM, VM, ANY, VM],
+        [ANY] * 5 + [VM, ANY, VM, VM, VM], [VM, VM, VM, VM, ANY, VM],
         [
             pltpu.VMEM((SEQ, WIDE), LOW), pltpu.VMEM((SEQ, WIDE), LOW), pltpu.VMEM((WIDE, QW), LOW),
             pltpu.VMEM((WIDE, WIDE), LOW), pltpu.VMEM((SEQ, WIDE), LOW), pltpu.VMEM((SEQ, HW), LOW), pltpu.VMEM((SEQ, QW), LOW),
@@ -1393,10 +1412,9 @@
     mine = (jnp.arange(4) == rank).astype(F32)[:, None, None]
     grad_bq = head_join(mine * terms[0][None, None])[0]
     grad_bv = head_join(mine * terms[2][None, None])[0]
-    fc_terms = fc_terms.reshape(YN, 1, ZN, 1, PIECE)[..., :200]
-    spot = (jnp.arange(CN) == c)[None, :, None, None, None] & (jnp.arange(XN) == x)[
-        None, None, None, :, None
-    ]
+    fc_terms = fc_terms.reshape(YN, 1, HN, 1, XN, PIECE)[..., :200]
+    spot = (jnp.arange(CN) == c)[:, None, None] & (jnp.arange(LN) == l)
+    spot = spot[None, ..., None, None]
     grad_fc_bias = jnp.where(spot, fc_terms, 0.0).reshape(-1)
     front = jnp.concatenate([grad_gain_one, grad_shift_one, grad_bq, grad_bv])
     tail = jnp.concatenate(
@@ -1406,22 +1424,25 @@
         ]
     )
     small = jnp.concatenate([front.reshape(32, 200), tail.reshape(32, 400)], axis=1)
-    small = pad_to(small, 1, 1024).reshape(YN, CN, ZN, XN, 8, 128).transpose(0, 2, 1, 3, 4, 5)
+    small = pad_to(small, 1, 1024).reshape(YN, CN, HN, LN, XN, 8, 128).transpose(0, 2, 4, 1, 3, 5, 6)
     units_qkv = pad_to(grad_qkv[:200].reshape(4, 50, QW), 1, 64)
     units_fc = pad_to(grad_fc[:200].reshape(4, 50, WIDE), 1, 64)
     grad_in, got_qkv, got_fc, total = call(
         epilogue, "epilogue", 8,
-        (grad_in.reshape(2, BLK, D), units_qkv, units_fc, small.reshape(YN, ZN, 4, 8, 128)),
+        (grad_in.reshape(2, BLK, D), units_qkv, units_fc, small.reshape(8, 4, 8, 128)),
         [((MICRO, BLK, D), LOW), ((4, 64, QW), LOW), ((4, 64, WIDE), LOW), ((8, 128), F32)],
-        [ANY, ANY, ANY, VM], [ANY, ANY, ANY, VM],
-        [pltpu.VMEM((ZN, 4, 8, 128), F32), pltpu.VMEM((4, 4, 8, 128), F32), pltpu.VMEM((3, 8, 128), F32)],
-        2 * TEAM_SWAP_SEMS + TOKENS_SEMS + 14,
+        [VM] * 4, [ANY, ANY, ANY, VM],
+        [
+            pltpu.VMEM((7, 4, 8, 128), F32), pltpu.VMEM((4, 8, 128), F32),
+            pltpu.VMEM((3, 8, 128), F32),
+        ],
+        2 * TEAM_SWAP_SEMS + TOKENS_SEMS + 20,
     )
     parts = got_qkv[:, :50].reshape(4, 50, 3, HW)
     grad_qkv = jnp.stack([head_join(parts[:, :, i]) for i in range(3)], axis=1)
     grad_qkv = grad_qkv.astype(F32).reshape(-1)
-    grad_fc = got_fc[:, :50].reshape(CN, XN, 50, YN, ZN, PIECE)[..., :200]
-    grad_fc = grad_fc.transpose(2, 3, 0, 4, 1, 5).astype(F32).reshape(-1)
+    grad_fc = got_fc[:, :50].reshape(CN, LN, 50, YN, HN, XN, PIECE)[..., :200]
+    grad_fc = grad_fc.transpose(2, 3, 0, 4, 1, 5, 6).astype(F32).reshape(-1)
     total = total.reshape(-1)
     return (
         outputs[:, None],

time: 662 us -> 616 us (0.931)
  Pallas kernels: 552 us -> 512 us
  other arithmetic: 22.8 us -> 13.8 us
  matrix products: 17.8 us -> 25.6 us
    pallas_call x5, Pallas kernels: 552 us -> 512 us  [call(): pl.pallas_call(body, out_shape=[jax.ShapeDtypeStruct(s, d) for s, d in ou...]
    dot_general x2 -> x3, matrix products: 6.33 us -> 20.3 us  [back_product(): lax.dot_general(grad, weight, (((1,), (1,)), ((), ())), preferred_element...]
    convert_element_type x2 -> x0, other arithmetic: 8.96 us -> none  [one_hot(): return (rows == jnp.asarray(order)[None, :]).astype(LOW)]
where the time goes in v5:
time: 616 us; the launch traced here: 609 us
  Pallas kernels  512 us (83%)
  local copies, waits for them, and re-layouts  55.4 us (9%)
  matrix products  25.6 us (4%)
  other arithmetic  13.8 us (2%)
    pallas_call x5, Pallas kernels, call(): pl.pallas_call(body, out_shape=[jax.ShapeDtypeStruct(s, d) for s, d in ou...  512 us
    dot_general x3, matrix products, back_product(): lax.dot_general(grad, weight, (((1,), (1,)), ((), ())), preferred_element...  20.3 us

profile of v5, /device:TPU:0, one launch (start us, length us, event | category | flops | bytes accessed | tf_op | source)
XLA Modules:
  0.0 609.0 jit_solution(6299738553307804371)
XLA Ops:
  0.9 1.3 pad_bitcast_fusion.9.small
  2.1 1.1 reshape.439
  3.2 0.7 pad.98.piece_proj
  3.9 1.9 reshape.434
  5.9 0.7 fusion.20
  7.4 0.5 copy.101
  8.0 0.7 reshape.478
  8.7 0.9 pad.94.units_qkv
  9.6 0.5 reshape.444
  10.2 0.9 pad.99.piece_out
  11.1 2.4 reshape.436
  13.5 0.6 copy.123
  14.1 0.7 pad.95.clone
  14.8 1.1 reshape.479
  15.9 1.0 pad.96.units_fc
  16.9 1.2 copy.80
  18.2 1.2 copy.88
  19.4 99.1 %prologue.1 = (bf16[2,128,1600]{2,1,0:T(8,128)(2,1)}, bf16[8,4,16,128]{3,2,1,0:T(8,128)(2,1)}, bf16[8,208,1344]{2,1,0:T(8,128)(2,1)}, bf16[4,8,64,1600]{3,2,1,0:T(8,128)(2,1)}, bf16[208,1664]{1,0:T(8,128)(2,1)}) custom-call(bf16[2,128,1600]{2,1,0:T(8,128)(2,1)} %bitcast.210, bf16[4,64,1344]{2,1,0:T(8,128)(2,1)} %pad.94.units_qkv, ...), custom_call_target="tpu_custom_call" | custom-call | tf_op jit(solution)/shard_map/prologue/pallas_call | solution.py:401
  118.6 1.0 reshape.441
  119.6 1.4 convert_reduce_fusion
  121.0 0.4 fusion.1
  121.9 0.7 reshape_reshape.7.bias_fc
  122.9 0.7 reshape_reshape.6.bias_qkv
  123.6 0.6 reshape.449.shift2
  124.2 0.6 reshape.447.bias_proj
  124.8 0.6 reshape.448.gain2
  125.4 5.3 convolution_convert_fusion.2
  130.6 145.5 %forward.1 = (bf16[8,128,1664]{2,1,0:T(8,128)(2,1)}, bf16[2,128,1600]{2,1,0:T(8,128)(2,1)}, bf16[8,128,1600]{2,1,0:T(8,128)(2,1)}, bf16[8,208,1664]{2,1,0:T(8,12...) custom-call(bf16[2,128,1664]{2,1,0:T(8,128)(2,1)} %bitcast.222, ...), custom_call_target="tpu_custom_call" | custom-call | tf_op jit(solution)/shard_map/forward/pallas_call | solution.py:401
  276.1 96.1 %feed_forward.1 = (f32[2,128,1600]{2,1,0:T(8,128)}, f32[2,128,1664]{2,1,0:T(8,128)}, f32[208,1600]{1,0:T(8,128)}, bf16[1024,1664]{1,0:T(8,128)(2,1)}, f32[1,1664]{1,0:T(1,128)}) custom-call(bf16[1024,1664]{1,0:T(8,128)(2,1)} %bitcast.203, bf16[8,128,1600]{2,1,0:T(8,128)(2,1)} %get-tuple-element.45.grad_all, bf16[1664,1664]{1,0:T(8,128)(2,1)} %bitcast.207, ...), custom_call_target="tpu_custom_call" | custom-call | tf_op jit(solution)/shard_map/feed_forward/pallas_call | solution.py:401
  373.8 1.5 convert_element_type.124
  375.4 5.5 fusion.28
  381.0 1.7 reshape.469
  382.7 1.8 copy.89
  384.5 0.5 multiply_reduce_fusion
  385.0 0.9 copy-done.9
  385.9 1.5 fusion.17
  387.8 0.8 copy-done.3
  388.6 9.4 %convolution_convert_fusion = bf16[256,1792]{1,0:T(8,128)(2,1)S(1)} fusion(bf16[1792,2048]{1,0:T(8,128)(2,1)} %constant.103.clone.to_proj, bf16[256,1600]{1,0:T(8,128)(2,1)S(1)} %get-tuple-element.105.branch, bf16[2048,1600]{1,0:T(8,128)(2,1)} %bitcast.206), kind=kOutput, calls=%fused_computation | convolution fusion | flops 3557752832 | bytes 15630336 | tf_op jit(solution)/shard_map/dot_general | solution.py:73
  398.6 1.1 pad_maximum_fusion.swap_parts
  399.7 135.5 %backward.1 = (f32[2,128,1664]{2,1,0:T(8,128)}, bf16[208,1344]{1,0:T(8,128)(2,1)}, bf16[208,1664]{1,0:T(8,128)(2,1)}, f32[64,1600]{1,0:T(8,128)}, bf16[2,128,1600]{2,1,0:T(8,128)(2,1)}, /*index=5*/f32[1,1344]{1,0:T(1,128)}) custom-call(bf16[1024,1664]{1,0:T(8,128)(2,1)} %bitcast.211, bf16[1024,1664]{1,0:T(8,128)(2,1)} %bitcast.204, ...), custom_call_target="tpu_custom_call" | custom-call | tf_op jit(solution)/shard_map/backward/pallas_call | solution.py:401
  535.2 2.2 copy.98
  537.4 0.7 fusion.27
  538.7 0.9 reshape.465
  539.9 0.9 pad.107.units_qkv
  541.0 1.0 pad.108.units_fc
  542.0 0.6 copy-done.8
  542.7 5.4 fusion.29
  548.2 1.8 copy.90
  550.0 0.4 multiply_reduce_fusion.2
  550.5 0.8 multiply_reduce_fusion.1
  551.6 3.1 add_convert_fusion
  554.8 0.7 copy.93
  555.5 36.0 %epilogue.1 = (bf16[2,128,1600]{2,1,0:T(8,128)(2,1)}, bf16[4,64,1344]{2,1,0:T(8,128)(2,1)}, bf16[4,64,1664]{2,1,0:T(8,128)(2,1)}, f32[8,128]{1,0:T(8,128)}) custom-call(bf16[2,128,1600]{2,1,0:T(8,128)(2,1)} %bitcast.209, bf16[4,64,1344]{2,1,0:T(8,128)(2,1)} %pad.107.units_qkv, bf16[4,64,1664]{2,1,0:T(8,128)(2,1)} %pad.108.units_fc, f32[8,4,8,128]{3,2,1,0:T(8,128)} %bitcast.228), custom_call_target="tpu_custom_call" | custom-call | tf_op jit(solution)/shard_map/epilogue/pallas_call | solution.py:401
  591.5 1.2 slice.369
  592.8 1.3 slice.370
  594.1 1.1 slice.343
  595.5 0.8 reshape.464
  596.2 0.8 fusion.19
  598.4 1.8 reshape.474
  600.3 1.4 reshape.480
  601.7 0.9 convert_bitcast_fusion
  602.6 0.8 copy.97
  603.4 3.7 reshape.476
  607.2 1.6 copy.99
  (160 shorter events, 7.2 us)
Async XLA Ops:
  8.0 1.7 copy-start.15
  8.7 2.4 copy-start.16
  14.8 2.1 copy-start.12
  15.9 2.2 copy-start.13
  118.5 2.4 copy-start
  276.1 96.2 %copy-start.2 = (f32[256,1600]{1,0:T(8,128)S(1)}, f32[256,1600]{1,0:T(8,128)}, u32[]{:S(2)}) copy-start(f32[256,1600]{1,0:T(8,128)} %get-tuple-element.53) | copy-start | bytes 4915204
  372.3 0.7 copy-start.20
  372.3 1.2 copy-start.4
  375.4 5.5 copy-start.10
  384.5 1.5 copy-start.9
  385.9 1.5 copy-start.5
  387.4 1.2 copy-start.3
  388.6 9.5 %copy-start.7 = (bf16[256,1600]{1,0:T(8,128)(2,1)}, bf16[256,1600]{1,0:T(8,128)(2,1)S(1)}, u32[]{:S(2)}) copy-start(bf16[256,1600]{1,0:T(8,128)(2,1)S(1)} %get-tuple-element.105.branch) | copy-start | bytes 2457604
  535.2 3.5 copy-start.19
  535.2 4.5 copy-start.18
  539.7 1.1 copy-start.17
  540.8 1.8 copy-start.8
  548.1 1.9 copy-start.1
  550.5 1.2 copy-start.6
  598.4 1.9 copy-start.14
  603.4 3.7 copy-start.11

commit v6 on v5

--- a/solution.py
+++ b/solution.py
@@ -996,9 +996,10 @@
 
 def backward(
     hidden_one, hidden_two, grad_pre, mat_qkv, mixed_all, totals, swap_parts, context, branch, result,
-    hidden, grad_qkv, grad_fc, grad_proj, outputs, terms,
+    tokens, grad_resid, gain1, to_wide,
+    units_qkv, got_fc, grad_proj, outputs, grad_in, terms, norms,
     ha, hb, wq, part_f, part_h, grads, mixed, acc_k, acc_v,
-    l1, s1, a1, l2, l3, l4, pm, pk, px, sems,
+    l1, s1, a1, l2, l3, l4, pm, px, hidden, grad_low, wide_fc, wide_qkv, units_fc, sems,
 ):
     spot = y, c, h, l, x = here()
     wires = Wires(sems)
@@ -1032,8 +1033,14 @@
         return outer_sum(context[:, at], branch[...])
 
     to_side = wires.far(pm.at[side(1 - l)], px, device(y, c, h, 1 - l, x))
-    proj = Scatter(wires, pk, l4, spot)
+    proj = Scatter(wires, px, l4, spot)
     move = Tokens(wires, result, outputs, spot)
+    back = Tokens(wires, grad_low, grad_in, spot)
+    swap_fc = TeamSwap(
+        wires, lambda p, q: units_fc.at[p * LN + q], lambda p, q: got_fc.at[p * LN + q], spot
+    )
+    spread = part_f.at[pl.ds(0, D)]
+    load_wide = wires.near(to_wide, spread)
     load[0].wait()
     load[1].wait()
     outer_into(part_f, ha, lambda: hb[...])
@@ -1074,39 +1081,59 @@
     qkv.start()
     first.step(0)
     first.step(1)
-    fc.finish(grad_fc)
+    fc.finish(wide_fc)
+    load_wide.start()
+    split_units(wide_fc, units_fc)
+    swap_fc.start()
     to_side.wait_recv()
-    pk[...] = (
-        pm[side(l), :D].astype(F32) + term(c, l) + px[:, :D].astype(F32)
-    ).astype(LOW)
+    px[:, :D] = (pm[side(l), :D].astype(F32) + term(c, l) + px[:, :D].astype(F32)).astype(LOW)
     proj.start()
     qkv.step(1)
     terms[...] = jnp.sum(mixed[...].astype(F32), axis=0, keepdims=True)
+    load_wide.wait()
     qkv.step(2)
     proj.step(1)
+    first.finish(hidden)
+    grad = back_product(hidden[...].reshape(2 * BLK, WIDE).astype(LOW), spread[...])
+    grad, norms[0:1, :], norms[1:2, :] = norm_back(tokens[...].astype(F32), gain1[...], grad)
+    grad_low[...] = (grad_resid[...] + grad).astype(LOW).reshape(2, BLK, D)
+    back.start()
     qkv.step(3)
     proj.step(2)
     proj.step(3)
-    first.finish(hidden)
-    qkv.finish(grad_qkv)
+    qkv.finish(wide_qkv)
+    split_units(wide_qkv, units_qkv)
     proj.finish(grad_proj)
+    swap_fc.finish()
     move.finish()
+    back.finish()
     to_mate.wait_send()
     to_side.wait_send()
 
 
-def epilogue(
-    grads, units_qkv, units_fc, small, grad_in, got_qkv, got_fc, total, by_team, own, by_rank, sems
-):
+def split_units(wide, units):
+    wide[PIECE:, :] = jnp.zeros((224 - PIECE, wide.shape[1]), F32)
+    for k in range(4):
+        units[k] = wide[k * 50 : k * 50 + 64, :].astype(LOW)
+
+
+def norm_back(values, gain, grad):
+    center = values - jnp.mean(values, axis=1, keepdims=True)
+    scale = lax.rsqrt(jnp.mean(center * center, axis=1, keepdims=True) + EPS)
+    unit = center * scale
+    grad_gain = jnp.sum(grad * unit, axis=0, keepdims=True)
+    grad_shift = jnp.sum(grad, axis=0, keepdims=True)
+    grad = grad * gain
+    inner = jnp.mean(grad * unit, axis=1, keepdims=True)
+    return scale * (grad - jnp.mean(grad, axis=1, keepdims=True) - unit * inner), grad_gain, grad_shift
+
+
+def epilogue(units_qkv, small, got_qkv, total, by_team, own, by_rank, sems):
     spot = y, c, h, l, x = here()
     wires = Wires(sems)
-    meet_tokens(team_peers(*spot) + team_twins(*spot), spot)
-    move = Tokens(wires, grads, grad_in, spot)
+    meet(team_peers(*spot) + team_twins(*spot))
     qkv = TeamSwap(
         wires, lambda p, q: units_qkv.at[p * LN + q], lambda p, q: got_qkv.at[p * LN + q], spot
-    )
-    fc = TeamSwap(
-        wires, lambda p, q: units_fc.at[p * LN + q], lambda p, q: got_fc.at[p * LN + q], spot
     )
     here_team = team_number(y, h, x)
     ways = ((0, 0, 1), (1, 0, 0), (0, 1, 0), (1, 0, 1), (0, 1, 1), (1, 1, 0), (1, 1, 1))
@@ -1121,8 +1148,6 @@
     for copy in twins:
         copy.start()
     qkv.start()
-    fc.start()
-    move.start()
     for copy in twins:
         copy.wait()
     summed = small[here_team]
@@ -1139,8 +1164,6 @@
         copy.wait()
     total[...] = own[c * LN + l] + by_rank[0] + by_rank[1] + by_rank[2]
     qkv.finish()
-    fc.finish()
-    move.finish()
 
 
 QB = 256
@@ -1320,7 +1343,7 @@
 
     tokens_low = tokens.reshape(2 * BLK, D)
     tokens = tokens_low.astype(F32)
-    hidden_one, ln1_pull = jax.vjp(layer_norm, tokens, gain1, shift1)
+    hidden_one = layer_norm(tokens, gain1, shift1)
     hidden_one = dot(hidden_one.astype(LOW), to_wide).astype(LOW)
     (
         hidden_one, cotangent, grad_all, mat_fc, mat_out, hidden_two, mixed, totals, context, resid,
@@ -1379,34 +1402,34 @@
     grad_context = jnp.stack(
         [grad_context[:, r * HW : (r + 1) * HW] for r in range(4)]
     ).reshape(4, 2, BLK, HW)
-    grad_hidden_one, grad_qkv, grad_fc, grad_proj, outputs, terms = call(
+    units_qkv, got_fc, grad_proj, outputs, grad_in, terms, norms = call(
         backward, "backward", 7,
         (
             hidden_one, hidden_two, grad_pre, mat_qkv, mixed, totals, grad_context, context,
-            grad_branch, result.reshape(2, BLK, D),
+            grad_branch, result.reshape(2, BLK, D), tokens_low, grad_resid, gain1.reshape(1, D),
+            to_wide,
         ),
         [
-            ((2, BLK, WIDE), F32), ((PIECE, QW), LOW), ((PIECE, WIDE), LOW), ((PB, D), F32),
-            ((2, BLK, D), LOW), ((1, QW), F32),
+            ((4, 64, QW), LOW), ((4, 64, WIDE), LOW), ((PB, WIDE), F32), ((2, BLK, D), LOW),
+            ((2, BLK, D), LOW), ((1, QW), F32), ((2, D), F32),
         ],
-        [ANY] * 5 + [VM, ANY, VM, VM, VM], [VM, VM, VM, VM, ANY, VM],
+        [ANY] * 5 + [VM, ANY] + [VM] * 6 + [ANY], [VM, ANY, VM, ANY, ANY, VM, VM],
         [
             pltpu.VMEM((SEQ, WIDE), LOW), pltpu.VMEM((SEQ, WIDE), LOW), pltpu.VMEM((WIDE, QW), LOW),
-            pltpu.VMEM((WIDE, WIDE), LOW), pltpu.VMEM((SEQ, WIDE), LOW), pltpu.VMEM((SEQ, HW), LOW), pltpu.VMEM((SEQ, QW), LOW),
+            pltpu.VMEM((WIDE, WIDE), LOW), pltpu.VMEM((SEQ, WIDE), LOW),
+            pltpu.VMEM((SEQ, HW), LOW), pltpu.VMEM((SEQ, QW), LOW),
             pltpu.VMEM((SEQ, HEAD), F32), pltpu.VMEM((SEQ, HEAD), F32),
         ]
         + team_scatter_scratch(WIDE) + scatter_scratch(PIECE, WIDE) + scatter_scratch(PIECE, QW)
-        + scatter_scratch(PB, D)
+        + scatter_scratch(PB, WIDE)
         + [
-            pltpu.VMEM((PROJ // 2, WIDE), LOW), pltpu.VMEM((PROJ // 4, D), LOW),
-            pltpu.VMEM((PROJ // 4, WIDE), LOW),
+            pltpu.VMEM((PROJ // 2, WIDE), LOW), pltpu.VMEM((PROJ // 4, WIDE), LOW),
+            pltpu.VMEM((2, BLK, WIDE), F32), pltpu.VMEM((2, BLK, D), LOW),
+            pltpu.VMEM((224, WIDE), F32), pltpu.VMEM((224, QW), F32), pltpu.VMEM((4, 64, WIDE), LOW),
         ],
-        TEAM_SCATTER_SEMS + 3 * SCATTER_SEMS + TOKENS_SEMS + 2 * TEAM_SWAP_SEMS + 9,
-    )
-    grad_hidden_one = back_product(grad_hidden_one.reshape(2 * BLK, WIDE).astype(LOW), to_wide)
-    grad_ln_one, grad_gain_one, grad_shift_one = ln1_pull(grad_hidden_one)
-    grad_in = (grad_resid + grad_ln_one).astype(LOW)
-    grad_proj = grad_proj[:50].reshape(-1)
+        TEAM_SCATTER_SEMS + 3 * SCATTER_SEMS + 2 * TOKENS_SEMS + 3 * TEAM_SWAP_SEMS + 10,
+    )
+    grad_proj = grad_proj[:50, :D].reshape(-1)
 
     terms = terms.reshape(3, HW)
     mine = (jnp.arange(4) == rank).astype(F32)[:, None, None]
@@ -1416,7 +1439,7 @@
     spot = (jnp.arange(CN) == c)[:, None, None] & (jnp.arange(LN) == l)
     spot = spot[None, ..., None, None]
     grad_fc_bias = jnp.where(spot, fc_terms, 0.0).reshape(-1)
-    front = jnp.concatenate([grad_gain_one, grad_shift_one, grad_bq, grad_bv])
+    front = jnp.concatenate([norms.reshape(-1), grad_bq, grad_bv])
     tail = jnp.concatenate(
         [
             ones_row(grad_branch), grad_gain_two, grad_shift_two, grad_fc_bias,
@@ -1425,18 +1448,15 @@
     )
     small = jnp.concatenate([front.reshape(32, 200), tail.reshape(32, 400)], axis=1)
     small = pad_to(small, 1, 1024).reshape(YN, CN, HN, LN, XN, 8, 128).transpose(0, 2, 4, 1, 3, 5, 6)
-    units_qkv = pad_to(grad_qkv[:200].reshape(4, 50, QW), 1, 64)
-    units_fc = pad_to(grad_fc[:200].reshape(4, 50, WIDE), 1, 64)
-    grad_in, got_qkv, got_fc, total = call(
-        epilogue, "epilogue", 8,
-        (grad_in.reshape(2, BLK, D), units_qkv, units_fc, small.reshape(8, 4, 8, 128)),
-        [((MICRO, BLK, D), LOW), ((4, 64, QW), LOW), ((4, 64, WIDE), LOW), ((8, 128), F32)],
-        [VM] * 4, [ANY, ANY, ANY, VM],
+    got_qkv, total = call(
+        epilogue, "epilogue", 8, (units_qkv, small.reshape(8, 4, 8, 128)),
+        [((4, 64, QW), LOW), ((8, 128), F32)],
+        [VM] * 2, [ANY, VM],
         [
             pltpu.VMEM((7, 4, 8, 128), F32), pltpu.VMEM((4, 8, 128), F32),
             pltpu.VMEM((3, 8, 128), F32),
         ],
-        2 * TEAM_SWAP_SEMS + TOKENS_SEMS + 20,
+        TEAM_SWAP_SEMS + 20,
     )
     parts = got_qkv[:, :50].reshape(4, 50, 3, HW)
     grad_qkv = jnp.stack([head_join(parts[:, :, i]) for i in range(3)], axis=1)

time: 616 us -> 600 us (0.974)
  local copies, waits for them, and re-layouts: 55.4 us -> 48.9 us
    dot_general x3 -> x2, matrix products: 20.3 us -> 14.9 us  [back_product(): lax.dot_general(grad, weight, (((1,), (1,)), ((), ())), preferred_element...]
where the time goes in v6:
time: 600 us; the launch traced here: 593 us
  Pallas kernels  512 us (85%)
  local copies, waits for them, and re-layouts  48.9 us (8%)
  matrix products  20.2 us (3%)
  other arithmetic  10.5 us (2%)
    pallas_call x5, Pallas kernels, call(): pl.pallas_call(body, out_shape=[jax.ShapeDtypeStruct(s, d) for s, d in ou...  512 us
    dot_general x2, matrix products, back_product(): lax.dot_general(grad, weight, (((1,), (1,)), ((), ())), preferred_element...  14.9 us

profile of v6, /device:TPU:0, one launch (start us, length us, event | category | flops | bytes accessed | tf_op | source)
XLA Modules:
  0.0 593.3 jit_solution(10199174037934600814)
XLA Ops:
  0.9 1.3 pad_bitcast_fusion.9.small
  2.1 1.1 reshape.409
  3.2 0.7 pad.92.piece_proj
  3.9 1.9 reshape.404
  5.9 0.7 fusion.16
  7.4 0.5 copy.93
  8.0 0.7 reshape.447
  8.7 0.9 pad.88.units_qkv
  9.6 0.5 reshape.414
  10.2 0.9 pad.93.piece_out
  11.1 2.4 reshape.406
  13.5 0.6 copy.115
  14.1 0.7 pad.89.clone
  14.8 1.1 reshape.448
  15.9 1.0 pad.90.units_fc
  16.9 1.2 copy.74
  18.2 1.2 copy.82
  19.4 99.1 %prologue.1 = (bf16[2,128,1600]{2,1,0:T(8,128)(2,1)}, bf16[8,4,16,128]{3,2,1,0:T(8,128)(2,1)}, bf16[8,208,1344]{2,1,0:T(8,128)(2,1)}, bf16[4,8,64,1600]{3,2,1,0:T(8,128)(2,1)}, bf16[208,1664]{1,0:T(8,128)(2,1)}) custom-call(bf16[2,128,1600]{2,1,0:T(8,128)(2,1)} %bitcast.191, bf16[4,64,1344]{2,1,0:T(8,128)(2,1)} %pad.88.units_qkv, ...), custom_call_target="tpu_custom_call" | custom-call | tf_op jit(solution)/shard_map/prologue/pallas_call | solution.py:401
  118.6 1.0 reshape.411
  119.6 1.4 convert_reduce_fusion
  121.0 0.4 fusion.1
  121.9 0.7 reshape_reshape.7.bias_fc
  122.9 0.7 reshape_reshape.6.bias_qkv
  123.6 0.6 reshape.419.shift2
  124.2 0.6 reshape.417.bias_proj
  124.8 0.6 broadcast_in_dim.61.gain1
  125.4 0.6 reshape.418.gain2
  126.0 5.3 convolution_convert_fusion.2
  131.3 145.5 %forward.1 = (bf16[8,128,1664]{2,1,0:T(8,128)(2,1)}, bf16[2,128,1600]{2,1,0:T(8,128)(2,1)}, bf16[8,128,1600]{2,1,0:T(8,128)(2,1)}, bf16[8,208,1664]{2,1,0:T(8,12...) custom-call(bf16[2,128,1664]{2,1,0:T(8,128)(2,1)} %bitcast.201, ...), custom_call_target="tpu_custom_call" | custom-call | tf_op jit(solution)/shard_map/forward/pallas_call | solution.py:401
  276.8 96.2 %feed_forward.1 = (f32[2,128,1600]{2,1,0:T(8,128)}, f32[2,128,1664]{2,1,0:T(8,128)}, f32[208,1600]{1,0:T(8,128)}, bf16[1024,1664]{1,0:T(8,128)(2,1)}, f32[1,1664]{1,0:T(1,128)}) custom-call(bf16[1024,1664]{1,0:T(8,128)(2,1)} %bitcast.181, bf16[8,128,1600]{2,1,0:T(8,128)(2,1)} %get-tuple-element.44.grad_all, bf16[1664,1664]{1,0:T(8,128)(2,1)} %bitcast.188, ...), custom_call_target="tpu_custom_call" | custom-call | tf_op jit(solution)/shard_map/feed_forward/pallas_call | solution.py:401
  373.0 0.2 reduce_sum.91
  373.2 0.3 multiply_reduce_fusion.2
  373.5 0.2 copy-done.15
  373.8 0.3 copy-done.2
  374.5 1.5 convert_element_type.113
  376.0 5.5 fusion.24
  381.6 1.7 reshape.438
  383.4 1.8 copy.83
  385.1 0.5 multiply_reduce_fusion
  385.6 0.9 copy-done.5
  386.6 1.5 fusion.13
  388.1 1.5 convert_reduce_fusion.1
  389.6 9.4 %convolution_convert_fusion = bf16[256,1792]{1,0:T(8,128)(2,1)S(1)} fusion(bf16[1792,2048]{1,0:T(8,128)(2,1)} %constant.101.clone.to_proj, bf16[256,1600]{1,0:T(8,128)(2,1)S(1)} %get-tuple-element.101.branch, bf16[2048,1600]{1,0:T(8,128)(2,1)} %bitcast.187), kind=kOutput, calls=%fused_computation | convolution fusion | flops 3557752832 | bytes 15630336 | tf_op jit(solution)/shard_map/dot_general | solution.py:73
  399.3 0.3 fusion.14
  399.5 1.1 pad_maximum_fusion.swap_parts
  400.7 155.7 %backward.1 = (bf16[4,64,1344]{2,1,0:T(8,128)(2,1)}, bf16[4,64,1664]{2,1,0:T(8,128)(2,1)}, f32[64,1664]{1,0:T(8,128)}, bf16[2,128,1600]{2,1,0:T(8,128)(2,1)}, bf...) custom-call(bf16[1024,1664]{1,0:T(8,128)(2,1)} %bitcast.190, bf16[1024,1664]{1,0:T(8,128)(2,1)} %bitcast.182, ...), custom_call_target="tpu_custom_call" | custom-call | tf_op jit(solution)/shard_map/backward/pallas_call | solution.py:401
  556.4 2.1 copy.90
  558.5 0.7 fusion.23
  560.0 0.7 copy.85
  560.7 15.3 %epilogue.1 = (bf16[4,64,1344]{2,1,0:T(8,128)(2,1)}, f32[8,128]{1,0:T(8,128)}) custom-call(bf16[4,64,1344]{2,1,0:T(8,128)(2,1)} %get-tuple-element.57.units_qkv, f32[8,4,8,128]{3,2,1,0:T(8,128)} %bitcast.208), custom_call_target="tpu_custom_call" | custom-call | tf_op jit(solution)/shard_map/epilogue/pallas_call | solution.py:401
  576.1 1.2 slice.335
  577.2 0.2 copy.86
  577.5 0.6 slice.361
  578.0 0.6 slice.362
  578.7 0.9 reshape.433
  579.7 0.9 reshape.434
  580.6 0.8 fusion.15
  582.4 0.3 copy.87
  582.7 1.8 reshape.443
  584.6 1.4 reshape.449
  586.0 0.9 convert_bitcast_fusion
  586.9 0.8 copy.89
  587.7 3.7 reshape.445
  591.5 1.6 copy.91
  (138 shorter events, 4.2 us)
Async XLA Ops:
  8.0 1.7 copy-start.11
  8.7 2.4 copy-start.12
  14.8 2.1 copy-start.8
  15.9 2.2 copy-start.9
  118.5 2.4 copy-start.1
  276.7 96.2 %copy-start = (f32[256,1600]{1,0:T(8,128)S(1)}, f32[256,1600]{1,0:T(8,128)}, u32[]{:S(2)}) copy-start(f32[256,1600]{1,0:T(8,128)} %get-tuple-element.52) | copy-start | bytes 4915204
  373.0 0.7 copy-start.15
  373.0 1.2 copy-start.2
  376.0 5.5 copy-start.6
  385.1 1.5 copy-start.5
  386.6 1.5 copy-start.3
  389.6 9.5 %copy-start.4 = (bf16[256,1600]{1,0:T(8,128)(2,1)}, bf16[256,1600]{1,0:T(8,128)(2,1)S(1)}, u32[]{:S(2)}) copy-start(bf16[256,1600]{1,0:T(8,128)(2,1)S(1)} %get-tuple-element.101.branch) | copy-start | bytes 2457604
  556.3 3.3 copy-start.14
  576.0 1.4 copy-start.16
  576.0 3.6 copy-start.13
  582.7 1.9 copy-start.10
  587.7 3.7 copy-start.7

commit v7 on v6

--- a/solution.py
+++ b/solution.py
@@ -925,9 +925,11 @@
 
 
 def feed_forward(
-    hidden_two, grad_all, mat_fc, mat_out, bias_fc,
-    result, hidden, grad_out_w, grad_pre, terms,
-    h2, dy, wf, wo, activ, part_r, part_h, part_o, l1, s1, a1, l2, s2, a2, l3, sems,
+    hidden_two, grad_all, mat_fc, mat_out, mat_proj, to_proj, to_wide,
+    bias_fc, bias_out, gain2, resid, cotangent,
+    result, grad_out_w, grad_pre, terms, grad_resid, branch, swap_parts, norms,
+    h2, dy, wf, wo, activ, part_r, part_o, l1, s1, a1, l2, s2, a2, l3,
+    hidden, total_r, spread, sems,
 ):
     spot = y, c, h, l, x = here()
     wires = Wires(sems)
@@ -936,8 +938,14 @@
     ]
     for copy in load:
         copy.start()
+    load_wide = wires.near(to_wide, wf.at[pl.ds(0, D)])
+    load_proj = [wires.near(mat_proj.at[pl.ds(0, WIDE)], wo)] + [
+        wires.near(mat_proj.at[pl.ds(WIDE + k * BLK, BLK)], dy.at[k]) for k in range(3)
+    ]
+    load_spread = [wires.near(to_proj.at[pl.ds(r * HW, HW)], spread) for r in range(4)]
+    load_spread[0].start()
     meet(team_peers(*spot) + grid_peers(*spot))
-    second = TeamScatter(wires, part_h, l2, s2, a2, spot)
+    second = TeamScatter(wires, h2, l2, s2, a2, spot)
     first = TeamScatter(wires, part_r, l1, s1, a1, spot)
     out = Scatter(wires, part_o, l3, spot)
     load[0].wait()
@@ -974,10 +982,11 @@
 
         return half
 
-    half = into(part_h, lambda rows: back_product(grad_pre[rows, :], wf[...]))
+    half = into(h2, lambda rows: back_product(grad_pre[rows, :], wf[...]))
     half(1 - c)
     second.start()
     half(c)
+    load_wide.start()
     out.step(1)
     second.step(0)
     second.step(1)
@@ -985,12 +994,36 @@
     half(1 - c)
     first.start()
     half(c)
+    for copy in load_proj:
+        copy.start()
     out.step(2)
     first.step(0)
     first.step(1)
+    load_wide.wait()
     second.finish(hidden)
     out.step(3)
-    first.finish(result)
+    grad = back_product(hidden[...].reshape(2 * BLK, WIDE).astype(LOW), wf[:D, :])
+    grad, norms[0:1, :], norms[1:2, :] = norm_back(resid[...], gain2[...], grad)
+    own = cotangent[...].reshape(2 * BLK, D).astype(F32)
+    norms[3:4, :] = jnp.sum(own, axis=0, keepdims=True)
+    grad = own + grad
+    grad_resid[...] = grad
+    branch[...] = grad.astype(LOW)
+    norms[2:3, :] = jnp.sum(branch[...].astype(F32), axis=0, keepdims=True)
+    for copy in load_proj:
+        copy.wait()
+    low = back_product(branch[...], wo[...]).astype(LOW)
+    high = back_product(branch[...], dy[0:3].reshape(3 * BLK, D)).astype(LOW)
+    for r in range(4):
+        load_spread[r].wait()
+        part = back_product(low, spread[:, :WIDE]) + back_product(high, spread[:, WIDE:])
+        swap_parts[r] = part.astype(LOW).reshape(2, BLK, HW)
+        if r < 3:
+            load_spread[r + 1].start()
+    first.finish(total_r)
+    result[...] = (
+        resid[...].reshape(2, BLK, D) + total_r[...] + bias_out[...].reshape(1, 1, D)
+    ).astype(LOW)
     out.finish(grad_out_w)
 
 
@@ -1372,41 +1405,38 @@
     hidden_two = hidden_two.reshape(SEQ, WIDE)
     mat_out = mat_out.reshape(WIDE, D)
     mat_fc = mat_fc.reshape(WIDE, WIDE)
-    _, ln2_pull = jax.vjp(layer_norm, resid, gain2, shift2)
-    result, grad_hidden_two, grad_out_w, grad_pre, fc_terms = call(
+    (
+        result, grad_out_w, grad_pre, fc_terms, grad_resid, grad_branch, swap_parts, norms_two,
+    ) = call(
         feed_forward, "feed_forward", 5,
-        (hidden_two, grad_all, mat_fc, mat_out, bias_fc.reshape(1, WIDE)),
+        (
+            hidden_two, grad_all, mat_fc, mat_out, mat_proj, to_proj, to_wide,
+            bias_fc.reshape(1, WIDE), bias_out.reshape(1, D), gain2.reshape(1, D), resid, cotangent,
+        ),
         [
-            ((2, BLK, D), F32), ((2, BLK, WIDE), F32), ((PIECE, D), F32), ((SEQ, WIDE), LOW),
-            ((1, WIDE), F32),
+            ((2, BLK, D), LOW), ((PIECE, D), F32), ((SEQ, WIDE), LOW), ((1, WIDE), F32),
+            ((2 * BLK, D), F32), ((2 * BLK, D), LOW), ((4, 2, BLK, HW), LOW), ((4, D), F32),
         ],
-        [ANY] * 4 + [VM], [VM] * 5,
+        [ANY] * 7 + [VM] * 5, [VM] * 8,
         [
             pltpu.VMEM((SEQ, WIDE), LOW), pltpu.VMEM((8, BLK, D), LOW), pltpu.VMEM((WIDE, WIDE), LOW),
             pltpu.VMEM((WIDE, D), LOW), pltpu.VMEM((SEQ, WIDE), LOW), pltpu.VMEM((SEQ, D), LOW),
-            pltpu.VMEM((SEQ, WIDE), LOW), pltpu.VMEM((WIDE, D), LOW),
+            pltpu.VMEM((WIDE, D), LOW),
         ]
-        + team_scatter_scratch(D) + team_scatter_scratch(WIDE) + scatter_scratch(PIECE, D),
-        2 * TEAM_SCATTER_SEMS + SCATTER_SEMS + 4,
-    )
-    result = (resid + result.reshape(2 * BLK, D) + bias_out).astype(LOW)
+        + team_scatter_scratch(D) + team_scatter_scratch(WIDE) + scatter_scratch(PIECE, D)
+        + [
+            pltpu.VMEM((2, BLK, WIDE), F32), pltpu.VMEM((2, BLK, D), F32),
+            pltpu.VMEM((HW, PROJ), LOW),
+        ],
+        2 * TEAM_SCATTER_SEMS + SCATTER_SEMS + 13,
+    )
     grad_out_w = grad_out_w[:200].reshape(-1)
 
-    grad_full = cotangent.reshape(2 * BLK, D).astype(F32)
-    grad_hidden_two = back_product(grad_hidden_two.reshape(2 * BLK, WIDE).astype(LOW), to_wide)
-    grad_ln_two, grad_gain_two, grad_shift_two = ln2_pull(grad_hidden_two)
-    grad_resid = grad_full + grad_ln_two
-    grad_branch = grad_resid.astype(LOW)
-    grad_context = back_product(grad_branch, mat_proj).astype(LOW)
-    grad_context = back_product(grad_context, to_proj).astype(LOW)
-    grad_context = jnp.stack(
-        [grad_context[:, r * HW : (r + 1) * HW] for r in range(4)]
-    ).reshape(4, 2, BLK, HW)
     units_qkv, got_fc, grad_proj, outputs, grad_in, terms, norms = call(
         backward, "backward", 7,
         (
-            hidden_one, hidden_two, grad_pre, mat_qkv, mixed, totals, grad_context, context,
-            grad_branch, result.reshape(2, BLK, D), tokens_low, grad_resid, gain1.reshape(1, D),
+            hidden_one, hidden_two, grad_pre, mat_qkv, mixed, totals, swap_parts, context,
+            grad_branch, result, tokens_low, grad_resid, gain1.reshape(1, D),
             to_wide,
         ),
         [
@@ -1442,8 +1472,7 @@
     front = jnp.concatenate([norms.reshape(-1), grad_bq, grad_bv])
     tail = jnp.concatenate(
         [
-            ones_row(grad_branch), grad_gain_two, grad_shift_two, grad_fc_bias,
-            jnp.sum(grad_full, axis=0),
+            norms_two[2], norms_two[0], norms_two[1], grad_fc_bias, norms_two[3],
         ]
     )
     small = jnp.concatenate([front.reshape(32, 200), tail.reshape(32, 400)], axis=1)

time: 600 us -> 577 us (0.962)
  matrix products: 20.2 us -> 5.28 us
  other arithmetic: 10.5 us -> 3.64 us
    dot_general x2 -> x0, matrix products: 14.9 us -> none  [back_product(): lax.dot_general(grad, weight, (((1,), (1,)), ((), ())), preferred_element...]
where the time goes in v7:
time: 577 us; the launch traced here: 570 us
  Pallas kernels  513 us (89%)
  local copies, waits for them, and re-layouts  46.1 us (8%)
    pallas_call x5, Pallas kernels, call(): pl.pallas_call(body, out_shape=[jax.ShapeDtypeStruct(s, d) for s, d in ou...  513 us

profile of v7, /device:TPU:0, one launch (start us, length us, event | category | flops | bytes accessed | tf_op | source)
XLA Modules:
  0.0 570.2 jit_solution(18156957106388642931)
XLA Ops:
  0.9 1.3 pad_bitcast_fusion.9.small
  2.1 1.1 reshape.361
  3.2 0.7 pad.92.piece_proj
  3.9 1.9 reshape.356
  5.8 0.7 fusion.11
  6.6 0.1 fusion.12
  6.9 0.1 fusion.14
  7.3 0.1 pad_maximum_fusion
  7.4 0.5 copy.85
  8.0 0.7 reshape.397
  8.7 0.9 pad.88.units_qkv
  9.6 0.5 reshape.366
  10.2 0.9 pad.93.piece_out
  11.1 2.4 reshape.358
  13.5 0.6 copy.107
  14.1 0.7 pad.89.clone
  14.8 1.1 reshape.398
  15.9 1.0 pad.90.units_fc
  16.9 1.2 copy.68
  18.1 1.2 copy.76
  19.4 99.1 %prologue.1 = (bf16[2,128,1600]{2,1,0:T(8,128)(2,1)}, bf16[8,4,16,128]{3,2,1,0:T(8,128)(2,1)}, bf16[8,208,1344]{2,1,0:T(8,128)(2,1)}, bf16[4,8,64,1600]{3,2,1,0:T(8,128)(2,1)}, bf16[208,1664]{1,0:T(8,128)(2,1)}) custom-call(bf16[2,128,1600]{2,1,0:T(8,128)(2,1)} %bitcast.171, bf16[4,64,1344]{2,1,0:T(8,128)(2,1)} %pad.88.units_qkv, ...), custom_call_target="tpu_custom_call" | custom-call | tf_op jit(solution)/shard_map/prologue/pallas_call | solution.py:401
  118.5 1.0 reshape.363
  119.6 1.4 convert_reduce_fusion
  120.9 0.4 fusion.1
  121.4 0.1 reshape.391
  121.7 0.6 reshape.377.bias_out
  122.3 0.1 reshape.376
  122.4 0.7 reshape_reshape.7.bias_fc
  123.1 0.6 reshape.370.gain2
  124.0 0.7 reshape_reshape.6.bias_qkv
  124.7 0.6 reshape.371.shift2
  125.3 0.6 reshape.369.bias_proj
  125.9 0.6 broadcast_in_dim.49.gain1
  126.5 5.3 convolution_convert_fusion
  131.8 145.4 %forward.1 = (bf16[8,128,1664]{2,1,0:T(8,128)(2,1)}, bf16[2,128,1600]{2,1,0:T(8,128)(2,1)}, bf16[8,128,1600]{2,1,0:T(8,128)(2,1)}, bf16[8,208,1664]{2,1,0:T(8,12...) custom-call(bf16[2,128,1664]{2,1,0:T(8,128)(2,1)} %bitcast.175, ...), custom_call_target="tpu_custom_call" | custom-call | tf_op jit(solution)/shard_map/forward/pallas_call | solution.py:401
  277.2 97.9 %feed_forward.1 = (bf16[2,128,1600]{2,1,0:T(8,128)(2,1)}, f32[208,1600]{1,0:T(8,128)}, bf16[1024,1664]{1,0:T(8,128)(2,1)}, f32[1,1664]{1,0:T(1,128)}, f32[256,16...) custom-call(bf16[1024,1664]{1,0:T(8,128)(2,1)} %bitcast.163, ...), custom_call_target="tpu_custom_call" | custom-call | tf_op jit(solution)/shard_map/feed_forward/pallas_call | solution.py:401
  375.1 155.8 %backward.1 = (bf16[4,64,1344]{2,1,0:T(8,128)(2,1)}, bf16[4,64,1664]{2,1,0:T(8,128)(2,1)}, f32[64,1664]{1,0:T(8,128)}, bf16[2,128,1600]{2,1,0:T(8,128)(2,1)}, bf...) custom-call(bf16[1024,1664]{1,0:T(8,128)(2,1)} %bitcast.170, bf16[1024,1664]{1,0:T(8,128)(2,1)} %bitcast.164, ...), custom_call_target="tpu_custom_call" | custom-call | tf_op jit(solution)/shard_map/backward/pallas_call | solution.py:401
  530.9 2.2 copy.82
  533.1 0.7 fusion.18
  534.0 0.1 concatenate.25
  534.2 0.1 concatenate.24
  534.7 0.1 select_n.48
  535.2 0.7 copy.77
  535.9 15.1 %epilogue.1 = (bf16[4,64,1344]{2,1,0:T(8,128)(2,1)}, f32[8,128]{1,0:T(8,128)}) custom-call(bf16[4,64,1344]{2,1,0:T(8,128)(2,1)} %get-tuple-element.62.units_qkv, f32[8,4,8,128]{3,2,1,0:T(8,128)} %bitcast.182), custom_call_target="tpu_custom_call" | custom-call | tf_op jit(solution)/shard_map/epilogue/pallas_call | solution.py:401
  551.1 1.2 slice.335
  552.3 0.2 copy.78
  552.5 0.6 slice.361
  553.1 0.6 slice.362
  553.7 0.9 reshape.384
  554.7 0.9 reshape.385
  555.6 0.8 fusion.10
  556.6 0.2 concatenate.31
  556.9 0.2 concatenate.30
  557.1 0.2 concatenate.29
  557.3 0.1 maximum_convert_fusion
  557.4 0.3 copy.79
  557.8 1.8 reshape.393
  559.7 1.4 reshape.399
  561.0 0.9 convert_bitcast_fusion
  562.0 0.8 copy.81
  562.8 3.7 reshape.395
  566.5 1.7 reshape.389
  568.3 0.1 bitcast_convert_fusion
  568.4 1.6 copy.83
  (116 shorter events, 2.5 us)
Async XLA Ops:
  8.0 1.7 copy-start.6
  8.7 2.4 copy-start.7
  14.8 2.1 copy-start.3
  15.9 2.2 copy-start.4
  118.5 2.4 copy-start
  530.9 2.9 copy-start.11
  530.9 3.4 copy-start.10
  530.9 3.9 copy-start.9
  551.1 1.4 copy-start.12
  551.1 3.6 copy-start.8
  557.8 1.9 copy-start.5
  562.8 3.7 copy-start.1
  566.5 1.7 copy-start.2

commit v8 on v7

--- a/solution.py
+++ b/solution.py
@@ -814,7 +814,8 @@
 def forward(
     hidden, grads, piece_fc, piece_out, mat_qkv, mat_proj, to_proj, to_wide,
     tokens, bias_qkv, bias_proj, gain2, shift2,
-    hidden_all, cotangent, grad_all, all_fc, all_out, second_all, mixed, totals, context_out, resid,
+    hidden_out, cotangent, grad_all, all_fc, all_out, second_all, mixed_out, totals, context_out, resid,
+    hidden_all, mixed,
     mat_in, proj_in, to_proj_in, to_wide_in, context, got, second, sems,
 ):
     spot = y, c, h, l, x = here()
@@ -828,6 +829,7 @@
     for copy in load:
         copy.start()
     meet_tokens(team_peers(*spot) + grid_peers(*spot), spot)
+    keep = [wires.near(hidden_all, hidden_out), wires.near(mixed, mixed_out)]
     team = TeamGather(wires, hidden, hidden_all, spot)
     fc = Gather(wires, piece_fc, all_fc, spot)
     out = Gather(wires, piece_out, all_out, spot)
@@ -849,6 +851,7 @@
     team.step(1)
     load[0].wait()
     team.finish()
+    keep[0].start()
     bring.start()
     fc.step(1)
 
@@ -858,6 +861,7 @@
         flat = hidden_all[pl.ds(pl.multiple_of(i * 2, 2), 2)].reshape(QB, WIDE)
         mixed[rows, :] = (dot(flat, mat_in[...]) + bias_qkv[...]).astype(LOW)
 
+    keep[1].start()
     fc.step(2)
     for head in range(SLOTS):
         attend(mixed, context, totals, head)
@@ -897,6 +901,8 @@
     team_two.finish()
     team_three.finish()
     out.finish()
+    for copy in keep:
+        copy.wait()
 
 
 def gelu_both(f):
@@ -927,29 +933,31 @@
 def feed_forward(
     hidden_two, grad_all, mat_fc, mat_out, mat_proj, to_proj, to_wide,
     bias_fc, bias_out, gain2, resid, cotangent,
-    result, grad_out_w, grad_pre, terms, grad_resid, branch, swap_parts, norms,
+    result, grad_out_w, grad_pre_out, terms, grad_resid, branch, swap_parts, norms,
     h2, dy, wf, wo, activ, part_r, part_o, l1, s1, a1, l2, s2, a2, l3,
-    hidden, total_r, spread, sems,
+    hidden, total_r, spread, grad_pre, sems,
 ):
     spot = y, c, h, l, x = here()
     wires = Wires(sems)
     load = [
         wires.near(*both) for both in ((hidden_two, h2), (mat_fc, wf), (grad_all, dy), (mat_out, wo))
     ]
-    for copy in load:
+    for copy in load[:2]:
         copy.start()
+    keep = wires.near(grad_pre, grad_pre_out)
     load_wide = wires.near(to_wide, wf.at[pl.ds(0, D)])
     load_proj = [wires.near(mat_proj.at[pl.ds(0, WIDE)], wo)] + [
         wires.near(mat_proj.at[pl.ds(WIDE + k * BLK, BLK)], dy.at[k]) for k in range(3)
     ]
     load_spread = [wires.near(to_proj.at[pl.ds(r * HW, HW)], spread) for r in range(4)]
-    load_spread[0].start()
     meet(team_peers(*spot) + grid_peers(*spot))
     second = TeamScatter(wires, h2, l2, s2, a2, spot)
     first = TeamScatter(wires, part_r, l1, s1, a1, spot)
     out = Scatter(wires, part_o, l3, spot)
     load[0].wait()
     load[1].wait()
+    for copy in load[2:] + load_spread[:1]:
+        copy.start()
 
     @pl.loop(0, SEQ // QB)
     def _(i):
@@ -972,6 +980,8 @@
         df = (back_product(here_dy, wo[...]) * grad_pre[rows, :].astype(F32)).astype(LOW)
         grad_pre[rows, :] = df
         terms[...] += jnp.sum(df.astype(F32), axis=0, keepdims=True)
+
+    keep.start()
 
     def into(target, make):
         def half(which):
@@ -1025,6 +1035,7 @@
         resid[...].reshape(2, BLK, D) + total_r[...] + bias_out[...].reshape(1, 1, D)
     ).astype(LOW)
     out.finish(grad_out_w)
+    keep.wait()
 
 
 def backward(
@@ -1032,13 +1043,13 @@
     tokens, grad_resid, gain1, to_wide,
     units_qkv, got_fc, grad_proj, outputs, grad_in, terms, norms,
     ha, hb, wq, part_f, part_h, grads, mixed, acc_k, acc_v,
-    l1, s1, a1, l2, l3, l4, pm, px, hidden, grad_low, wide_fc, wide_qkv, units_fc, sems,
+    l1, s1, a1, l2, l3, l4, l5, pm, part_t, got_t, hidden, grad_low, wide_fc, wide_qkv, units_fc, sems,
 ):
     spot = y, c, h, l, x = here()
     wires = Wires(sems)
     load = [wires.near(*both) for both in ((hidden_two, ha), (grad_pre, hb), (mixed_all, mixed), (mat_qkv, wq))]
     again = wires.near(hidden_one, ha)
-    for copy in load:
+    for copy in load[:2]:
         copy.start()
     meet_tokens(team_peers(*spot) + grid_peers(*spot), spot)
     swaps = [
@@ -1065,8 +1076,9 @@
         at = pl.ds(pl.multiple_of((p * 2 + q) * quarter, quarter), quarter)
         return outer_sum(context[:, at], branch[...])
 
-    to_side = wires.far(pm.at[side(1 - l)], px, device(y, c, h, 1 - l, x))
-    proj = Scatter(wires, px, l4, spot)
+    to_side = wires.far(part_t, got_t, device(y, c, h, 1 - l, x))
+    proj = Scatter(wires, pm.at[side(l)], l4, spot)
+    beside = Scatter(wires, pm.at[side(1 - l)], l5, spot)
     move = Tokens(wires, result, outputs, spot)
     back = Tokens(wires, grad_low, grad_in, spot)
     swap_fc = TeamSwap(
@@ -1076,6 +1088,8 @@
     load_wide = wires.near(to_wide, spread)
     load[0].wait()
     load[1].wait()
+    for copy in load[2:]:
+        copy.start()
     outer_into(part_f, ha, lambda: hb[...])
     fc.start()
     again.start()
@@ -1090,11 +1104,12 @@
         if head == 0:
             fc.step(1)
             to_mate.wait_recv()
-            pm[side(1 - l), :D] = (pm[side(1 - l), :D].astype(F32) + term(c, 1 - l)).astype(LOW)
-        if head == 1:
-            to_side.start()
+            for q in range(2):
+                pm[side(q), :D] = (pm[side(q), :D].astype(F32) + term(c, q)).astype(LOW)
         if head == 2:
             fc.step(2)
+            beside.start()
+            proj.start()
         if head == 4:
             fc.step(3)
             move.start()
@@ -1110,6 +1125,8 @@
     first.start()
     half(c)
     again.wait()
+    beside.step(1)
+    proj.step(1)
     outer_into(wq, ha, lambda: mixed[...])
     qkv.start()
     first.step(0)
@@ -1118,25 +1135,27 @@
     load_wide.start()
     split_units(wide_fc, units_fc)
     swap_fc.start()
-    to_side.wait_recv()
-    px[:, :D] = (pm[side(l), :D].astype(F32) + term(c, l) + px[:, :D].astype(F32)).astype(LOW)
-    proj.start()
+    beside.step(2)
+    proj.step(2)
     qkv.step(1)
+    beside.step(3)
+    proj.step(3)
     terms[...] = jnp.sum(mixed[...].astype(F32), axis=0, keepdims=True)
     load_wide.wait()
     qkv.step(2)
-    proj.step(1)
     first.finish(hidden)
     grad = back_product(hidden[...].reshape(2 * BLK, WIDE).astype(LOW), spread[...])
     grad, norms[0:1, :], norms[1:2, :] = norm_back(tokens[...].astype(F32), gain1[...], grad)
     grad_low[...] = (grad_resid[...] + grad).astype(LOW).reshape(2, BLK, D)
     back.start()
+    beside.finish(part_t)
+    to_side.start()
     qkv.step(3)
-    proj.step(2)
-    proj.step(3)
+    proj.finish(grad_proj)
+    to_side.wait_recv()
+    grad_proj[...] = grad_proj[...] + got_t[...].astype(F32)
     qkv.finish(wide_qkv)
     split_units(wide_qkv, units_qkv)
-    proj.finish(grad_proj)
     swap_fc.finish()
     move.finish()
     back.finish()
@@ -1393,13 +1412,14 @@
             ((8, BLK, WIDE), LOW), ((SEQ, QW), LOW), ((SEQ, SLOTS), F32), ((2 * BLK, PROJ), LOW),
             ((2 * BLK, D), F32),
         ],
-        [VM] * 4 + [ANY] * 4 + [VM] * 5, [VM, VM] + [ANY] * 4 + [VM] * 4,
+        [VM] * 4 + [ANY] * 4 + [VM] * 5, [ANY, VM] + [ANY] * 5 + [VM] * 3,
         [
+            pltpu.VMEM((8, BLK, WIDE), LOW), pltpu.VMEM((SEQ, QW), LOW),
             pltpu.VMEM((WIDE, QW), LOW), pltpu.VMEM((PROJ, D), LOW), pltpu.VMEM((4 * HW, PROJ), LOW),
             pltpu.VMEM((D, WIDE), LOW), pltpu.VMEM((SEQ, HW), LOW), pltpu.VMEM((4, 2, BLK, HW), LOW),
             pltpu.VMEM((2, BLK, WIDE), LOW),
         ],
-        3 * TEAM_GATHER_SEMS + TOKENS_SEMS + 2 * GATHER_SEMS + 2 * TEAM_SWAP_SEMS + 4,
+        3 * TEAM_GATHER_SEMS + TOKENS_SEMS + 2 * GATHER_SEMS + 2 * TEAM_SWAP_SEMS + 6,
     )
     hidden_one = hidden_one.reshape(SEQ, WIDE)
     hidden_two = hidden_two.reshape(SEQ, WIDE)
@@ -1417,7 +1437,7 @@
             ((2, BLK, D), LOW), ((PIECE, D), F32), ((SEQ, WIDE), LOW), ((1, WIDE), F32),
             ((2 * BLK, D), F32), ((2 * BLK, D), LOW), ((4, 2, BLK, HW), LOW), ((4, D), F32),
         ],
-        [ANY] * 7 + [VM] * 5, [VM] * 8,
+        [ANY] * 7 + [VM] * 5, [VM, VM, ANY] + [VM] * 5,
         [
             pltpu.VMEM((SEQ, WIDE), LOW), pltpu.VMEM((8, BLK, D), LOW), pltpu.VMEM((WIDE, WIDE), LOW),
             pltpu.VMEM((WIDE, D), LOW), pltpu.VMEM((SEQ, WIDE), LOW), pltpu.VMEM((SEQ, D), LOW),
@@ -1426,9 +1446,9 @@
         + team_scatter_scratch(D) + team_scatter_scratch(WIDE) + scatter_scratch(PIECE, D)
         + [
             pltpu.VMEM((2, BLK, WIDE), F32), pltpu.VMEM((2, BLK, D), F32),
-            pltpu.VMEM((HW, PROJ), LOW),
+            pltpu.VMEM((HW, PROJ), LOW), pltpu.VMEM((SEQ, WIDE), LOW),
         ],
-        2 * TEAM_SCATTER_SEMS + SCATTER_SEMS + 13,
+        2 * TEAM_SCATTER_SEMS + SCATTER_SEMS + 14,
     )
     grad_out_w = grad_out_w[:200].reshape(-1)
 
@@ -1451,13 +1471,13 @@
             pltpu.VMEM((SEQ, HEAD), F32), pltpu.VMEM((SEQ, HEAD), F32),
         ]
         + team_scatter_scratch(WIDE) + scatter_scratch(PIECE, WIDE) + scatter_scratch(PIECE, QW)
-        + scatter_scratch(PB, WIDE)
+        + scatter_scratch(PB, WIDE) + scatter_scratch(PB, WIDE)
         + [
-            pltpu.VMEM((PROJ // 2, WIDE), LOW), pltpu.VMEM((PROJ // 4, WIDE), LOW),
+            pltpu.VMEM((PROJ // 2, WIDE), LOW), pltpu.VMEM((PB, WIDE), LOW), pltpu.VMEM((PB, WIDE), LOW),
             pltpu.VMEM((2, BLK, WIDE), F32), pltpu.VMEM((2, BLK, D), LOW),
             pltpu.VMEM((224, WIDE), F32), pltpu.VMEM((224, QW), F32), pltpu.VMEM((4, 64, WIDE), LOW),
         ],
-        TEAM_SCATTER_SEMS + 3 * SCATTER_SEMS + 2 * TOKENS_SEMS + 3 * TEAM_SWAP_SEMS + 10,
+        TEAM_SCATTER_SEMS + 4 * SCATTER_SEMS + 2 * TOKENS_SEMS + 3 * TEAM_SWAP_SEMS + 10,
     )
     grad_proj = grad_proj[:50, :D].reshape(-1)
 

time: 577 us -> 574 us (level)
  no operation moved by 1% of the time
where the time goes in v8:
time: 574 us; the launch traced here: 567 us
  Pallas kernels  511 us (89%)
  local copies, waits for them, and re-layouts  46.1 us (8%)
    pallas_call x5, Pallas kernels, call(): pl.pallas_call(body, out_shape=[jax.ShapeDtypeStruct(s, d) for s, d in ou...  511 us

profile of v8, /device:TPU:0, one launch (start us, length us, event | category | flops | bytes accessed | tf_op | source)
XLA Modules:
  0.0 567.4 jit_solution(7863760209193427301)
XLA Ops:
  0.9 1.3 pad_bitcast_fusion.9.small
  2.1 1.1 reshape.361
  3.2 0.7 pad.92.piece_proj
  3.9 1.9 reshape.356
  5.8 0.7 fusion.11
  6.6 0.1 fusion.12
  6.9 0.1 fusion.14
  7.3 0.1 pad_maximum_fusion
  7.4 0.5 copy.85
  8.0 0.7 reshape.397
  8.7 0.9 pad.88.units_qkv
  9.6 0.5 reshape.366
  10.2 0.9 pad.93.piece_out
  11.1 2.4 reshape.358
  13.5 0.6 copy.107
  14.1 0.7 pad.89.clone
  14.8 1.1 reshape.398
  15.9 1.0 pad.90.units_fc
  16.9 1.2 copy.68
  18.1 1.2 copy.76
  19.4 99.1 %prologue.1 = (bf16[2,128,1600]{2,1,0:T(8,128)(2,1)}, bf16[8,4,16,128]{3,2,1,0:T(8,128)(2,1)}, bf16[8,208,1344]{2,1,0:T(8,128)(2,1)}, bf16[4,8,64,1600]{3,2,1,0:T(8,128)(2,1)}, bf16[208,1664]{1,0:T(8,128)(2,1)}) custom-call(bf16[2,128,1600]{2,1,0:T(8,128)(2,1)} %bitcast.171, bf16[4,64,1344]{2,1,0:T(8,128)(2,1)} %pad.88.units_qkv, ...), custom_call_target="tpu_custom_call" | custom-call | tf_op jit(solution)/shard_map/prologue/pallas_call | solution.py:401
  118.5 1.0 reshape.363
  119.6 1.4 convert_reduce_fusion
  120.9 0.4 fusion.1
  121.4 0.1 reshape.391
  121.7 0.6 reshape.377.bias_out
  122.3 0.1 reshape.376
  122.4 0.7 reshape_reshape.7.bias_fc
  123.1 0.6 reshape.370.gain2
  124.0 0.7 reshape_reshape.6.bias_qkv
  124.7 0.6 reshape.371.shift2
  125.3 0.6 reshape.369.bias_proj
  125.9 0.6 broadcast_in_dim.49.gain1
  126.5 5.3 convolution_convert_fusion
  131.8 143.6 %forward.1 = (bf16[8,128,1664]{2,1,0:T(8,128)(2,1)}, bf16[2,128,1600]{2,1,0:T(8,128)(2,1)}, bf16[8,128,1600]{2,1,0:T(8,128)(2,1)}, bf16[8,208,1664]{2,1,0:T(8,12...) custom-call(bf16[2,128,1664]{2,1,0:T(8,128)(2,1)} %bitcast.175, ...), custom_call_target="tpu_custom_call" | custom-call | tf_op jit(solution)/shard_map/forward/pallas_call | solution.py:401
  275.4 96.5 %feed_forward.1 = (bf16[2,128,1600]{2,1,0:T(8,128)(2,1)}, f32[208,1600]{1,0:T(8,128)}, bf16[1024,1664]{1,0:T(8,128)(2,1)}, f32[1,1664]{1,0:T(1,128)}, f32[256,16...) custom-call(bf16[1024,1664]{1,0:T(8,128)(2,1)} %bitcast.163, ...), custom_call_target="tpu_custom_call" | custom-call | tf_op jit(solution)/shard_map/feed_forward/pallas_call | solution.py:401
  371.9 147.8 %backward.1 = (bf16[4,64,1344]{2,1,0:T(8,128)(2,1)}, bf16[4,64,1664]{2,1,0:T(8,128)(2,1)}, f32[64,1664]{1,0:T(8,128)}, bf16[2,128,1600]{2,1,0:T(8,128)(2,1)}, bf...) custom-call(bf16[1024,1664]{1,0:T(8,128)(2,1)} %bitcast.170, bf16[1024,1664]{1,0:T(8,128)(2,1)} %bitcast.164, ...), custom_call_target="tpu_custom_call" | custom-call | tf_op jit(solution)/shard_map/backward/pallas_call | solution.py:401
  519.7 2.2 copy.82
  521.9 0.7 fusion.18
  522.8 0.1 concatenate.25
  523.0 0.1 concatenate.24
  523.5 0.1 select_n.48
  524.0 0.7 copy.77
  524.7 23.6 %epilogue.1 = (bf16[4,64,1344]{2,1,0:T(8,128)(2,1)}, f32[8,128]{1,0:T(8,128)}) custom-call(bf16[4,64,1344]{2,1,0:T(8,128)(2,1)} %get-tuple-element.62.units_qkv, f32[8,4,8,128]{3,2,1,0:T(8,128)} %bitcast.182), custom_call_target="tpu_custom_call" | custom-call | tf_op jit(solution)/shard_map/epilogue/pallas_call | solution.py:401
  548.3 1.2 slice.335
  549.5 0.2 copy.78
  549.7 0.6 slice.361
  550.3 0.6 slice.362
  551.0 0.9 reshape.384
  551.9 0.9 reshape.385
  552.8 0.8 fusion.10
  553.8 0.2 concatenate.31
  554.1 0.2 concatenate.30
  554.4 0.2 concatenate.29
  554.5 0.1 maximum_convert_fusion
  554.6 0.3 copy.79
  555.0 1.8 reshape.393
  556.9 1.4 reshape.399
  558.3 0.9 convert_bitcast_fusion
  559.2 0.8 copy.81
  560.0 3.7 reshape.395
  563.8 1.7 reshape.389
  565.5 0.1 bitcast_convert_fusion
  565.6 1.6 copy.83
  (116 shorter events, 2.5 us)
Async XLA Ops:
  8.0 1.7 copy-start.6
  8.7 2.4 copy-start.7
  14.8 2.1 copy-start.3
  15.9 2.2 copy-start.4
  118.5 2.4 copy-start
  519.7 2.9 copy-start.11
  519.7 3.4 copy-start.10
  519.7 3.9 copy-start.9
  548.3 1.4 copy-start.12
  548.3 3.6 copy-start.8
  555.0 1.9 copy-start.5
  560.0 3.7 copy-start.1
  563.7 1.7 copy-start.2
